TPU v7x, 32 devices: a whole 2x2x4 slice. The times are simulated.
32 devices in a mesh: layer: 2 (over x), row: 4 (over y, core), col: 4 (over z).
Axes of the slice: x: 2, y: 2, z: 4, core: 2. Of those that a mesh axis runs over, the one named last changes fastest.
Arguments:
- partials: float32 [2, 1, 4, 256, 1, 4, 256], P('layer', None, 'row', None, None, 'col'), as said below
- pattern: int32 [1, 4, 2, 1, 4, 2], P(None, 'row', None, None, 'col'), may hold values from 0 to 1, as said below
Outputs:
- schur: float32 [1, 4, 2, 128, 1, 4, 256], P(None, 'row', 'layer', None, None, 'col')
- factor_panels: float32 [2, 1, 4, 256, 256], P(None, None, 'row')
Inputs may be any that keep to these rules, and one draw needn't show every extreme that they name: `partials`: each layer's partial is symmetric; in their sum the leading principal submatrix of order 2 * 256 is positive definite. `pattern`: symmetric in the global tile index.
All inputs are finite; a program needn't handle non-finite values.
Results may differ from a plain program's by a relative error of at most 0.0001.
Values sent between devices are 32-bit elements; how exact they have to be, the bound alone decides.
No kernel may reach another device: no remote copies, remote signals or barrier semaphores. Data moves between devices by JAX's collectives and lax.ppermute only.
A program may use at most 64 MiB of HBM per device.

v0:
```python
import jax
import jax.numpy as jnp
from jax import lax
from jax.sharding import PartitionSpec as P


def broadcast(block, axis, owner):
    block = jnp.where(lax.axis_index(axis) == owner, block, jnp.zeros_like(block))
    return lax.psum(block, axis)


def right_solve(diag_factor, block):
    return jax.scipy.linalg.solve_triangular(diag_factor, block.T, lower=True).T


def left_solve(diag_factor, block):
    return jax.scipy.linalg.solve_triangular(diag_factor, block, lower=True)


def on_device(partials, pattern):
    row_count = lax.axis_size("row")
    col_count = lax.axis_size("col")
    layer_count = lax.axis_size("layer")
    row_index = lax.axis_index("row")
    col_index = lax.axis_index("col")
    layer_index = lax.axis_index("layer")
    row_blocks = partials.shape[1]
    panel_width = partials.shape[3]
    col_blocks = partials.shape[4]
    tiles_per = pattern.shape[2]
    tile_size = panel_width // tiles_per
    slab_rows = panel_width // layer_count
    own_part = partials.reshape(row_blocks, panel_width, col_blocks, panel_width)
    front_sum = lax.psum(own_part, "layer")
    held_rows = front_sum.shape[1]
    row_ids = jnp.arange(row_blocks, dtype=jnp.int32) * row_count + row_index
    col_ids = jnp.arange(col_blocks, dtype=jnp.int32) * col_count + col_index
    tile_pattern = pattern.reshape(row_blocks, tiles_per, col_blocks, tiles_per)
    kept_tiles = (
        (tile_pattern > 0) | (row_ids[:, None, None, None] < 2) | (col_ids[None, None, :, None] < 2)
    )
    entry_keep = jnp.broadcast_to(
        kept_tiles[:, :, None, :, :, None],
        (row_blocks, tiles_per, tile_size, col_blocks, tiles_per, tile_size),
    )
    entry_keep = entry_keep.reshape(row_blocks, panel_width, col_blocks, panel_width)
    panel_list = []
    for panel in range(2):
        root_row = panel % row_count
        local_row = panel // row_count
        root_col = panel % col_count
        local_col = panel // col_count
        block_row = front_sum[local_row]
        diagonal = broadcast(
            block_row[:, local_col, :], ("row", "col"), root_row * col_count + root_col
        )
        diag_factor = jnp.linalg.cholesky(diagonal)
        rows_below = row_ids > panel
        rows_panel = row_ids == panel
        cols_below = col_ids > panel
        column_raw = front_sum[:, :, local_col, :].reshape(row_blocks * held_rows, panel_width)
        solved = right_solve(diag_factor, column_raw).reshape(row_blocks, held_rows, panel_width)
        lower_mine = jnp.where(
            rows_below[:, None, None],
            solved,
            jnp.where(rows_panel[:, None, None], diag_factor[None], 0.0),
        )
        lower_rows = broadcast(lower_mine, "col", root_col)
        row_raw = block_row.reshape(panel_width, col_blocks * panel_width)
        upper_mine = left_solve(diag_factor, row_raw).reshape(panel_width, col_blocks, panel_width)
        upper_mine = jnp.where(cols_below[None, :, None], upper_mine, 0.0)
        upper_cols = broadcast(upper_mine, "row", root_row)
        product = jnp.einsum(
            "aij,jbk->aibk",
            lower_rows,
            upper_cols,
            precision=lax.Precision.HIGHEST,
            preferred_element_type=jnp.float32,
        )
        front_sum = front_sum - jnp.where(entry_keep, product, 0.0)
        panel_list.append(lower_rows)
    stacked = jnp.stack(panel_list)
    layered = front_sum.reshape(row_blocks, layer_count, slab_rows, col_blocks, panel_width)
    own_slab = lax.dynamic_slice_in_dim(layered, layer_index, 1, 1)
    schur = own_slab.reshape(row_blocks, 1, 1, slab_rows, col_blocks, 1, panel_width)
    factor_panels = stacked.reshape(2, row_blocks, 1, panel_width, panel_width)
    return (schur, factor_panels)


def solution(mesh):
    return jax.shard_map(
        on_device,
        mesh=mesh,
        in_specs=(
            P("layer", None, "row", None, None, "col", None),
            P(None, "row", None, None, "col", None),
        ),
        out_specs=(
            P(None, "row", "layer", None, None, "col", None),
            P(None, None, "row", None, None),
        ),
        check_vma=False,
    )
```

profile of v0, /device:TPU:0, one launch (start us, length us, event | category | flops | bytes accessed | tf_op | source)
XLA Modules:
  0.0 502.7 jit_solution(14008100188385892164)
XLA Ops:
  7.2 1.8 copy.24
  9.1 27.7 %all-reduce.9.cloned.1.call-done = f32[1,256,1,256]{1,3,2,0:T(8,128)} async-done(((f32[1,256,1,256]{1,3,2,0:T(8,128)}), f32[1,256,1,256]{1,3,2,0:T(8,128)}) %all-reduce.9.cloned.1.call-update) | async-done | bytes 262160 | tf_op jit(solution)/shard_map/psum | solution.py:34
  36.8 1.7 broadcast_select_fusion.1
  38.5 91.3 %all-reduce.11.cloned.1.call-done = f32[256,256]{0,1:T(8,128)} async-done(((f32[256,256]{0,1:T(8,128)}), f32[256,256]{0,1:T(8,128)}) %all-reduce.11.cloned.1.call-update) | async-done | bytes 262160 | tf_op jit(solution)/shard_map/psum | solution.py:9
  129.9 1.1 copy.25
  131.1 11.7 %cholesky.130 = f32[128,128]{1,0:T(8,128)S(1)} custom-call(f32[128,128]{1,0:T(8,128)S(1)} %cholesky.194), custom_call_target="Cholesky" | custom-call | tf_op jit(solution)/shard_map/jit(cholesky)/cholesky | solution.py:57
  142.9 9.8 %custom-call.15 = f32[1,128,128]{1,2,0:T(8,128)S(1)} custom-call(f32[1,128,128]{2,1,0:T(8,128)S(1)} %get-tuple-element.93), custom_call_target="InvertDiagBlocksLowerTriangular" | custom-call | tf_op jit(solution)/shard_map/jit(cholesky)/cholesky | solution.py:57
  153.3 11.7 %cholesky.147 = f32[128,128]{1,0:T(8,128)S(1)} custom-call(f32[128,128]{1,0:T(8,128)S(1)} %convolution_subtract_fusion.5), custom_call_target="Cholesky" | custom-call | tf_op jit(solution)/shard_map/jit(cholesky)/cholesky | solution.py:57
  167.4 4.4 while.8
  168.1 1.4 dynamic-slice.16
  170.2 1.4 dynamic-slice.16
  171.7 19.7 %custom-call.16 = f32[2,128,128]{1,2,0:T(8,128)S(1)} custom-call(f32[2,128,128]{2,1,0:T(8,128)S(1)} %get-tuple-element.30), custom_call_target="InvertDiagBlocksLowerTriangular" | custom-call | tf_op jit(solution)/shard_map/jit(_solve_triangular)/triangular_solve | solution.py:13
  193.5 0.7 fusion.7
  194.3 0.8 fusion.6
  196.1 30.7 %all-reduce.15.cloned.1.call-done = f32[256,256]{0,1:T(8,128)} async-done(((f32[256,256]{0,1:T(8,128)}), f32[256,256]{0,1:T(8,128)}) %all-reduce.15.cloned.1.call-update) | async-done | bytes 262160 | tf_op jit(solution)/shard_map/psum | solution.py:9
  226.8 37.5 %all-reduce.13.cloned.1.call-done = f32[1,256,256]{1,2,0:T(8,128)} async-done(((f32[1,256,256]{1,2,0:T(8,128)}), f32[1,256,256]{1,2,0:T(8,128)}) %all-reduce.13.cloned.1.call-update) | async-done | bytes 262160 | tf_op jit(solution)/shard_map/psum | solution.py:9
  264.4 2.1 broadcast_select_fusion
  266.6 90.4 %all-reduce.17.cloned.1.call-done = f32[256,256]{0,1:T(8,128)} async-done(((f32[256,256]{0,1:T(8,128)}), f32[256,256]{0,1:T(8,128)}) %all-reduce.17.cloned.1.call-update) | async-done | bytes 262160 | tf_op jit(solution)/shard_map/psum | solution.py:9
  357.0 1.1 copy.34
  358.2 11.7 %cholesky.164 = f32[128,128]{1,0:T(8,128)S(1)} custom-call(f32[128,128]{1,0:T(8,128)S(1)} %cholesky.197), custom_call_target="Cholesky" | custom-call | tf_op jit(solution)/shard_map/jit(cholesky)/cholesky | solution.py:57
  370.1 9.8 %custom-call.18 = f32[1,128,128]{1,2,0:T(8,128)S(1)} custom-call(f32[1,128,128]{2,1,0:T(8,128)S(1)} %get-tuple-element.91), custom_call_target="InvertDiagBlocksLowerTriangular" | custom-call | tf_op jit(solution)/shard_map/jit(cholesky)/cholesky | solution.py:57
  380.5 11.7 %cholesky.181 = f32[128,128]{1,0:T(8,128)S(1)} custom-call(f32[128,128]{1,0:T(8,128)S(1)} %convolution_subtract_fusion.4), custom_call_target="Cholesky" | custom-call | tf_op jit(solution)/shard_map/jit(cholesky)/cholesky | solution.py:57
  395.0 4.4 while.9
  395.9 1.4 dynamic-slice.18
  398.0 1.4 dynamic-slice.18
  399.5 19.7 %custom-call.19 = f32[2,128,128]{1,2,0:T(8,128)S(1)} custom-call(f32[2,128,128]{2,1,0:T(8,128)S(1)} %get-tuple-element.32), custom_call_target="InvertDiagBlocksLowerTriangular" | custom-call | tf_op jit(solution)/shard_map/jit(_solve_triangular)/triangular_solve | solution.py:13
  422.0 0.8 fusion.10
  422.8 31.8 %all-reduce.21.cloned.1.call-done = f32[256,256]{0,1:T(8,128)} async-done(((f32[256,256]{0,1:T(8,128)}), f32[256,256]{0,1:T(8,128)}) %all-reduce.21.cloned.1.call-update) | async-done | bytes 262160 | tf_op jit(solution)/shard_map/psum | solution.py:9
  454.5 37.7 %all-reduce.19.cloned.1.call-done = f32[1,256,256]{1,2,0:T(8,128)} async-done(((f32[1,256,256]{1,2,0:T(8,128)}), f32[1,256,256]{1,2,0:T(8,128)}) %all-reduce.19.cloned.1.call-update) | async-done | bytes 262160 | tf_op jit(solution)/shard_map/psum | solution.py:9
  492.2 1.4 fusion.3
  493.9 0.8 copy.43
  494.9 1.0 copy.44
  (98 shorter events, 13.3 us)
Async XLA Ops:
  7.2 29.6 %all-reduce.9.cloned.1.call-start = ((), (), s32[]{:S(2)}) async-start(), calls=%async_computation | async-start | bytes 524288 | tf_op jit(solution)/shard_map/psum | solution.py:34
  9.0 120.8 %all-reduce.11.cloned.1.call-start = ((), (), s32[]{:S(2)}) async-start(), calls=%async_computation.1 | async-start | bytes 524288 | tf_op jit(solution)/shard_map/psum | solution.py:9
  38.4 188.4 %all-reduce.15.cloned.1.call-start = ((), (), s32[]{:S(2)}) async-start(), calls=%async_computation.3 | async-start | bytes 524288 | tf_op jit(solution)/shard_map/psum | solution.py:9
  129.9 1.2 copy-start.2
  167.3 24.1 %copy-start = (f32[1,256,1,256]{1,3,2,0:T(8,128)S(1)}, f32[1,256,1,256]{1,3,2,0:T(8,128)}, u32[]{:S(2)}) copy-start(f32[1,256,1,256]{1,3,2,0:T(8,128)} %all-reduce.9.cloned.1.call-done) | copy-start | bytes 786436
  194.2 70.2 %all-reduce.13.cloned.1.call-start = ((), (), s32[]{:S(2)}) async-start(), calls=%async_computation.2 | async-start | bytes 524288 | tf_op jit(solution)/shard_map/psum | solution.py:9
  195.0 162.0 %all-reduce.17.cloned.1.call-start = ((), (), s32[]{:S(2)}) async-start(), calls=%async_computation.4 | async-start | bytes 524288 | tf_op jit(solution)/shard_map/psum | solution.py:9
  195.1 0.7 copy-start.5
  266.5 188.0 %all-reduce.21.cloned.1.call-start = ((), (), s32[]{:S(2)}) async-start(), calls=%async_computation.6 | async-start | bytes 524288 | tf_op jit(solution)/shard_map/psum | solution.py:9
  357.0 1.2 copy-start.1
  421.9 70.3 %all-reduce.19.cloned.1.call-start = ((), (), s32[]{:S(2)}) async-start(), calls=%async_computation.5 | async-start | bytes 524288 | tf_op jit(solution)/shard_map/psum | solution.py:9
  493.8 1.0 copy-start.3
  493.8 1.0 copy-start.4
Sparse Core Ops, SparseCore 0:
  10.8 25.8 all-reduce.8
  41.1 88.7 all-reduce.10
  194.3 32.4 all-reduce.14
  229.0 35.2 all-reduce.12
  268.5 88.4 all-reduce.16
  422.0 32.4 all-reduce.20
  456.9 35.2 all-reduce.18
where the time goes:
time: 503 us
  waiting for transfers between devices  347 us (69%)
  other arithmetic  113 us (22%)
  between operations  17.2 us (3%)
  local copies, waits for them, and re-layouts  16.3 us (3%)
  matrix products  8.29 us (2%)
    psum x6, waiting for transfers between devices, broadcast(): return lax.psum(block, axis)  319 us
    another operation x13, other arithmetic, on_device(): diag_factor = jnp.linalg.cholesky(diagonal)  68.7 us
    another operation x5, other arithmetic, right_solve(): return jax.scipy.linalg.solve_triangular(diag_factor, block.T, lower=True).T  39.4 us
    psum x1, waiting for transfers between devices, on_device(): front_sum = lax.psum(own_part, 'layer')  27.7 us
  transfers between devices with their start and end apart: 7, of which 7 were waited for; matrix products, arithmetic and copies ran while one was open for 0% of the time, Pallas kernels for 0%

commit v1 on v0

v1 whole, which is shorter than its diff:
```python
import functools

import jax
import jax.numpy as jnp
from jax import lax
from jax.experimental import pallas as pl
from jax.experimental.pallas import tpu as pltpu
from jax.sharding import PartitionSpec as P

F32 = jnp.float32
SUB = 8
NT = (((1,), (1,)), ((), ()))
NN = (((1,), (0,)), ((), ()))


def dot(a, b, dims=NN):
    return lax.dot_general(
        a, b, dims, precision=lax.Precision.HIGHEST, preferred_element_type=F32
    )


def lane_splat(x, lane):
    return jnp.broadcast_to(x[:, lane : lane + 1], x.shape)


def row_splat(x, row):
    return jnp.broadcast_to(x[row : row + 1, :], x.shape)


def recip(x):
    return pl.reciprocal(x, approx=True)


def total(terms):
    while len(terms) > 1:
        terms = [terms[i] + terms[i + 1] for i in range(0, len(terms), 2)]
    return terms[0]


def factor_rows(rows):
    groups = len(rows)
    sub = lax.broadcasted_iota(jnp.int32, rows[0].shape, 0)
    lane = lax.broadcasted_iota(jnp.int32, rows[0].shape, 1)
    here = [sub == j for j in range(SUB)]
    held = list(rows)
    out = []
    cols = [lane_splat(held[0], k) for k in range(SUB)]
    for b in range(groups):
        y = held[b]
        near = range(b + 1, min(b + 3, groups))
        side = {g: [lane_splat(held[g], b * SUB + k) for k in range(SUB)] for g in near}
        below = {g: [lane_splat(held[g], b * SUB + k) for k in range(SUB)] for g in range(b + 3, groups)}
        if b + 1 < groups:
            ahead = [lane_splat(held[b + 1], (b + 1) * SUB + k) for k in range(SUB)]
        done = jnp.zeros_like(y)
        for j in range(0, SUB, 2):
            c0, c1 = cols[j], cols[j + 1]
            p, q, s = row_splat(c0, j), row_splat(c1, j), row_splat(c1, j + 1)
            r = recip(p * s - q * q)
            m0 = jnp.where(here[j], c0 - 1.0, c0)
            m1 = jnp.where(here[j + 1], c1 - 1.0, c1)
            for k in range(j + 2, SUB):
                a0, a1 = row_splat(cols[k], j), row_splat(cols[k], j + 1)
                n0, n1 = s * a0 - q * a1, p * a1 - q * a0
                cols[k] = cols[k] - (m0 * n0 + m1 * n1) * r
                for g in near:
                    side[g][k] = side[g][k] - (side[g][j] * n0 + side[g][j + 1] * n1) * r
            if b + 1 < groups:
                s0, s1 = side[b + 1][j], side[b + 1][j + 1]
                for k in range(SUB):
                    a0, a1 = row_splat(s0, k), row_splat(s1, k)
                    n0, n1 = s * a0 - q * a1, p * a1 - q * a0
                    ahead[k] = ahead[k] - (s0 * n0 + s1 * n1) * r
            y0, y1 = row_splat(y, j), row_splat(y, j + 1)
            w0, w1 = (s * y0 - q * y1) * r, (p * y1 - q * y0) * r
            for g in near:
                held[g] = held[g] - (side[g][j] * w0 + side[g][j + 1] * w1)
            y = y - (m0 * w0 + m1 * w1)
            root0 = lax.rsqrt(p)
            ratio = q * root0 * root0
            root1 = lax.rsqrt(s - q * ratio)
            done = jnp.where(here[j], y0 * root0, done)
            done = jnp.where(here[j + 1], (y1 - ratio * y0) * root1, done)
        out.append(jnp.where(lane >= sub + b * SUB, done, 0.0))
        if b + 1 == groups:
            break
        cols = ahead
        yk = [row_splat(y, k) for k in range(SUB)]
        for g, c in below.items():
            held[g] = held[g] - total([c[k] * yk[k] for k in range(SUB)])
    return out


def tile_rows(tile):
    return [tile[g * SUB : (g + 1) * SUB, :] for g in range(tile.shape[0] // SUB)]


def factor(tile, lower_ref, inverse_ref, work):
    order = tile.shape[0]
    half = order // 2
    at_row = lax.broadcasted_iota(jnp.int32, tile.shape, 0)
    at_col = lax.broadcasted_iota(jnp.int32, tile.shape, 1)
    diagonal = jnp.sum(jnp.where(at_row == at_col, tile, 0.0), axis=0, keepdims=True)
    scale = jnp.broadcast_to(lax.rsqrt(diagonal), tile.shape)
    down = scale.T
    a = tile * scale * down
    one = jnp.where(at_row[:half, :half] == at_col[:half, :half], 1.0, 0.0).astype(F32)
    beside = jnp.where(at_row[:half] + half == at_col[:half], 1.0, 0.0).astype(F32)
    work[half:, :half] = a[half:, half:]
    work[half:, half:] = one
    first = jnp.concatenate(factor_rows(tile_rows(jnp.where(at_col[:half] < half, a[:half], beside))), axis=0)
    inverse0 = first[:, half:]
    under = dot(a[half:, :half], inverse0, NT)
    work[half:, :half] -= dot(under, under, NT)
    second = jnp.concatenate(factor_rows(tile_rows(work[half:, :])), axis=0)
    inverse1 = second[:, half:]
    inverse_ref[:half, :half] = inverse0 * scale[:half, :half]
    inverse_ref[:half, half:] = jnp.zeros((half, half), F32)
    inverse_ref[half:, :half] = -dot(inverse1, dot(under, inverse0)) * scale[half:, :half]
    inverse_ref[half:, half:] = inverse1 * scale[half:, half:]
    work[:half, :] = jnp.where(at_col[:half] < half, first, 0.0)
    work[half:, :half] = jnp.zeros((half, half), F32)
    work[half:, half:] = second[:, :half]
    up = recip(down)
    lower_ref[...] = work[...].T * up
    lower_ref[half:, :half] = under * up[half:, :half]


def pack_kernel(index_ref, source_ref, mine_ref, *refs):
    *send_refs, linear_ref, arrived = refs
    layer = index_ref[0]
    first = (index_ref[1] == 0) & (index_ref[2] == 0)
    height, tile = mine_ref.shape
    piece = linear_ref.shape[0] // (len(send_refs) + 1)
    out_refs = (mine_ref, *send_refs)

    @pl.when(first)
    def _():
        load = pltpu.make_async_copy(source_ref, linear_ref, arrived.at[0])
        load.start()
        load.wait()
        at_row = lax.broadcasted_iota(jnp.int32, (tile, tile), 0)
        at_col = lax.broadcasted_iota(jnp.int32, (tile, tile), 1)
        corner = linear_ref[pl.ds(2 * tile + 1, tile, 2), :]
        mixed = jnp.where(at_row >= at_col, linear_ref[pl.ds(0, tile, 2), :], corner)
        below = linear_ref[pl.ds(2 * tile, tile, 2), :]
        diagonal = jnp.sum(jnp.where(at_row == at_col, corner, 0.0), axis=0, keepdims=True)
        for ref in out_refs:
            ref[:tile, :] = mixed
            ref[tile : 2 * tile, :] = below
            ref[2 * tile :, :] = jnp.broadcast_to(diagonal, (height - 2 * tile, tile))

    @pl.when(jnp.logical_not(first))
    def _():
        loads = []
        for k, ref in enumerate(out_refs):
            start = pl.multiple_of((layer ^ k) * piece, piece)
            from_ref = source_ref.at[pl.ds(start, piece), :]
            loads.append(pltpu.make_async_copy(from_ref, ref.at[pl.ds(0, piece), :], arrived.at[k]))
            loads[-1].start()
        for ref in out_refs:
            ref[piece:, :] = jnp.zeros((height - piece, tile), F32)
        for load in loads:
            load.wait()


def unpack(pieces, to_ref):
    tile = pieces[0].shape[1]
    slab = pieces[0].shape[0] // 2
    for t, piece in enumerate(pieces):
        to_ref[t * slab : (t + 1) * slab, :tile] = piece[pl.ds(0, slab, 2), :]
        to_ref[t * slab : (t + 1) * slab, tile:] = piece[pl.ds(1, slab, 2), :]


def symmetric(lower, keep):
    part = jnp.where(keep, lower, 0.0)
    at = lax.broadcasted_iota(jnp.int32, lower.shape, 0) == lax.broadcasted_iota(jnp.int32, lower.shape, 1)
    return part + jnp.where(at, 0.0, part).T


def first_kernel(packed_ref, block_ref, lower_ref, inverse_ref, left_ref, rest_ref, work):
    tile = packed_ref.shape[1]
    at_row = lax.broadcasted_iota(jnp.int32, (tile, tile), 0)
    at_col = lax.broadcasted_iota(jnp.int32, (tile, tile), 1)
    mixed = packed_ref[:tile, :]
    below = packed_ref[tile : 2 * tile, :]
    tile0 = symmetric(mixed, at_row >= at_col)
    upper1 = jnp.where(at_row < at_col, mixed, 0.0)
    diagonal = jnp.broadcast_to(packed_ref[2 * tile : 2 * tile + 1, :], (tile, tile))
    tile1 = upper1 + upper1.T + jnp.where(at_row == at_col, diagonal, 0.0)
    block_ref[:tile, :tile] = tile0
    block_ref[tile:, :tile] = below
    block_ref[:tile, tile:] = below.T
    block_ref[tile:, tile:] = tile1
    factor(tile0, lower_ref, inverse_ref, work)
    left = dot(below, inverse_ref[...], NT)
    left_ref[...] = left
    rest_ref[...] = tile1 - dot(left, left, NT)


def second_kernel(lower0_ref, inverse0_ref, left_ref, rest_ref, lower_ref, inverse_ref, work):
    tile = rest_ref.shape[0]
    zero = jnp.zeros((tile, tile), F32)
    first, second = slice(0, tile), slice(tile, 2 * tile)
    lower_ref[first, first] = lower0_ref[...]
    lower_ref[first, second] = zero
    lower_ref[second, first] = left_ref[...]
    inverse_ref[first, first] = inverse0_ref[...]
    inverse_ref[first, second] = zero
    factor(rest_ref[...], lower_ref.at[second, second], inverse_ref.at[second, second], work)
    inverse_ref[second, first] = -dot(inverse_ref[second, second], dot(left_ref[...], inverse0_ref[...]))


def third_kernel(
    lead_ref, inverse0_ref, left_ref, lower_ref, inverse_ref, under_ref, rest_ref,
    corner_ref, below_ref, work,
):
    tile = lower_ref.shape[0]
    unpack([lead_ref.at[t, 0] for t in range(lead_ref.shape[0])], below_ref)
    unpack([lead_ref.at[t, 1] for t in range(lead_ref.shape[0])], corner_ref)
    left_ref[...] = dot(below_ref[...], inverse0_ref[...], NT)
    top, bottom = left_ref[:tile, :], left_ref[tile:, :]
    factor(corner_ref[:tile, :tile] - dot(top, top, NT), lower_ref, inverse_ref, work)
    under = dot(corner_ref[tile:, :tile] - dot(bottom, top, NT), inverse_ref[...], NT)
    under_ref[...] = under
    rest_ref[...] = corner_ref[tile:, tile:] - dot(bottom, bottom, NT) - dot(under, under, NT)


def fourth_kernel(
    left_ref, inverse0_ref, lower0_ref, small_ref, under_ref, rest_ref, lower_ref, inverse_ref, cross_ref, work
):
    second_kernel(lower0_ref, small_ref, under_ref, rest_ref, lower_ref, inverse_ref, work)
    cross_ref[...] = -dot(inverse_ref[...], dot(left_ref[...], inverse0_ref[...]))


def final_kernel(
    index_ref, keep_ref, own_ref, block_ref, rows_ref, cols_ref,
    lower0_ref, inverse0_ref, lower1_ref, inverse1_ref, left_ref, cross_ref,
    schur_ref, panels_ref, upper_ref, row_ref,
):
    layer, row, col = index_ref[0], index_ref[1], index_ref[2]
    width = upper_ref.shape[1]
    tiles_per = keep_ref.shape[0]
    tile = width // tiles_per
    slabs = rows_ref.shape[0]
    slab_rows = width // slabs

    @pl.when(row == 0)
    def _():
        panels_ref[0] = lower0_ref[...]
        panels_ref[1] = jnp.zeros((width, width), F32)

    @pl.when(row == 1)
    def _():
        panels_ref[0] = left_ref[...]
        panels_ref[1] = lower1_ref[...]

    @pl.when(row > 1)
    def _():
        for k in range(2):
            unpack([rows_ref.at[t, k] for t in range(slabs)], row_ref.at[k])
        panels_ref[0] = dot(row_ref[0], inverse0_ref[...], NT)
        panels_ref[1] = dot(row_ref[0], cross_ref[...], NT) + dot(row_ref[1], inverse1_ref[...], NT)

    @pl.when(col == 0)
    def _():
        upper_ref[...] = jnp.zeros(upper_ref.shape, F32)

    @pl.when(col == 1)
    def _():
        upper_ref[:width, :] = left_ref[...].T
        upper_ref[width:, :] = jnp.zeros((width, width), F32)

    @pl.when(col > 1)
    def _():
        for k in range(2):
            unpack([cols_ref.at[t, k] for t in range(slabs)], row_ref.at[k])
        upper_ref[:width, :] = dot(inverse0_ref[...], row_ref[0])
        upper_ref[width:, :] = dot(cross_ref[...], row_ref[0]) + dot(inverse1_ref[...], row_ref[1])

    slab = pl.ds(pl.multiple_of(layer * slab_rows, slab_rows), slab_rows)
    product = dot(panels_ref[0, slab, :], upper_ref[:width, :]) + dot(panels_ref[1, slab, :], upper_ref[width:, :])
    at_row = (lax.broadcasted_iota(jnp.int32, (slab_rows, tile), 0) + layer * slab_rows) // tile
    for j in range(tiles_per):
        keep = jnp.zeros((slab_rows, tile), jnp.int32)
        for i in range(tiles_per):
            keep = jnp.where(at_row == i, keep_ref[i, j], keep)
        own = own_ref[pl.ds(j, slab_rows, tiles_per), :]
        at = slice(j * tile, (j + 1) * tile)
        own = jnp.where((row == 0) & (col == 0), block_ref[slab, at], own)
        schur_ref[pl.ds(j, slab_rows, tiles_per), :] = own - jnp.where(keep > 0, product[:, at], 0.0)


AXES = ("layer", "row", "col")


def trade(x, axis, k):
    return lax.ppermute(x, axis, [(i, i ^ k) for i in range(lax.axis_size(axis))])


def ask_layers(x, members=None):
    parts = [x]
    layers, rows, cols = (lax.axis_size(a) for a in AXES)
    for k in range(1, layers):
        if members is None:
            parts.append(trade(x, "layer", k))
        else:
            pairs = [
                (((i * rows) + r) * cols + c, (((i ^ k) * rows) + r) * cols + c)
                for i in range(layers)
                for r, c in members
            ]
            parts.append(lax.ppermute(x, AXES, pairs))
    return parts


def in_order(parts, *late):
    layer = lax.axis_index("layer").astype(jnp.int32)
    parts = parts[:1] + [after(part, *late) for part in parts[1:]]
    ordered = []
    for t in range(len(parts)):
        held = parts[0]
        for k in range(1, len(parts)):
            held = jnp.where(layer ^ t == k, parts[k], held)
        ordered.append(held)
    return jnp.stack(ordered)


def strides(count, least):
    step = 1
    while 2 * step < count:
        step *= 2
    out = []
    while step >= least:
        out.append(step)
        step //= 2
    return out


def after(x, *others):
    return lax.optimization_barrier((x,) + others)[0]


def run(kernel, outs, ins, scratch=(), flops=0, name=None, smem=0, source=pltpu.VMEM):
    vmem = pl.BlockSpec(memory_space=pltpu.VMEM)
    ins_at = [pl.BlockSpec(memory_space=pltpu.SMEM)] * smem + [pl.BlockSpec(memory_space=source)] * (len(ins) - smem)
    return pl.pallas_call(
        kernel,
        out_shape=tuple(jax.ShapeDtypeStruct(s, F32) for s in outs),
        in_specs=ins_at,
        out_specs=tuple(vmem for _ in outs),
        scratch_shapes=[pltpu.VMEM(s, F32) if isinstance(s, tuple) else s for s in scratch],
        compiler_params=pltpu.CompilerParams(vmem_limit_bytes=24 * 1024 * 1024),
        cost_estimate=pl.CostEstimate(flops=flops, bytes_accessed=10**6, transcendentals=0),
        name=name,
    )(*ins)


def on_device(partials, pattern):
    layers, rows, cols = (lax.axis_size(a) for a in AXES)
    layer, row, col = (lax.axis_index(a).astype(jnp.int32) for a in AXES)
    width = partials.shape[3]
    tiles_per = pattern.shape[2]
    tile = width // tiles_per
    slab_rows = width // layers
    piece_rows = slab_rows * tiles_per
    height = 2 * tile + SUB
    even_row, even_col = row % 2 == 0, col % 2 == 0
    index = jnp.stack([layer, row, col])
    square, big = (tile, tile), (width, width)

    mine, *sends = run(
        pack_kernel,
        ((height, tile),) * layers,
        (index, pltpu.with_memory_space_constraint(partials.reshape(width * tiles_per, tile), pltpu.HBM)),
        scratch=((width * tiles_per, tile), pltpu.SemaphoreType.DMA((layers,))),
        name="k0",
        smem=1,
        source=pltpu.HBM,
    )
    front = total([mine] + [trade(x, "layer", k + 1) for k, x in enumerate(sends)])
    piece = front[:piece_rows]

    keep = (pattern.reshape(tiles_per, tiles_per) > 0) | (row < 2) | (col < 2)
    keep = keep.astype(jnp.int32)
    fall = after(piece, keep)
    for s in strides(rows, 2):
        fall_from, fall_got = fall, trade(fall, "row", s)
        if s > 2:
            fall = jnp.where(row % (2 * s) >= s, fall_got, fall_from)

    lead = front
    for s in strides(cols, 2):
        lead = jnp.where(col % (2 * s) >= s, trade(lead, "col", s), lead)
    fall_got = after(fall_got, lead)
    fall = jnp.where(row % 4 >= 2, fall_got, fall_from)
    lead = after(lead, fall_got)
    fall = after(fall, lead)
    fall_other = trade(fall, "row", 1)
    got = trade(lead, "col", 1)
    low, high = jnp.where(even_col, lead, got), jnp.where(even_col, got, lead)
    panels_in = jnp.stack([low[:piece_rows], high[:piece_rows]])
    high = high[:piece_rows]

    low = after(low, fall_other)
    high = after(high, low)
    cols_in = ask_layers(
        jnp.stack([jnp.where(even_row, fall, fall_other), jnp.where(even_row, fall_other, fall)])
    )
    for s in strides(rows, 2):
        low = jnp.where(row % (2 * s) >= s, trade(low, "row", s), low)
    for s in strides(rows, 2):
        high_from, high_got = high, trade(high, "row", s)
        if s > 2:
            high = jnp.where(row % (2 * s) >= s, high_got, high_from)
    high = jnp.where(row % 4 >= 2, after(high_got, low), high_from)
    packed = jnp.where(even_row, low, trade(low, "row", 1))
    lead = jnp.stack([low[:piece_rows], high])
    lead_parts = ask_layers(lead, [(r, c) for r in range(1, rows, 2) for c in range(cols)])
    packed = after(packed, high)

    block0, small_lower, small_inverse, left0, rest0 = run(
        first_kernel,
        (big, square, square, square, square),
        (packed,),
        scratch=(square,),
        flops=5 * 10**9,
        name="k1",
    )
    lead = in_order(lead_parts, rest0)
    lead_other = trade(lead, "row", 1)
    rows_in = ask_layers(after(panels_in, lead))

    lower0, inverse0 = run(
        second_kernel,
        (big, big),
        (small_lower, small_inverse, left0, after(rest0, lead)),
        scratch=(square,),
        flops=5 * 10**9,
        name="k2",
    )
    lead_other = after(lead_other, inverse0)
    lead = jnp.where(even_row, lead_other, lead)
    left1, small_lower, small_inverse, under, rest1 = run(
        third_kernel,
        (big, square, square, square, square),
        (lead, inverse0),
        scratch=(big, big, square),
        flops=5 * 10**9,
        name="k3",
    )
    lower1, inverse1, cross = run(
        fourth_kernel,
        (big, big, big),
        (left1, inverse0, small_lower, small_inverse, under, rest1),
        scratch=(square,),
        flops=5 * 10**9,
        name="k4",
    )
    rows_in, cols_in = in_order(rows_in, cross), in_order(cols_in, cross)
    schur, panels = run(
        final_kernel,
        ((piece_rows, tile), (2, width, width)),
        (index, keep, piece, block0, rows_in, cols_in, lower0, inverse0, lower1, inverse1, left1, cross),
        scratch=((2 * width, width), (2, width, width)),
        flops=10**9,
        name="kf",
        smem=2,
    )
    return (
        schur.reshape(1, 1, 1, slab_rows, 1, 1, width),
        panels.reshape(2, 1, 1, width, width),
    )


def solution(mesh):
    return jax.shard_map(
        on_device,
        mesh=mesh,
        in_specs=(
            P("layer", None, "row", None, None, "col", None),
            P(None, "row", None, None, "col", None),
        ),
        out_specs=(
            P(None, "row", "layer", None, None, "col", None),
            P(None, None, "row", None, None),
        ),
        check_vma=False,
    )
```

time: 503 us -> 55 us (0.11)
  waiting for transfers between devices: 347 us -> 16.9 us
  other arithmetic: 113 us -> 0.58 us
  Pallas kernels: 0 us -> 20.3 us
  between operations: 17.2 us -> 0.89 us
  local copies, waits for them, and re-layouts: 16.3 us -> 0.03 us
  starting transfers between devices: 0.29 us -> 15.9 us
  matrix products: 8.29 us -> 0 us
    psum x7 -> x0, waiting for transfers between devices: 347 us -> none  [the longest x6 319 us: broadcast(): return lax.psum(block, axis)]
    another operation x18 -> x10, other arithmetic: 108 us -> 0.38 us  [the longest x5 0.22 us: in_order(): return jnp.stack(ordered)]
    pallas_call x0 -> x6, Pallas kernels: none -> 20.3 us  [run(): pl.pallas_call(kernel, out_shape=tuple((jax.ShapeDtypeStruct(s, F32) for...]
    ppermute x0 -> x12, waiting for transfers between devices: none -> 16.9 us  [the longest x11 16.9 us: trade(): lax.ppermute(x, axis, [(i, i ^ k) for i in range(lax.axis_size(axis))])]
    ppermute x0 -> x12, starting transfers between devices: none -> 15.9 us  [the longest x11 15.2 us: trade(): lax.ppermute(x, axis, [(i, i ^ k) for i in range(lax.axis_size(axis))])]
    another operation x39 -> x2, local copies, waits for them, and re-layouts: 9.1 us -> 0.02 us  [the longest x1 0.01 us: on_device(): lead = jnp.stack([low[:piece_rows], high])]
  transfers between devices with their start and end apart: 7 -> 12, of which waited for: 7 -> 6; matrix products, arithmetic and copies ran while one was open for 0% -> 1% of each run, Pallas kernels for 0% -> 31%
where the time goes in v1:
time: 55 us; the launch traced here: 54.6 us
  Pallas kernels  20.3 us (37%)
  waiting for transfers between devices  16.9 us (31%)
  starting transfers between devices  15.9 us (29%)
  between operations  0.89 us (2%)
  other arithmetic  0.58 us (1%)
    pallas_call x6, Pallas kernels, run(): pl.pallas_call(kernel, out_shape=tuple((jax.ShapeDtypeStruct(s, F32) for...  20.3 us
    ppermute x11, waiting for transfers between devices, trade(): lax.ppermute(x, axis, [(i, i ^ k) for i in range(lax.axis_size(axis))])  16.9 us
    ppermute x11, starting transfers between devices, trade(): lax.ppermute(x, axis, [(i, i ^ k) for i in range(lax.axis_size(axis))])  15.2 us
  transfers between devices with their start and end apart: 12, of which 6 were waited for; matrix products, arithmetic and copies ran while one was open for 1% of the time, Pallas kernels for 31%

profile of v1, /device:TPU:0, one launch (start us, length us, event | category | flops | bytes accessed | tf_op | source)
XLA Modules:
  0.0 54.6 jit_solution(13262100597717252505)
XLA Ops:
  0.6 0.1 pad_add_fusion.index_ref
  0.7 1.5 %k0.1 = (f32[264,128]{1,0:T(8,128)S(1)}, f32[264,128]{1,0:T(8,128)S(1)}) custom-call(s32[3]{0:T(128)S(1)} %pad_add_fusion.index_ref, f32[512,128]{1,0:T(8,128)} %bitcast.35), custom_call_target="tpu_custom_call" | custom-call | bytes 1000000 | tf_op jit(solution)/shard_map/k0/pallas_call | solution.py:347
  2.3 3.0 %collective-permute-start = (f32[264,128]{1,0:T(8,128)S(1)}, f32[264,128]{1,0:T(8,128)S(1)}, u32[]{:S(2)}, u32[]{:S(2)}) collective-permute-start(f32[264,128]{1,0:T(8,128)S(1)} %get-tuple-element.36), channel_id=1, source_target_pairs={{0,16},{16,0},{1,17},{17,1},{2,18},{18,2},{3,19},{19,3},{4,20},{20... | collective-permute-start | bytes 405512 | tf_op jit(solution)/shard_map/ppermute | solution.py:298
  5.3 3.6 %collective-permute-done = f32[264,128]{1,0:T(8,128)S(1)} collective-permute-done((f32[264,128]{1,0:T(8,128)S(1)}, f32[264,128]{1,0:T(8,128)S(1)}, u32[]{:S(2)}, u32[]{:S(2)}) %collective-permute-start) | collective-permute-done | bytes 135200 | tf_op jit(solution)/shard_map/ppermute | solution.py:298
  8.9 2.9 %collective-permute-start.1 = (f32[264,128]{1,0:T(8,128)S(1)}, f32[264,128]{1,0:T(8,128)S(1)}, u32[]{:S(2)}, u32[]{:S(2)}) collective-permute-start(f32[264,128]{1,0:T(8,128)S(1)} %add.18), channel_id=1, source_target_pairs={{0,2},{1,3},{2,0},{3,1},{4,6},{5,7},{6,4},{7,5},{8,10},{9,11},{10,... | collective-permute-start | bytes 405512 | tf_op jit(solution)/shard_map/ppermute | solution.py:298
  11.8 1.6 %collective-permute-start.2 = (f32[256,128]{1,0:T(8,128)S(1)}, f32[256,128]{1,0:T(8,128)S(1)}, u32[]{:S(2)}, u32[]{:S(2)}) collective-permute-start(f32[256,128]{1,0:T(8,128)S(1)} %slice.17.own_ref), channel_id=1, source_target_pairs={{0,8},{4,12},{8,0},{12,4},{1,9},{5,13},{9,1},{13,5},{2,10},{6,14},... | collective-permute-start | bytes 393224 | tf_op jit(solution)/shard_map/ppermute | solution.py:298
  13.4 4.1 %collective-permute-done.1 = f32[264,128]{1,0:T(8,128)S(1)} collective-permute-done((f32[264,128]{1,0:T(8,128)S(1)}, f32[264,128]{1,0:T(8,128)S(1)}, u32[]{:S(2)}, u32[]{:S(2)}) %collective-permute-start.1) | collective-permute-done | bytes 135200 | tf_op jit(solution)/shard_map/ppermute | solution.py:298
  17.5 0.0 collective-permute-done.2
  17.5 0.1 collective-permute-start.4
  17.7 0.9 %collective-permute-start.3 = (f32[264,128]{1,0:T(8,128)S(1)}, f32[264,128]{1,0:T(8,128)S(1)}, u32[]{:S(2)}, u32[]{:S(2)}) collective-permute-start(f32[264,128]{1,0:T(8,128)S(1)} %broadcast_select_fusion.1), channel_id=1, source_target_pairs={{0,1},{1,0},{2,3},{3,2},{4,5},{5,4},{6,7},{7,6},{8,9},{9,8},{10,11... | collective-permute-start | bytes 405512 | tf_op jit(solution)/shard_map/ppermute | solution.py:298
  18.6 0.4 collective-permute-done.4
  19.0 1.5 %collective-permute-start.11 = (f32[2,256,128]{2,1,0:T(8,128)S(1)}, f32[2,256,128]{2,1,0:T(8,128)S(1)}, u32[]{:S(2)}, u32[]{:S(2)}) collective-permute-start(f32[2,256,128]{2,1,0:T(8,128)S(1)} %pad_maximum_fusion.5), channel_id=1, source_target_pairs={{0,16},{16,0},{1,17},{17,1},{2,18},{18,2},{3,19},{19,3},{4,20},{20... | collective-permute-start | bytes 786440 | tf_op jit(solution)/shard_map/ppermute | solution.py:298
  20.5 3.1 %collective-permute-done.3 = f32[264,128]{1,0:T(8,128)S(1)} collective-permute-done((f32[264,128]{1,0:T(8,128)S(1)}, f32[264,128]{1,0:T(8,128)S(1)}, u32[]{:S(2)}, u32[]{:S(2)}) %collective-permute-start.3) | collective-permute-done | bytes 135200 | tf_op jit(solution)/shard_map/ppermute | solution.py:298
  23.7 1.5 %collective-permute-start.5 = (f32[264,128]{1,0:T(8,128)S(1)}, f32[264,128]{1,0:T(8,128)S(1)}, u32[]{:S(2)}, u32[]{:S(2)}) collective-permute-start(f32[264,128]{1,0:T(8,128)S(1)} %broadcast_select_fusion.2), channel_id=1, source_target_pairs={{0,8},{4,12},{8,0},{12,4},{1,9},{5,13},{9,1},{13,5},{2,10},{6,14},... | collective-permute-start | bytes 405512 | tf_op jit(solution)/shard_map/ppermute | solution.py:298
  25.2 0.6 %collective-permute-start.7 = (f32[256,128]{1,0:T(8,128)S(1)}, f32[256,128]{1,0:T(8,128)S(1)}, u32[]{:S(2)}, u32[]{:S(2)}) collective-permute-start(f32[256,128]{1,0:T(8,128)S(1)} %slice_select_fusion), channel_id=1, source_target_pairs={{0,8},{4,12},{8,0},{12,4},{1,9},{5,13},{9,1},{13,5},{2,10},{6,14},... | collective-permute-start | bytes 393224 | tf_op jit(solution)/shard_map/ppermute | solution.py:298
  25.8 4.4 %collective-permute-done.5 = f32[264,128]{1,0:T(8,128)S(1)} collective-permute-done((f32[264,128]{1,0:T(8,128)S(1)}, f32[264,128]{1,0:T(8,128)S(1)}, u32[]{:S(2)}, u32[]{:S(2)}) %collective-permute-start.5) | collective-permute-done | bytes 135200 | tf_op jit(solution)/shard_map/ppermute | solution.py:298
  30.2 0.1 collective-permute-start.6
  30.3 1.3 %collective-permute-done.7 = f32[256,128]{1,0:T(8,128)S(1)} collective-permute-done((f32[256,128]{1,0:T(8,128)S(1)}, f32[256,128]{1,0:T(8,128)S(1)}, u32[]{:S(2)}, u32[]{:S(2)}) %collective-permute-start.7) | collective-permute-done | bytes 131104 | tf_op jit(solution)/shard_map/ppermute | solution.py:298
  31.7 0.7 %collective-permute-start.8 = (f32[2,256,128]{2,1,0:T(8,128)S(1)}, f32[2,256,128]{2,1,0:T(8,128)S(1)}, u32[]{:S(2)}, u32[]{:S(2)}) collective-permute-start(f32[2,256,128]{2,1,0:T(8,128)S(1)} %pad_maximum_fusion.4), channel_id=1, source_target_pairs={{4,20},{5,21},{6,22},{7,23},{12,28},{13,29},{14,30},{15,31},{20,4}... | collective-permute-start | bytes 786440 | tf_op jit(solution)/shard_map/ppermute | solution.py:313
  32.4 4.1 %k1.1 = (f32[256,256]{1,0:T(8,128)S(1)}, f32[128,128]{1,0:T(8,128)S(1)}, f32[128,128]{1,0:T(8,128)S(1)}, f32[128,128]{1,0:T(8,128)S(1)}, f32[128,128]{1,0:T(8,128)S(1)}) custom-call(f32[264,128]{1,0:T(8,128)S(1)} %broadcast_select_fusion.4.packed_ref), custom_call_target="tpu_custom_call" | custom-call | flops 5000000000 | bytes 1000000 | tf_op jit(solution)/shard_map/k1/pallas_call | solution.py:347
  36.6 0.0 collective-permute-done.8
  36.7 1.6 %collective-permute-start.10 = (f32[2,2,256,128]{3,2,1,0:T(8,128)S(1)}, f32[2,2,256,128]{3,2,1,0:T(8,128)S(1)}, u32[]{:S(2)}, u32[]{:S(2)}) collective-permute-start(f32[2,2,256,128]{3,2,1,0:T(8,128)S(1)} %pad_maximum_fusion), channel_id=1, source_target_pairs={{0,4},{4,0},{8,12},{12,8},{1,5},{5,1},{9,13},{13,9},{2,6},{6,2},{1... | collective-permute-start | bytes 1572872 | tf_op jit(solution)/shard_map/ppermute | solution.py:298
  38.3 1.4 %collective-permute-start.9 = (f32[2,256,128]{2,1,0:T(8,128)S(1)}, f32[2,256,128]{2,1,0:T(8,128)S(1)}, u32[]{:S(2)}, u32[]{:S(2)}) collective-permute-start(f32[2,256,128]{2,1,0:T(8,128)S(1)} %pad_maximum_fusion.3), channel_id=1, source_target_pairs={{0,16},{16,0},{1,17},{17,1},{2,18},{18,2},{3,19},{19,3},{4,20},{20... | collective-permute-start | bytes 786440 | tf_op jit(solution)/shard_map/ppermute | solution.py:298
  39.7 3.6 %k2.1 = (f32[256,256]{1,0:T(8,128)S(1)}, f32[256,256]{1,0:T(8,128)S(1)}) custom-call(f32[128,128]{1,0:T(8,128)S(1)} %get-tuple-element.49.lower0_ref, f32[128,128]{1,0:T(8,128)S(1)} %get-tuple-element.50.inverse0_ref, f32[128,128]{1,0:T(8,128)S(1)} %get-tuple-element.51.left_ref, f32[128,128]{1,0:T(8,128)S(1)} %get-tuple-element.52.rest_ref), custom_call_target="tpu_custom_call" | custom-call | flops 5000000000 | bytes 1000000 | tf_op jit(solution)/shard_map/k2/pallas_call | solution.py:347
  43.3 0.0 collective-permute-done.10
  43.3 0.1 broadcast_select_fusion.lead_ref
  43.4 4.9 %k3.1 = (f32[256,256]{1,0:T(8,128)S(1)}, f32[128,128]{1,0:T(8,128)S(1)}, f32[128,128]{1,0:T(8,128)S(1)}, f32[128,128]{1,0:T(8,128)S(1)}, f32[128,128]{1,0:T(8,128)S(1)}) custom-call(f32[2,2,256,128]{3,2,1,0:T(8,128)S(1)} %broadcast_select_fusion.lead_ref, f32[256,256]{1,0:T(8,128)S(1)} %get-tuple-element.53.inverse0_ref), custom_call_target="tpu_custom_call" | custom-call | flops 5000000000 | bytes 1000000 | tf_op jit(solution)/shard_map/k3/pallas_call | solution.py:347
  48.3 4.4 %k4.1 = (f32[256,256]{1,0:T(8,128)S(1)}, f32[256,256]{1,0:T(8,128)S(1)}, f32[256,256]{1,0:T(8,128)S(1)}) custom-call(f32[256,256]{1,0:T(8,128)S(1)} %get-tuple-element.55.left_ref, f32[256,256]{1,0:T(8,128)S(1)} %get-tuple-element.53.inverse0_ref, f32[128,128]{1,0:T(8,128)S(1)} %get-tuple-element.56.lower0_ref, f32[128,128]{1,0:T(8,128)S(1)} %get-tuple-element.57.small_ref, ...), custom_call_target="tpu_custom_call" | custom-call | flops 5000000000 | bytes 1000000 | tf_op jit(solution)/shard_map/k4/pallas_call | solution.py:347
  52.7 0.0 collective-permute-done.11
  52.7 0.0 collective-permute-done.9
  52.7 0.1 select_bitcast_fusion.1
  52.9 1.8 %kf.1 = (f32[256,128]{1,0:T(8,128)}, f32[2,256,256]{2,1,0:T(8,128)}) custom-call(s32[3]{0:T(128)S(1)} %pad_add_fusion.index_ref, s32[2,2]{1,0:T(2,128)S(1)} %bitcast.31, f32[256,128]{1,0:T(8,128)S(1)} %slice.17.own_ref, f32[256,256]{1,0:T(8,128)S(1)} %get-tuple-element.45.block_ref, f32[2,2,256,128]{3,2,1,0:T(8,128)S(1)} %pad_maximum_fusion.1.rows_ref, ...), custom_call_target="tpu_custom_call" | custom-call | flops 1000000000 | bytes 1000000 | tf_op jit(solution)/shard_map/kf/pallas_call | solution.py:347
  (23 shorter events, 0.4 us)
Async XLA Ops:
  2.3 6.6 %collective-permute-start = (f32[264,128]{1,0:T(8,128)S(1)}, f32[264,128]{1,0:T(8,128)S(1)}, u32[]{:S(2)}, u32[]{:S(2)}) collective-permute-start(f32[264,128]{1,0:T(8,128)S(1)} %get-tuple-element.36), channel_id=1, source_target_pairs={{0,16},{16,0},{1,17},{17,1},{2,18},{18,2},{3,19},{19,3},{4,20},{20... | collective-permute-start | bytes 405512 | tf_op jit(solution)/shard_map/ppermute | solution.py:298
  8.8 2.9 %copy-start = (s32[1,1,2,1,1,2]{5,4,3,2,1,0:T(1,128)S(1)}, s32[1,1,2,1,1,2]{5,4,3,2,1,0:T(1,128)}, u32[]{:S(2)}) copy-start(s32[1,1,2,1,1,2]{5,4,3,2,1,0:T(1,128)} %param.3) | copy-start | bytes 52
  8.9 8.6 %collective-permute-start.1 = (f32[264,128]{1,0:T(8,128)S(1)}, f32[264,128]{1,0:T(8,128)S(1)}, u32[]{:S(2)}, u32[]{:S(2)}) collective-permute-start(f32[264,128]{1,0:T(8,128)S(1)} %add.18), channel_id=1, source_target_pairs={{0,2},{1,3},{2,0},{3,1},{4,6},{5,7},{6,4},{7,5},{8,10},{9,11},{10,... | collective-permute-start | bytes 405512 | tf_op jit(solution)/shard_map/ppermute | solution.py:298
  11.8 5.7 %collective-permute-start.2 = (f32[256,128]{1,0:T(8,128)S(1)}, f32[256,128]{1,0:T(8,128)S(1)}, u32[]{:S(2)}, u32[]{:S(2)}) collective-permute-start(f32[256,128]{1,0:T(8,128)S(1)} %slice.17.own_ref), channel_id=1, source_target_pairs={{0,8},{4,12},{8,0},{12,4},{1,9},{5,13},{9,1},{13,5},{2,10},{6,14},... | collective-permute-start | bytes 393224 | tf_op jit(solution)/shard_map/ppermute | solution.py:298
  17.5 1.4 %collective-permute-start.4 = (f32[256,128]{1,0:T(8,128)S(1)}, f32[256,128]{1,0:T(8,128)S(1)}, u32[]{:S(2)}, u32[]{:S(2)}) collective-permute-start(f32[256,128]{1,0:T(8,128)S(1)} %broadcast_select_fusion.6), channel_id=1, source_target_pairs={{0,4},{4,0},{8,12},{12,8},{1,5},{5,1},{9,13},{13,9},{2,6},{6,2},{1... | collective-permute-start | bytes 393224 | tf_op jit(solution)/shard_map/ppermute | solution.py:298
  17.7 6.0 %collective-permute-start.3 = (f32[264,128]{1,0:T(8,128)S(1)}, f32[264,128]{1,0:T(8,128)S(1)}, u32[]{:S(2)}, u32[]{:S(2)}) collective-permute-start(f32[264,128]{1,0:T(8,128)S(1)} %broadcast_select_fusion.1), channel_id=1, source_target_pairs={{0,1},{1,0},{2,3},{3,2},{4,5},{5,4},{6,7},{7,6},{8,9},{9,8},{10,11... | collective-permute-start | bytes 405512 | tf_op jit(solution)/shard_map/ppermute | solution.py:298
  19.0 33.7 %collective-permute-start.11 = (f32[2,256,128]{2,1,0:T(8,128)S(1)}, f32[2,256,128]{2,1,0:T(8,128)S(1)}, u32[]{:S(2)}, u32[]{:S(2)}) collective-permute-start(f32[2,256,128]{2,1,0:T(8,128)S(1)} %pad_maximum_fusion.5), channel_id=1, source_target_pairs={{0,16},{16,0},{1,17},{17,1},{2,18},{18,2},{3,19},{19,3},{4,20},{20... | collective-permute-start | bytes 786440 | tf_op jit(solution)/shard_map/ppermute | solution.py:298
  23.7 6.6 %collective-permute-start.5 = (f32[264,128]{1,0:T(8,128)S(1)}, f32[264,128]{1,0:T(8,128)S(1)}, u32[]{:S(2)}, u32[]{:S(2)}) collective-permute-start(f32[264,128]{1,0:T(8,128)S(1)} %broadcast_select_fusion.2), channel_id=1, source_target_pairs={{0,8},{4,12},{8,0},{12,4},{1,9},{5,13},{9,1},{13,5},{2,10},{6,14},... | collective-permute-start | bytes 405512 | tf_op jit(solution)/shard_map/ppermute | solution.py:298
  25.2 6.5 %collective-permute-start.7 = (f32[256,128]{1,0:T(8,128)S(1)}, f32[256,128]{1,0:T(8,128)S(1)}, u32[]{:S(2)}, u32[]{:S(2)}) collective-permute-start(f32[256,128]{1,0:T(8,128)S(1)} %slice_select_fusion), channel_id=1, source_target_pairs={{0,8},{4,12},{8,0},{12,4},{1,9},{5,13},{9,1},{13,5},{2,10},{6,14},... | collective-permute-start | bytes 393224 | tf_op jit(solution)/shard_map/ppermute | solution.py:298
  30.2 2.2 %collective-permute-start.6 = (f32[264,128]{1,0:T(8,128)S(1)}, f32[264,128]{1,0:T(8,128)S(1)}, u32[]{:S(2)}, u32[]{:S(2)}) collective-permute-start(f32[264,128]{1,0:T(8,128)S(1)} %broadcast_select_fusion.3), channel_id=1, source_target_pairs={{0,4},{4,0},{8,12},{12,8},{1,5},{5,1},{9,13},{13,9},{2,6},{6,2},{1... | collective-permute-start | bytes 405512 | tf_op jit(solution)/shard_map/ppermute | solution.py:298
  31.7 4.8 %collective-permute-start.8 = (f32[2,256,128]{2,1,0:T(8,128)S(1)}, f32[2,256,128]{2,1,0:T(8,128)S(1)}, u32[]{:S(2)}, u32[]{:S(2)}) collective-permute-start(f32[2,256,128]{2,1,0:T(8,128)S(1)} %pad_maximum_fusion.4), channel_id=1, source_target_pairs={{4,20},{5,21},{6,22},{7,23},{12,28},{13,29},{14,30},{15,31},{20,4}... | collective-permute-start | bytes 786440 | tf_op jit(solution)/shard_map/ppermute | solution.py:313
  36.7 6.6 %collective-permute-start.10 = (f32[2,2,256,128]{3,2,1,0:T(8,128)S(1)}, f32[2,2,256,128]{3,2,1,0:T(8,128)S(1)}, u32[]{:S(2)}, u32[]{:S(2)}) collective-permute-start(f32[2,2,256,128]{3,2,1,0:T(8,128)S(1)} %pad_maximum_fusion), channel_id=1, source_target_pairs={{0,4},{4,0},{8,12},{12,8},{1,5},{5,1},{9,13},{13,9},{2,6},{6,2},{1... | collective-permute-start | bytes 1572872 | tf_op jit(solution)/shard_map/ppermute | solution.py:298
  38.3 14.4 %collective-permute-start.9 = (f32[2,256,128]{2,1,0:T(8,128)S(1)}, f32[2,256,128]{2,1,0:T(8,128)S(1)}, u32[]{:S(2)}, u32[]{:S(2)}) collective-permute-start(f32[2,256,128]{2,1,0:T(8,128)S(1)} %pad_maximum_fusion.3), channel_id=1, source_target_pairs={{0,16},{16,0},{1,17},{17,1},{2,18},{18,2},{3,19},{19,3},{4,20},{20... | collective-permute-start | bytes 786440 | tf_op jit(solution)/shard_map/ppermute | solution.py:298

commit v2 on v1

--- a/solution.py
+++ b/solution.py
@@ -42,39 +42,39 @@
     sub = lax.broadcasted_iota(jnp.int32, rows[0].shape, 0)
     lane = lax.broadcasted_iota(jnp.int32, rows[0].shape, 1)
     here = [sub == j for j in range(SUB)]
+    unit = [jnp.where(h, 1.0, 0.0).astype(F32) for h in here]
     held = list(rows)
     out = []
     cols = [lane_splat(held[0], k) for k in range(SUB)]
     for b in range(groups):
         y = held[b]
-        near = range(b + 1, min(b + 3, groups))
-        side = {g: [lane_splat(held[g], b * SUB + k) for k in range(SUB)] for g in near}
-        below = {g: [lane_splat(held[g], b * SUB + k) for k in range(SUB)] for g in range(b + 3, groups)}
-        if b + 1 < groups:
-            ahead = [lane_splat(held[b + 1], (b + 1) * SUB + k) for k in range(SUB)]
+        last = b + 1 == groups
+        if not last:
+            near = held[b + 1]
+            side = [lane_splat(near, b * SUB + k) for k in range(SUB)]
+            ahead = [lane_splat(near, (b + 1) * SUB + k) for k in range(SUB)]
+        below = {g: [lane_splat(held[g], b * SUB + k) for k in range(SUB)] for g in range(b + 2, groups)}
         done = jnp.zeros_like(y)
         for j in range(0, SUB, 2):
             c0, c1 = cols[j], cols[j + 1]
             p, q, s = row_splat(c0, j), row_splat(c1, j), row_splat(c1, j + 1)
             r = recip(p * s - q * q)
-            m0 = jnp.where(here[j], c0 - 1.0, c0)
-            m1 = jnp.where(here[j + 1], c1 - 1.0, c1)
+            m0, m1 = c0 - unit[j], c1 - unit[j + 1]
+            if j + 2 < SUB:
+                v0, v1 = s * c0 - q * c1, p * c1 - q * c0
             for k in range(j + 2, SUB):
-                a0, a1 = row_splat(cols[k], j), row_splat(cols[k], j + 1)
-                n0, n1 = s * a0 - q * a1, p * a1 - q * a0
+                n0, n1 = row_splat(v0, k), row_splat(v1, k)
                 cols[k] = cols[k] - (m0 * n0 + m1 * n1) * r
-                for g in near:
-                    side[g][k] = side[g][k] - (side[g][j] * n0 + side[g][j + 1] * n1) * r
-            if b + 1 < groups:
-                s0, s1 = side[b + 1][j], side[b + 1][j + 1]
-                for k in range(SUB):
-                    a0, a1 = row_splat(s0, k), row_splat(s1, k)
-                    n0, n1 = s * a0 - q * a1, p * a1 - q * a0
-                    ahead[k] = ahead[k] - (s0 * n0 + s1 * n1) * r
+                if not last:
+                    side[k] = side[k] - (side[j] * n0 + side[j + 1] * n1) * r
             y0, y1 = row_splat(y, j), row_splat(y, j + 1)
             w0, w1 = (s * y0 - q * y1) * r, (p * y1 - q * y0) * r
-            for g in near:
-                held[g] = held[g] - (side[g][j] * w0 + side[g][j + 1] * w1)
+            if not last:
+                s0, s1 = side[j], side[j + 1]
+                v0, v1 = s * s0 - q * s1, p * s1 - q * s0
+                for k in range(SUB):
+                    ahead[k] = ahead[k] - (s0 * row_splat(v0, k) + s1 * row_splat(v1, k)) * r
+                near = near - (s0 * w0 + s1 * w1)
             y = y - (m0 * w0 + m1 * w1)
             root0 = lax.rsqrt(p)
             ratio = q * root0 * root0
@@ -82,10 +82,12 @@
             done = jnp.where(here[j], y0 * root0, done)
             done = jnp.where(here[j + 1], (y1 - ratio * y0) * root1, done)
         out.append(jnp.where(lane >= sub + b * SUB, done, 0.0))
-        if b + 1 == groups:
+        if last:
             break
+        held[b + 1] = near
         cols = ahead
-        yk = [row_splat(y, k) for k in range(SUB)]
+        if below:
+            yk = [row_splat(y, k) for k in range(SUB)]
         for g, c in below.items():
             held[g] = held[g] - total([c[k] * yk[k] for k in range(SUB)])
     return out
@@ -128,40 +130,33 @@
 
 def pack_kernel(index_ref, source_ref, mine_ref, *refs):
     *send_refs, linear_ref, arrived = refs
+    load = pltpu.make_async_copy(source_ref, linear_ref, arrived)
+    load.start()
     layer = index_ref[0]
     first = (index_ref[1] == 0) & (index_ref[2] == 0)
     height, tile = mine_ref.shape
+    load.wait()
     piece = linear_ref.shape[0] // (len(send_refs) + 1)
-    out_refs = (mine_ref, *send_refs)
 
     @pl.when(first)
     def _():
-        load = pltpu.make_async_copy(source_ref, linear_ref, arrived.at[0])
-        load.start()
-        load.wait()
         at_row = lax.broadcasted_iota(jnp.int32, (tile, tile), 0)
         at_col = lax.broadcasted_iota(jnp.int32, (tile, tile), 1)
         corner = linear_ref[pl.ds(2 * tile + 1, tile, 2), :]
         mixed = jnp.where(at_row >= at_col, linear_ref[pl.ds(0, tile, 2), :], corner)
         below = linear_ref[pl.ds(2 * tile, tile, 2), :]
         diagonal = jnp.sum(jnp.where(at_row == at_col, corner, 0.0), axis=0, keepdims=True)
-        for ref in out_refs:
+        for ref in (mine_ref, *send_refs):
             ref[:tile, :] = mixed
             ref[tile : 2 * tile, :] = below
             ref[2 * tile :, :] = jnp.broadcast_to(diagonal, (height - 2 * tile, tile))
 
     @pl.when(jnp.logical_not(first))
     def _():
-        loads = []
-        for k, ref in enumerate(out_refs):
+        for k, ref in enumerate((mine_ref, *send_refs)):
             start = pl.multiple_of((layer ^ k) * piece, piece)
-            from_ref = source_ref.at[pl.ds(start, piece), :]
-            loads.append(pltpu.make_async_copy(from_ref, ref.at[pl.ds(0, piece), :], arrived.at[k]))
-            loads[-1].start()
-        for ref in out_refs:
+            ref[:piece, :] = linear_ref[pl.ds(start, piece), :]
             ref[piece:, :] = jnp.zeros((height - piece, tile), F32)
-        for load in loads:
-            load.wait()
 
 
 def unpack(pieces, to_ref):
@@ -212,24 +207,26 @@
 
 
 def third_kernel(
-    lead_ref, inverse0_ref, left_ref, lower_ref, inverse_ref, under_ref, rest_ref,
-    corner_ref, below_ref, work,
+    corners_ref, belows_ref, inverse0_ref, left_ref, lower_ref, inverse_ref, cross_ref, corner_ref, below_ref, work,
 ):
-    tile = lower_ref.shape[0]
-    unpack([lead_ref.at[t, 0] for t in range(lead_ref.shape[0])], below_ref)
-    unpack([lead_ref.at[t, 1] for t in range(lead_ref.shape[0])], corner_ref)
-    left_ref[...] = dot(below_ref[...], inverse0_ref[...], NT)
-    top, bottom = left_ref[:tile, :], left_ref[tile:, :]
-    factor(corner_ref[:tile, :tile] - dot(top, top, NT), lower_ref, inverse_ref, work)
-    under = dot(corner_ref[tile:, :tile] - dot(bottom, top, NT), inverse_ref[...], NT)
-    under_ref[...] = under
-    rest_ref[...] = corner_ref[tile:, tile:] - dot(bottom, bottom, NT) - dot(under, under, NT)
-
-
-def fourth_kernel(
-    left_ref, inverse0_ref, lower0_ref, small_ref, under_ref, rest_ref, lower_ref, inverse_ref, cross_ref, work
-):
-    second_kernel(lower0_ref, small_ref, under_ref, rest_ref, lower_ref, inverse_ref, work)
+    tile = work.shape[0]
+    first, second = slice(0, tile), slice(tile, 2 * tile)
+    zero = jnp.zeros((tile, tile), F32)
+    unpack([belows_ref.at[t] for t in range(belows_ref.shape[0])], below_ref)
+    unpack([corners_ref.at[t] for t in range(corners_ref.shape[0])], corner_ref)
+    top = dot(below_ref[first, :], inverse0_ref[...], NT)
+    factor(corner_ref[first, first] - dot(top, top, NT), lower_ref.at[first, first], inverse_ref.at[first, first], work)
+    bottom = dot(below_ref[second, :], inverse0_ref[...], NT)
+    left_ref[first, :] = top
+    left_ref[second, :] = bottom
+    ahead = corner_ref[second, first] - dot(bottom, top, NT)
+    rest = corner_ref[second, second] - dot(bottom, bottom, NT)
+    under = dot(ahead, inverse_ref[first, first], NT)
+    lower_ref[first, second] = zero
+    lower_ref[second, first] = under
+    inverse_ref[first, second] = zero
+    factor(rest - dot(under, under, NT), lower_ref.at[second, second], inverse_ref.at[second, second], work)
+    inverse_ref[second, first] = -dot(inverse_ref[second, second], dot(under, inverse_ref[first, first]))
     cross_ref[...] = -dot(inverse_ref[...], dot(left_ref[...], inverse0_ref[...]))
 
 
@@ -298,20 +295,8 @@
     return lax.ppermute(x, axis, [(i, i ^ k) for i in range(lax.axis_size(axis))])
 
 
-def ask_layers(x, members=None):
-    parts = [x]
-    layers, rows, cols = (lax.axis_size(a) for a in AXES)
-    for k in range(1, layers):
-        if members is None:
-            parts.append(trade(x, "layer", k))
-        else:
-            pairs = [
-                (((i * rows) + r) * cols + c, (((i ^ k) * rows) + r) * cols + c)
-                for i in range(layers)
-                for r, c in members
-            ]
-            parts.append(lax.ppermute(x, AXES, pairs))
-    return parts
+def ask_layers(x):
+    return [x] + [trade(x, "layer", k) for k in range(1, lax.axis_size("layer"))]
 
 
 def in_order(parts, *late):
@@ -373,7 +358,7 @@
         pack_kernel,
         ((height, tile),) * layers,
         (index, pltpu.with_memory_space_constraint(partials.reshape(width * tiles_per, tile), pltpu.HBM)),
-        scratch=((width * tiles_per, tile), pltpu.SemaphoreType.DMA((layers,))),
+        scratch=((width * tiles_per, tile), pltpu.SemaphoreType.DMA),
         name="k0",
         smem=1,
         source=pltpu.HBM,
@@ -393,20 +378,14 @@
     for s in strides(cols, 2):
         lead = jnp.where(col % (2 * s) >= s, trade(lead, "col", s), lead)
     fall_got = after(fall_got, lead)
-    fall = jnp.where(row % 4 >= 2, fall_got, fall_from)
     lead = after(lead, fall_got)
-    fall = after(fall, lead)
-    fall_other = trade(fall, "row", 1)
     got = trade(lead, "col", 1)
     low, high = jnp.where(even_col, lead, got), jnp.where(even_col, got, lead)
     panels_in = jnp.stack([low[:piece_rows], high[:piece_rows]])
     high = high[:piece_rows]
 
-    low = after(low, fall_other)
     high = after(high, low)
-    cols_in = ask_layers(
-        jnp.stack([jnp.where(even_row, fall, fall_other), jnp.where(even_row, fall_other, fall)])
-    )
+
     for s in strides(rows, 2):
         low = jnp.where(row % (2 * s) >= s, trade(low, "row", s), low)
     for s in strides(rows, 2):
@@ -414,9 +393,10 @@
         if s > 2:
             high = jnp.where(row % (2 * s) >= s, high_got, high_from)
     high = jnp.where(row % 4 >= 2, after(high_got, low), high_from)
-    packed = jnp.where(even_row, low, trade(low, "row", 1))
-    lead = jnp.stack([low[:piece_rows], high])
-    lead_parts = ask_layers(lead, [(r, c) for r in range(1, rows, 2) for c in range(cols)])
+    got = trade(low, "row", 1)
+    packed = jnp.where(even_row, low, got)
+    lead_parts = ask_layers(jnp.where(even_row, got[:piece_rows], high))
+    rows_in = ask_layers(after(panels_in, lead_parts[0]))
     packed = after(packed, high)
 
     block0, small_lower, small_inverse, left0, rest0 = run(
@@ -428,9 +408,9 @@
         name="k1",
     )
     lead = in_order(lead_parts, rest0)
-    lead_other = trade(lead, "row", 1)
-    rows_in = ask_layers(after(panels_in, lead))
-
+    fall = jnp.where(row % 4 >= 2, fall_got, fall_from)
+    lead_other = trade(jnp.concatenate([lead, fall[None]], axis=0), "row", 1)
+    lead_other, fall_other = lead_other[:layers], lead_other[layers]
     lower0, inverse0 = run(
         second_kernel,
         (big, big),
@@ -440,22 +420,18 @@
         name="k2",
     )
     lead_other = after(lead_other, inverse0)
-    lead = jnp.where(even_row, lead_other, lead)
-    left1, small_lower, small_inverse, under, rest1 = run(
+    corners, belows = jnp.where(even_row, lead_other, lead), jnp.where(even_row, lead, lead_other)
+    fall_other = after(fall_other, inverse0)
+    cols_in = ask_layers(
+        jnp.stack([jnp.where(even_row, fall, fall_other), jnp.where(even_row, fall_other, fall)])
+    )
+    left1, lower1, inverse1, cross = run(
         third_kernel,
-        (big, square, square, square, square),
-        (lead, inverse0),
+        (big, big, big, big),
+        (corners, belows, inverse0),
         scratch=(big, big, square),
-        flops=5 * 10**9,
+        flops=10**10,
         name="k3",
-    )
-    lower1, inverse1, cross = run(
-        fourth_kernel,
-        (big, big, big),
-        (left1, inverse0, small_lower, small_inverse, under, rest1),
-        scratch=(square,),
-        flops=5 * 10**9,
-        name="k4",
     )
     rows_in, cols_in = in_order(rows_in, cross), in_order(cols_in, cross)
     schur, panels = run(

time: 55 us -> 51.2 us (0.931); the launches traced: 54.6 us -> 50.3 us
  Pallas kernels: 20.3 us -> 17.5 us
  starting transfers between devices: 15.9 us -> 14.3 us
    pallas_call x6 -> x5, Pallas kernels: 20.3 us -> 17.5 us  [run(): pl.pallas_call(kernel, out_shape=tuple((jax.ShapeDtypeStruct(s, F32) for...]
    ppermute x11, starting transfers between devices: 15.2 us -> 14.3 us  [trade(): lax.ppermute(x, axis, [(i, i ^ k) for i in range(lax.axis_size(axis))])]
    ppermute x1 -> x0, starting transfers between devices: 0.68 us -> none  [ask_layers(): parts.append(lax.ppermute(x, AXES, pairs))]
  transfers between devices with their start and end apart: 12 -> 11, of which waited for: 6 -> 6; matrix products, arithmetic and copies ran while one was open for 1% -> 1% of each run, Pallas kernels for 31% -> 28%
where the time goes in v2:
time: 51.2 us; the launch traced here: 50.3 us
  Pallas kernels  17.5 us (34%)
  waiting for transfers between devices  17 us (33%)
  starting transfers between devices  14.3 us (28%)
  between operations  0.83 us (2%)
  other arithmetic  0.54 us (1%)
    pallas_call x5, Pallas kernels, run(): pl.pallas_call(kernel, out_shape=tuple((jax.ShapeDtypeStruct(s, F32) for...  17.5 us
    ppermute x11, waiting for transfers between devices, trade(): lax.ppermute(x, axis, [(i, i ^ k) for i in range(lax.axis_size(axis))])  17 us
    ppermute x11, starting transfers between devices, trade(): lax.ppermute(x, axis, [(i, i ^ k) for i in range(lax.axis_size(axis))])  14.3 us
  transfers between devices with their start and end apart: 11, of which 6 were waited for; matrix products, arithmetic and copies ran while one was open for 1% of the time, Pallas kernels for 28%

profile of v2, /device:TPU:0, one launch (start us, length us, event | category | flops | bytes accessed | tf_op | source)
XLA Modules:
  0.0 50.3 jit_solution(5767683675648078970)
XLA Ops:
  0.6 0.1 pad_add_fusion.index_ref
  0.7 1.5 %k0.1 = (f32[264,128]{1,0:T(8,128)S(1)}, f32[264,128]{1,0:T(8,128)S(1)}) custom-call(s32[3]{0:T(128)S(1)} %pad_add_fusion.index_ref, f32[512,128]{1,0:T(8,128)} %bitcast.34), custom_call_target="tpu_custom_call" | custom-call | bytes 1000000 | tf_op jit(solution)/shard_map/k0/pallas_call | solution.py:332
  2.2 3.0 %collective-permute-start = (f32[264,128]{1,0:T(8,128)S(1)}, f32[264,128]{1,0:T(8,128)S(1)}, u32[]{:S(2)}, u32[]{:S(2)}) collective-permute-start(f32[264,128]{1,0:T(8,128)S(1)} %get-tuple-element.31), channel_id=1, source_target_pairs={{0,16},{16,0},{1,17},{17,1},{2,18},{18,2},{3,19},{19,3},{4,20},{20... | collective-permute-start | bytes 405512 | tf_op jit(solution)/shard_map/ppermute | solution.py:295
  5.3 3.6 %collective-permute-done = f32[264,128]{1,0:T(8,128)S(1)} collective-permute-done((f32[264,128]{1,0:T(8,128)S(1)}, f32[264,128]{1,0:T(8,128)S(1)}, u32[]{:S(2)}, u32[]{:S(2)}) %collective-permute-start) | collective-permute-done | bytes 135200 | tf_op jit(solution)/shard_map/ppermute | solution.py:295
  8.8 0.0 copy-start
  8.8 2.9 %collective-permute-start.1 = (f32[264,128]{1,0:T(8,128)S(1)}, f32[264,128]{1,0:T(8,128)S(1)}, u32[]{:S(2)}, u32[]{:S(2)}) collective-permute-start(f32[264,128]{1,0:T(8,128)S(1)} %add.18), channel_id=1, source_target_pairs={{0,2},{1,3},{2,0},{3,1},{4,6},{5,7},{6,4},{7,5},{8,10},{9,11},{10,... | collective-permute-start | bytes 405512 | tf_op jit(solution)/shard_map/ppermute | solution.py:295
  11.8 0.0 copy-done
  11.8 1.6 %collective-permute-start.2 = (f32[256,128]{1,0:T(8,128)S(1)}, f32[256,128]{1,0:T(8,128)S(1)}, u32[]{:S(2)}, u32[]{:S(2)}) collective-permute-start(f32[256,128]{1,0:T(8,128)S(1)} %slice.25.own_ref), channel_id=1, source_target_pairs={{0,8},{4,12},{8,0},{12,4},{1,9},{5,13},{9,1},{13,5},{2,10},{6,14},... | collective-permute-start | bytes 393224 | tf_op jit(solution)/shard_map/ppermute | solution.py:295
  13.4 4.1 %collective-permute-done.1 = f32[264,128]{1,0:T(8,128)S(1)} collective-permute-done((f32[264,128]{1,0:T(8,128)S(1)}, f32[264,128]{1,0:T(8,128)S(1)}, u32[]{:S(2)}, u32[]{:S(2)}) %collective-permute-start.1) | collective-permute-done | bytes 135200 | tf_op jit(solution)/shard_map/ppermute | solution.py:295
  17.5 0.0 collective-permute-done.2
  17.5 0.9 %collective-permute-start.3 = (f32[264,128]{1,0:T(8,128)S(1)}, f32[264,128]{1,0:T(8,128)S(1)}, u32[]{:S(2)}, u32[]{:S(2)}) collective-permute-start(f32[264,128]{1,0:T(8,128)S(1)} %broadcast_select_fusion.2), channel_id=1, source_target_pairs={{0,1},{1,0},{2,3},{3,2},{4,5},{5,4},{6,7},{7,6},{8,9},{9,8},{10,11... | collective-permute-start | bytes 405512 | tf_op jit(solution)/shard_map/ppermute | solution.py:295
  18.4 4.2 %collective-permute-done.3 = f32[264,128]{1,0:T(8,128)S(1)} collective-permute-done((f32[264,128]{1,0:T(8,128)S(1)}, f32[264,128]{1,0:T(8,128)S(1)}, u32[]{:S(2)}, u32[]{:S(2)}) %collective-permute-start.3) | collective-permute-done | bytes 135200 | tf_op jit(solution)/shard_map/ppermute | solution.py:295
  22.6 1.5 %collective-permute-start.4 = (f32[264,128]{1,0:T(8,128)S(1)}, f32[264,128]{1,0:T(8,128)S(1)}, u32[]{:S(2)}, u32[]{:S(2)}) collective-permute-start(f32[264,128]{1,0:T(8,128)S(1)} %broadcast_select_fusion.3), channel_id=1, source_target_pairs={{0,8},{4,12},{8,0},{12,4},{1,9},{5,13},{9,1},{13,5},{2,10},{6,14},... | collective-permute-start | bytes 405512 | tf_op jit(solution)/shard_map/ppermute | solution.py:295
  24.1 0.6 %collective-permute-start.6 = (f32[256,128]{1,0:T(8,128)S(1)}, f32[256,128]{1,0:T(8,128)S(1)}, u32[]{:S(2)}, u32[]{:S(2)}) collective-permute-start(f32[256,128]{1,0:T(8,128)S(1)} %slice_select_fusion.1), channel_id=1, source_target_pairs={{0,8},{4,12},{8,0},{12,4},{1,9},{5,13},{9,1},{13,5},{2,10},{6,14},... | collective-permute-start | bytes 393224 | tf_op jit(solution)/shard_map/ppermute | solution.py:295
  24.8 2.9 %collective-permute-done.4 = f32[264,128]{1,0:T(8,128)S(1)} collective-permute-done((f32[264,128]{1,0:T(8,128)S(1)}, f32[264,128]{1,0:T(8,128)S(1)}, u32[]{:S(2)}, u32[]{:S(2)}) %collective-permute-start.4) | collective-permute-done | bytes 135200 | tf_op jit(solution)/shard_map/ppermute | solution.py:295
  27.7 0.1 collective-permute-start.5
  27.8 1.4 %collective-permute-done.6 = f32[256,128]{1,0:T(8,128)S(1)} collective-permute-done((f32[256,128]{1,0:T(8,128)S(1)}, f32[256,128]{1,0:T(8,128)S(1)}, u32[]{:S(2)}, u32[]{:S(2)}) %collective-permute-start.6) | collective-permute-done | bytes 131104 | tf_op jit(solution)/shard_map/ppermute | solution.py:295
  29.2 0.0 collective-permute-done.5
  29.2 1.6 %collective-permute-start.8 = (f32[256,128]{1,0:T(8,128)S(1)}, f32[256,128]{1,0:T(8,128)S(1)}, u32[]{:S(2)}, u32[]{:S(2)}) collective-permute-start(f32[256,128]{1,0:T(8,128)S(1)} %slice_select_fusion), channel_id=1, source_target_pairs={{0,16},{16,0},{1,17},{17,1},{2,18},{18,2},{3,19},{19,3},{4,20},{20... | collective-permute-start | bytes 393224 | tf_op jit(solution)/shard_map/ppermute | solution.py:295
  30.8 0.5 %collective-permute-start.7 = (f32[2,256,128]{2,1,0:T(8,128)S(1)}, f32[2,256,128]{2,1,0:T(8,128)S(1)}, u32[]{:S(2)}, u32[]{:S(2)}) collective-permute-start(f32[2,256,128]{2,1,0:T(8,128)S(1)} %pad_maximum_fusion.3), channel_id=1, source_target_pairs={{0,16},{16,0},{1,17},{17,1},{2,18},{18,2},{3,19},{19,3},{4,20},{20... | collective-permute-start | bytes 786440 | tf_op jit(solution)/shard_map/ppermute | solution.py:295
  31.3 3.4 %k1.1 = (f32[256,256]{1,0:T(8,128)S(1)}, f32[128,128]{1,0:T(8,128)S(1)}, f32[128,128]{1,0:T(8,128)S(1)}, f32[128,128]{1,0:T(8,128)S(1)}, f32[128,128]{1,0:T(8,128)S(1)}) custom-call(f32[264,128]{1,0:T(8,128)S(1)} %broadcast_select_fusion.5.packed_ref), custom_call_target="tpu_custom_call" | custom-call | flops 5000000000 | bytes 1000000 | tf_op jit(solution)/shard_map/k1/pallas_call | solution.py:332
  34.7 0.9 %collective-permute-done.8 = f32[256,128]{1,0:T(8,128)S(1)} collective-permute-done((f32[256,128]{1,0:T(8,128)S(1)}, f32[256,128]{1,0:T(8,128)S(1)}, u32[]{:S(2)}, u32[]{:S(2)}) %collective-permute-start.8) | collective-permute-done | bytes 131104 | tf_op jit(solution)/shard_map/ppermute | solution.py:295
  35.7 0.1 collective-permute-start.9
  35.8 2.9 %k2.1 = (f32[256,256]{1,0:T(8,128)S(1)}, f32[256,256]{1,0:T(8,128)S(1)}) custom-call(f32[128,128]{1,0:T(8,128)S(1)} %get-tuple-element.42.lower0_ref, f32[128,128]{1,0:T(8,128)S(1)} %get-tuple-element.43.inverse0_ref, f32[128,128]{1,0:T(8,128)S(1)} %get-tuple-element.44.left_ref, f32[128,128]{1,0:T(8,128)S(1)} %get-tuple-element.45.rest_ref), custom_call_target="tpu_custom_call" | custom-call | flops 5000000000 | bytes 1000000 | tf_op jit(solution)/shard_map/k2/pallas_call | solution.py:332
  38.7 0.0 collective-permute-done.9
  38.9 1.6 %collective-permute-start.10 = (f32[2,256,128]{2,1,0:T(8,128)S(1)}, f32[2,256,128]{2,1,0:T(8,128)S(1)}, u32[]{:S(2)}, u32[]{:S(2)}) collective-permute-start(f32[2,256,128]{2,1,0:T(8,128)S(1)} %pad_maximum_fusion.5), channel_id=1, source_target_pairs={{0,16},{16,0},{1,17},{17,1},{2,18},{18,2},{3,19},{19,3},{4,20},{20... | collective-permute-start | bytes 786440 | tf_op jit(solution)/shard_map/ppermute | solution.py:295
  40.5 7.8 %k3.1 = (f32[256,256]{1,0:T(8,128)S(1)}, f32[256,256]{1,0:T(8,128)S(1)}, f32[256,256]{1,0:T(8,128)S(1)}, f32[256,256]{1,0:T(8,128)S(1)}) custom-call(f32[2,256,128]{2,1,0:T(8,128)S(1)} %get-tuple-element.67.corners_ref, f32[2,256,128]{2,1,0:T(8,128)S(1)} %get-tuple-element.66.belows_ref, f32[256,256]{1,0:T(8,128)S(1)} %get-tuple-element.46.inverse0_ref), custom_call_target="tpu_custom_call" | custom-call | flops 10000000000 | bytes 1000000 | tf_op jit(solution)/shard_map/k3/pallas_call | solution.py:332
  48.3 0.0 collective-permute-done.7
  48.3 0.0 collective-permute-done.10
  48.3 0.1 select_bitcast_fusion.1
  48.5 1.8 %kf.1 = (f32[256,128]{1,0:T(8,128)}, f32[2,256,256]{2,1,0:T(8,128)}) custom-call(s32[3]{0:T(128)S(1)} %pad_add_fusion.index_ref, s32[2,2]{1,0:T(2,128)S(1)} %bitcast.31, f32[256,128]{1,0:T(8,128)S(1)} %slice.25.own_ref, f32[256,256]{1,0:T(8,128)S(1)} %get-tuple-element.38.block_ref, f32[2,2,256,128]{3,2,1,0:T(8,128)S(1)} %pad_maximum_fusion.rows_ref, ...), custom_call_target="tpu_custom_call" | custom-call | flops 1000000000 | bytes 1000000 | tf_op jit(solution)/shard_map/kf/pallas_call | solution.py:332
  (21 shorter events, 0.4 us)
Async XLA Ops:
  2.2 6.6 %collective-permute-start = (f32[264,128]{1,0:T(8,128)S(1)}, f32[264,128]{1,0:T(8,128)S(1)}, u32[]{:S(2)}, u32[]{:S(2)}) collective-permute-start(f32[264,128]{1,0:T(8,128)S(1)} %get-tuple-element.31), channel_id=1, source_target_pairs={{0,16},{16,0},{1,17},{17,1},{2,18},{18,2},{3,19},{19,3},{4,20},{20... | collective-permute-start | bytes 405512 | tf_op jit(solution)/shard_map/ppermute | solution.py:295
  8.8 2.9 %copy-start = (s32[1,1,2,1,1,2]{5,4,3,2,1,0:T(1,128)S(1)}, s32[1,1,2,1,1,2]{5,4,3,2,1,0:T(1,128)}, u32[]{:S(2)}) copy-start(s32[1,1,2,1,1,2]{5,4,3,2,1,0:T(1,128)} %param.3) | copy-start | bytes 52
  8.8 8.6 %collective-permute-start.1 = (f32[264,128]{1,0:T(8,128)S(1)}, f32[264,128]{1,0:T(8,128)S(1)}, u32[]{:S(2)}, u32[]{:S(2)}) collective-permute-start(f32[264,128]{1,0:T(8,128)S(1)} %add.18), channel_id=1, source_target_pairs={{0,2},{1,3},{2,0},{3,1},{4,6},{5,7},{6,4},{7,5},{8,10},{9,11},{10,... | collective-permute-start | bytes 405512 | tf_op jit(solution)/shard_map/ppermute | solution.py:295
  11.8 5.7 %collective-permute-start.2 = (f32[256,128]{1,0:T(8,128)S(1)}, f32[256,128]{1,0:T(8,128)S(1)}, u32[]{:S(2)}, u32[]{:S(2)}) collective-permute-start(f32[256,128]{1,0:T(8,128)S(1)} %slice.25.own_ref), channel_id=1, source_target_pairs={{0,8},{4,12},{8,0},{12,4},{1,9},{5,13},{9,1},{13,5},{2,10},{6,14},... | collective-permute-start | bytes 393224 | tf_op jit(solution)/shard_map/ppermute | solution.py:295
  17.5 5.1 %collective-permute-start.3 = (f32[264,128]{1,0:T(8,128)S(1)}, f32[264,128]{1,0:T(8,128)S(1)}, u32[]{:S(2)}, u32[]{:S(2)}) collective-permute-start(f32[264,128]{1,0:T(8,128)S(1)} %broadcast_select_fusion.2), channel_id=1, source_target_pairs={{0,1},{1,0},{2,3},{3,2},{4,5},{5,4},{6,7},{7,6},{8,9},{9,8},{10,11... | collective-permute-start | bytes 405512 | tf_op jit(solution)/shard_map/ppermute | solution.py:295
  22.6 5.1 %collective-permute-start.4 = (f32[264,128]{1,0:T(8,128)S(1)}, f32[264,128]{1,0:T(8,128)S(1)}, u32[]{:S(2)}, u32[]{:S(2)}) collective-permute-start(f32[264,128]{1,0:T(8,128)S(1)} %broadcast_select_fusion.3), channel_id=1, source_target_pairs={{0,8},{4,12},{8,0},{12,4},{1,9},{5,13},{9,1},{13,5},{2,10},{6,14},... | collective-permute-start | bytes 405512 | tf_op jit(solution)/shard_map/ppermute | solution.py:295
  24.1 5.0 %collective-permute-start.6 = (f32[256,128]{1,0:T(8,128)S(1)}, f32[256,128]{1,0:T(8,128)S(1)}, u32[]{:S(2)}, u32[]{:S(2)}) collective-permute-start(f32[256,128]{1,0:T(8,128)S(1)} %slice_select_fusion.1), channel_id=1, source_target_pairs={{0,8},{4,12},{8,0},{12,4},{1,9},{5,13},{9,1},{13,5},{2,10},{6,14},... | collective-permute-start | bytes 393224 | tf_op jit(solution)/shard_map/ppermute | solution.py:295
  27.7 1.5 %collective-permute-start.5 = (f32[264,128]{1,0:T(8,128)S(1)}, f32[264,128]{1,0:T(8,128)S(1)}, u32[]{:S(2)}, u32[]{:S(2)}) collective-permute-start(f32[264,128]{1,0:T(8,128)S(1)} %broadcast_select_fusion.4), channel_id=1, source_target_pairs={{0,4},{4,0},{8,12},{12,8},{1,5},{5,1},{9,13},{13,9},{2,6},{6,2},{1... | collective-permute-start | bytes 405512 | tf_op jit(solution)/shard_map/ppermute | solution.py:295
  29.2 6.4 %collective-permute-start.8 = (f32[256,128]{1,0:T(8,128)S(1)}, f32[256,128]{1,0:T(8,128)S(1)}, u32[]{:S(2)}, u32[]{:S(2)}) collective-permute-start(f32[256,128]{1,0:T(8,128)S(1)} %slice_select_fusion), channel_id=1, source_target_pairs={{0,16},{16,0},{1,17},{17,1},{2,18},{18,2},{3,19},{19,3},{4,20},{20... | collective-permute-start | bytes 393224 | tf_op jit(solution)/shard_map/ppermute | solution.py:295
  30.8 17.5 %collective-permute-start.7 = (f32[2,256,128]{2,1,0:T(8,128)S(1)}, f32[2,256,128]{2,1,0:T(8,128)S(1)}, u32[]{:S(2)}, u32[]{:S(2)}) collective-permute-start(f32[2,256,128]{2,1,0:T(8,128)S(1)} %pad_maximum_fusion.3), channel_id=1, source_target_pairs={{0,16},{16,0},{1,17},{17,1},{2,18},{18,2},{3,19},{19,3},{4,20},{20... | collective-permute-start | bytes 786440 | tf_op jit(solution)/shard_map/ppermute | solution.py:295
  35.7 3.0 %collective-permute-start.9 = (f32[3,256,128]{2,1,0:T(8,128)S(1)}, f32[3,256,128]{2,1,0:T(8,128)S(1)}, u32[]{:S(2)}, u32[]{:S(2)}) collective-permute-start(f32[3,256,128]{2,1,0:T(8,128)S(1)} %pad_maximum_fusion.2), channel_id=1, source_target_pairs={{0,4},{4,0},{8,12},{12,8},{1,5},{5,1},{9,13},{13,9},{2,6},{6,2},{1... | collective-permute-start | bytes 1179656 | tf_op jit(solution)/shard_map/ppermute | solution.py:295
  38.9 9.4 %collective-permute-start.10 = (f32[2,256,128]{2,1,0:T(8,128)S(1)}, f32[2,256,128]{2,1,0:T(8,128)S(1)}, u32[]{:S(2)}, u32[]{:S(2)}) collective-permute-start(f32[2,256,128]{2,1,0:T(8,128)S(1)} %pad_maximum_fusion.5), channel_id=1, source_target_pairs={{0,16},{16,0},{1,17},{17,1},{2,18},{18,2},{3,19},{19,3},{4,20},{20... | collective-permute-start | bytes 786440 | tf_op jit(solution)/shard_map/ppermute | solution.py:295

commit v3 on v2

--- a/solution.py
+++ b/solution.py
@@ -17,6 +17,16 @@
     return lax.dot_general(
         a, b, dims, precision=lax.Precision.HIGHEST, preferred_element_type=F32
     )
+
+
+def split(x):
+    high = x.astype(jnp.bfloat16)
+    return high, (x - high.astype(F32)).astype(jnp.bfloat16)
+
+
+def dot_split(a, b, dims=NN):
+    part = lambda x, y: lax.dot_general(x, y, dims, preferred_element_type=F32)
+    return part(a[0], b[0]) + (part(a[0], b[1]) + part(a[1], b[0]))
 
 
 def lane_splat(x, lane):
@@ -231,7 +241,7 @@
 
 
 def final_kernel(
-    index_ref, keep_ref, own_ref, block_ref, rows_ref, cols_ref,
+    index_ref, keep_ref, own_ref, block_ref, rows_ref, col0_ref, col1_ref,
     lower0_ref, inverse0_ref, lower1_ref, inverse1_ref, left_ref, cross_ref,
     schur_ref, panels_ref, upper_ref, row_ref,
 ):
@@ -256,8 +266,9 @@
     def _():
         for k in range(2):
             unpack([rows_ref.at[t, k] for t in range(slabs)], row_ref.at[k])
-        panels_ref[0] = dot(row_ref[0], inverse0_ref[...], NT)
-        panels_ref[1] = dot(row_ref[0], cross_ref[...], NT) + dot(row_ref[1], inverse1_ref[...], NT)
+        f0, f1 = split(row_ref[0]), split(row_ref[1])
+        panels_ref[0] = dot_split(f0, split(inverse0_ref[...]), NT)
+        panels_ref[1] = dot_split(f0, split(cross_ref[...]), NT) + dot_split(f1, split(inverse1_ref[...]), NT)
 
     @pl.when(col == 0)
     def _():
@@ -270,13 +281,15 @@
 
     @pl.when(col > 1)
     def _():
-        for k in range(2):
-            unpack([cols_ref.at[t, k] for t in range(slabs)], row_ref.at[k])
-        upper_ref[:width, :] = dot(inverse0_ref[...], row_ref[0])
-        upper_ref[width:, :] = dot(cross_ref[...], row_ref[0]) + dot(inverse1_ref[...], row_ref[1])
+        for k, ref in enumerate((col0_ref, col1_ref)):
+            unpack([ref.at[t] for t in range(slabs)], row_ref.at[k])
+        g0, g1 = split(row_ref[0]), split(row_ref[1])
+        upper_ref[:width, :] = dot_split(split(inverse0_ref[...]), g0)
+        upper_ref[width:, :] = dot_split(split(cross_ref[...]), g0) + dot_split(split(inverse1_ref[...]), g1)
 
     slab = pl.ds(pl.multiple_of(layer * slab_rows, slab_rows), slab_rows)
-    product = dot(panels_ref[0, slab, :], upper_ref[:width, :]) + dot(panels_ref[1, slab, :], upper_ref[width:, :])
+    product = dot_split(split(panels_ref[0, slab, :]), split(upper_ref[:width, :]))
+    product += dot_split(split(panels_ref[1, slab, :]), split(upper_ref[width:, :]))
     at_row = (lax.broadcasted_iota(jnp.int32, (slab_rows, tile), 0) + layer * slab_rows) // tile
     for j in range(tiles_per):
         keep = jnp.zeros((slab_rows, tile), jnp.int32)
@@ -396,6 +409,8 @@
     got = trade(low, "row", 1)
     packed = jnp.where(even_row, low, got)
     lead_parts = ask_layers(jnp.where(even_row, got[:piece_rows], high))
+    fall = jnp.where(row % 4 >= 2, fall_got, fall_from)
+    fall_parts = ask_layers(after(fall, lead_parts[0]))
     rows_in = ask_layers(after(panels_in, lead_parts[0]))
     packed = after(packed, high)
 
@@ -408,9 +423,7 @@
         name="k1",
     )
     lead = in_order(lead_parts, rest0)
-    fall = jnp.where(row % 4 >= 2, fall_got, fall_from)
-    lead_other = trade(jnp.concatenate([lead, fall[None]], axis=0), "row", 1)
-    lead_other, fall_other = lead_other[:layers], lead_other[layers]
+    lead_other = trade(lead, "row", 1)
     lower0, inverse0 = run(
         second_kernel,
         (big, big),
@@ -421,10 +434,8 @@
     )
     lead_other = after(lead_other, inverse0)
     corners, belows = jnp.where(even_row, lead_other, lead), jnp.where(even_row, lead, lead_other)
-    fall_other = after(fall_other, inverse0)
-    cols_in = ask_layers(
-        jnp.stack([jnp.where(even_row, fall, fall_other), jnp.where(even_row, fall_other, fall)])
-    )
+    fall = in_order(fall_parts, inverse0)
+    fall_other = trade(fall, "row", 1)
     left1, lower1, inverse1, cross = run(
         third_kernel,
         (big, big, big, big),
@@ -433,11 +444,12 @@
         flops=10**10,
         name="k3",
     )
-    rows_in, cols_in = in_order(rows_in, cross), in_order(cols_in, cross)
+    rows_in, fall_other = in_order(rows_in, cross), after(fall_other, cross)
+    col0, col1 = jnp.where(even_row, fall, fall_other), jnp.where(even_row, fall_other, fall)
     schur, panels = run(
         final_kernel,
         ((piece_rows, tile), (2, width, width)),
-        (index, keep, piece, block0, rows_in, cols_in, lower0, inverse0, lower1, inverse1, left1, cross),
+        (index, keep, piece, block0, rows_in, col0, col1, lower0, inverse0, lower1, inverse1, left1, cross),
         scratch=((2 * width, width), (2, width, width)),
         flops=10**9,
         name="kf",

time: 51.2 us -> 49.8 us (0.973); the launches traced: 50.3 us -> 49.6 us
  waiting for transfers between devices: 17 us -> 16.1 us
    ppermute x11 -> x12, waiting for transfers between devices: 17 us -> 16.1 us  [trade(): lax.ppermute(x, axis, [(i, i ^ k) for i in range(lax.axis_size(axis))])]
    ppermute x11 -> x12, starting transfers between devices: 14.3 us -> 14.8 us  [trade(): lax.ppermute(x, axis, [(i, i ^ k) for i in range(lax.axis_size(axis))])]
  transfers between devices with their start and end apart: 11 -> 12, of which waited for: 6 -> 5; matrix products, arithmetic and copies ran while one was open for 1% -> 1% of each run, Pallas kernels for 28% -> 29%
where the time goes in v3:
time: 49.8 us; the launch traced here: 49.6 us
  Pallas kernels  17.3 us (35%)
  waiting for transfers between devices  16.1 us (32%)
  starting transfers between devices  14.8 us (30%)
  between operations  0.83 us (2%)
    pallas_call x5, Pallas kernels, run(): pl.pallas_call(kernel, out_shape=tuple((jax.ShapeDtypeStruct(s, F32) for...  17.3 us
    ppermute x12, waiting for transfers between devices, trade(): lax.ppermute(x, axis, [(i, i ^ k) for i in range(lax.axis_size(axis))])  16.1 us
    ppermute x12, starting transfers between devices, trade(): lax.ppermute(x, axis, [(i, i ^ k) for i in range(lax.axis_size(axis))])  14.8 us
  transfers between devices with their start and end apart: 12, of which 5 were waited for; matrix products, arithmetic and copies ran while one was open for 1% of the time, Pallas kernels for 29%

profile of v3, /device:TPU:0, one launch (start us, length us, event | category | flops | bytes accessed | tf_op | source)
XLA Modules:
  0.0 49.6 jit_solution(4129152524039276799)
XLA Ops:
  0.6 0.1 pad_add_fusion.index_ref
  0.7 1.5 %k0.1 = (f32[264,128]{1,0:T(8,128)S(1)}, f32[264,128]{1,0:T(8,128)S(1)}) custom-call(s32[3]{0:T(128)S(1)} %pad_add_fusion.index_ref, f32[512,128]{1,0:T(8,128)} %bitcast.26), custom_call_target="tpu_custom_call" | custom-call | bytes 1000000 | tf_op jit(solution)/shard_map/k0/pallas_call | solution.py:345
  2.2 3.0 %collective-permute-start = (f32[264,128]{1,0:T(8,128)S(1)}, f32[264,128]{1,0:T(8,128)S(1)}, u32[]{:S(2)}, u32[]{:S(2)}) collective-permute-start(f32[264,128]{1,0:T(8,128)S(1)} %get-tuple-element.32), channel_id=1, source_target_pairs={{0,16},{16,0},{1,17},{17,1},{2,18},{18,2},{3,19},{19,3},{4,20},{20... | collective-permute-start | bytes 405512 | tf_op jit(solution)/shard_map/ppermute | solution.py:308
  5.3 3.6 %collective-permute-done = f32[264,128]{1,0:T(8,128)S(1)} collective-permute-done((f32[264,128]{1,0:T(8,128)S(1)}, f32[264,128]{1,0:T(8,128)S(1)}, u32[]{:S(2)}, u32[]{:S(2)}) %collective-permute-start) | collective-permute-done | bytes 135200 | tf_op jit(solution)/shard_map/ppermute | solution.py:308
  8.8 0.0 copy-start
  8.8 2.9 %collective-permute-start.1 = (f32[264,128]{1,0:T(8,128)S(1)}, f32[264,128]{1,0:T(8,128)S(1)}, u32[]{:S(2)}, u32[]{:S(2)}) collective-permute-start(f32[264,128]{1,0:T(8,128)S(1)} %add.18), channel_id=1, source_target_pairs={{0,2},{1,3},{2,0},{3,1},{4,6},{5,7},{6,4},{7,5},{8,10},{9,11},{10,... | collective-permute-start | bytes 405512 | tf_op jit(solution)/shard_map/ppermute | solution.py:308
  11.8 0.0 copy-done
  11.8 1.6 %collective-permute-start.2 = (f32[256,128]{1,0:T(8,128)S(1)}, f32[256,128]{1,0:T(8,128)S(1)}, u32[]{:S(2)}, u32[]{:S(2)}) collective-permute-start(f32[256,128]{1,0:T(8,128)S(1)} %slice.17.own_ref), channel_id=1, source_target_pairs={{0,8},{4,12},{8,0},{12,4},{1,9},{5,13},{9,1},{13,5},{2,10},{6,14},... | collective-permute-start | bytes 393224 | tf_op jit(solution)/shard_map/ppermute | solution.py:308
  13.4 4.1 %collective-permute-done.1 = f32[264,128]{1,0:T(8,128)S(1)} collective-permute-done((f32[264,128]{1,0:T(8,128)S(1)}, f32[264,128]{1,0:T(8,128)S(1)}, u32[]{:S(2)}, u32[]{:S(2)}) %collective-permute-start.1) | collective-permute-done | bytes 135200 | tf_op jit(solution)/shard_map/ppermute | solution.py:308
  17.5 0.0 collective-permute-done.2
  17.5 0.9 %collective-permute-start.3 = (f32[264,128]{1,0:T(8,128)S(1)}, f32[264,128]{1,0:T(8,128)S(1)}, u32[]{:S(2)}, u32[]{:S(2)}) collective-permute-start(f32[264,128]{1,0:T(8,128)S(1)} %broadcast_select_fusion.4), channel_id=1, source_target_pairs={{0,1},{1,0},{2,3},{3,2},{4,5},{5,4},{6,7},{7,6},{8,9},{9,8},{10,11... | collective-permute-start | bytes 405512 | tf_op jit(solution)/shard_map/ppermute | solution.py:308
  18.4 4.2 %collective-permute-done.3 = f32[264,128]{1,0:T(8,128)S(1)} collective-permute-done((f32[264,128]{1,0:T(8,128)S(1)}, f32[264,128]{1,0:T(8,128)S(1)}, u32[]{:S(2)}, u32[]{:S(2)}) %collective-permute-start.3) | collective-permute-done | bytes 135200 | tf_op jit(solution)/shard_map/ppermute | solution.py:308
  22.6 1.5 %collective-permute-start.4 = (f32[264,128]{1,0:T(8,128)S(1)}, f32[264,128]{1,0:T(8,128)S(1)}, u32[]{:S(2)}, u32[]{:S(2)}) collective-permute-start(f32[264,128]{1,0:T(8,128)S(1)} %broadcast_select_fusion.5), channel_id=1, source_target_pairs={{0,8},{4,12},{8,0},{12,4},{1,9},{5,13},{9,1},{13,5},{2,10},{6,14},... | collective-permute-start | bytes 405512 | tf_op jit(solution)/shard_map/ppermute | solution.py:308
  24.1 0.6 %collective-permute-start.6 = (f32[256,128]{1,0:T(8,128)S(1)}, f32[256,128]{1,0:T(8,128)S(1)}, u32[]{:S(2)}, u32[]{:S(2)}) collective-permute-start(f32[256,128]{1,0:T(8,128)S(1)} %slice_select_fusion.1), channel_id=1, source_target_pairs={{0,8},{4,12},{8,0},{12,4},{1,9},{5,13},{9,1},{13,5},{2,10},{6,14},... | collective-permute-start | bytes 393224 | tf_op jit(solution)/shard_map/ppermute | solution.py:308
  24.8 2.9 %collective-permute-done.4 = f32[264,128]{1,0:T(8,128)S(1)} collective-permute-done((f32[264,128]{1,0:T(8,128)S(1)}, f32[264,128]{1,0:T(8,128)S(1)}, u32[]{:S(2)}, u32[]{:S(2)}) %collective-permute-start.4) | collective-permute-done | bytes 135200 | tf_op jit(solution)/shard_map/ppermute | solution.py:308
  27.7 0.1 collective-permute-start.5
  27.8 1.4 %collective-permute-done.6 = f32[256,128]{1,0:T(8,128)S(1)} collective-permute-done((f32[256,128]{1,0:T(8,128)S(1)}, f32[256,128]{1,0:T(8,128)S(1)}, u32[]{:S(2)}, u32[]{:S(2)}) %collective-permute-start.6) | collective-permute-done | bytes 131104 | tf_op jit(solution)/shard_map/ppermute | solution.py:308
  29.2 0.0 collective-permute-done.5
  29.2 1.6 %collective-permute-start.8 = (f32[256,128]{1,0:T(8,128)S(1)}, f32[256,128]{1,0:T(8,128)S(1)}, u32[]{:S(2)}, u32[]{:S(2)}) collective-permute-start(f32[256,128]{1,0:T(8,128)S(1)} %slice_select_fusion), channel_id=1, source_target_pairs={{0,16},{16,0},{1,17},{17,1},{2,18},{18,2},{3,19},{19,3},{4,20},{20... | collective-permute-start | bytes 393224 | tf_op jit(solution)/shard_map/ppermute | solution.py:308
  30.8 0.5 %collective-permute-start.10 = (f32[256,128]{1,0:T(8,128)S(1)}, f32[256,128]{1,0:T(8,128)S(1)}, u32[]{:S(2)}, u32[]{:S(2)}) collective-permute-start(f32[256,128]{1,0:T(8,128)S(1)} %broadcast_select_fusion.8), channel_id=1, source_target_pairs={{0,16},{16,0},{1,17},{17,1},{2,18},{18,2},{3,19},{19,3},{4,20},{20... | collective-permute-start | bytes 393224 | tf_op jit(solution)/shard_map/ppermute | solution.py:308
  31.3 1.5 %collective-permute-start.7 = (f32[2,256,128]{2,1,0:T(8,128)S(1)}, f32[2,256,128]{2,1,0:T(8,128)S(1)}, u32[]{:S(2)}, u32[]{:S(2)}) collective-permute-start(f32[2,256,128]{2,1,0:T(8,128)S(1)} %pad_maximum_fusion.1), channel_id=1, source_target_pairs={{0,16},{16,0},{1,17},{17,1},{2,18},{18,2},{3,19},{19,3},{4,20},{20... | collective-permute-start | bytes 786440 | tf_op jit(solution)/shard_map/ppermute | solution.py:308
  32.8 3.4 %k1.1 = (f32[256,256]{1,0:T(8,128)S(1)}, f32[128,128]{1,0:T(8,128)S(1)}, f32[128,128]{1,0:T(8,128)S(1)}, f32[128,128]{1,0:T(8,128)S(1)}, f32[128,128]{1,0:T(8,128)S(1)}) custom-call(f32[264,128]{1,0:T(8,128)S(1)} %broadcast_select_fusion.7.packed_ref), custom_call_target="tpu_custom_call" | custom-call | flops 5000000000 | bytes 1000000 | tf_op jit(solution)/shard_map/k1/pallas_call | solution.py:345
  36.2 0.0 collective-permute-done.8
  36.3 0.1 collective-permute-start.9
  36.4 2.9 %k2.1 = (f32[256,256]{1,0:T(8,128)S(1)}, f32[256,256]{1,0:T(8,128)S(1)}) custom-call(f32[128,128]{1,0:T(8,128)S(1)} %get-tuple-element.43.lower0_ref, f32[128,128]{1,0:T(8,128)S(1)} %get-tuple-element.44.inverse0_ref, f32[128,128]{1,0:T(8,128)S(1)} %get-tuple-element.45.left_ref, f32[128,128]{1,0:T(8,128)S(1)} %get-tuple-element.46.rest_ref), custom_call_target="tpu_custom_call" | custom-call | flops 5000000000 | bytes 1000000 | tf_op jit(solution)/shard_map/k2/pallas_call | solution.py:345
  39.3 0.0 collective-permute-done.10
  39.4 0.6 %collective-permute-start.11 = (f32[2,256,128]{2,1,0:T(8,128)S(1)}, f32[2,256,128]{2,1,0:T(8,128)S(1)}, u32[]{:S(2)}, u32[]{:S(2)}) collective-permute-start(f32[2,256,128]{2,1,0:T(8,128)S(1)} %pad_maximum_fusion.3), channel_id=1, source_target_pairs={{0,4},{4,0},{8,12},{12,8},{1,5},{5,1},{9,13},{13,9},{2,6},{6,2},{1... | collective-permute-start | bytes 786440 | tf_op jit(solution)/shard_map/ppermute | solution.py:308
  40.0 0.0 collective-permute-done.9
  40.0 7.8 %k3.1 = (f32[256,256]{1,0:T(8,128)S(1)}, f32[256,256]{1,0:T(8,128)S(1)}, f32[256,256]{1,0:T(8,128)S(1)}, f32[256,256]{1,0:T(8,128)S(1)}) custom-call(f32[2,256,128]{2,1,0:T(8,128)S(1)} %get-tuple-element.69.corners_ref, f32[2,256,128]{2,1,0:T(8,128)S(1)} %get-tuple-element.68.belows_ref, f32[256,256]{1,0:T(8,128)S(1)} %get-tuple-element.47.inverse0_ref), custom_call_target="tpu_custom_call" | custom-call | flops 10000000000 | bytes 1000000 | tf_op jit(solution)/shard_map/k3/pallas_call | solution.py:345
  47.9 0.0 collective-permute-done.11
  47.9 0.0 collective-permute-done.7
  48.0 1.6 %kf.1 = (f32[256,128]{1,0:T(8,128)}, f32[2,256,256]{2,1,0:T(8,128)}) custom-call(s32[3]{0:T(128)S(1)} %pad_add_fusion.index_ref, s32[2,2]{1,0:T(2,128)S(1)} %bitcast.24, f32[256,128]{1,0:T(8,128)S(1)} %slice.17.own_ref, f32[256,256]{1,0:T(8,128)S(1)} %get-tuple-element.39.block_ref, f32[2,2,256,128]{3,2,1,0:T(8,128)S(1)} %pad_maximum_fusion.rows_ref, ...), custom_call_target="tpu_custom_call" | custom-call | flops 1000000000 | bytes 1000000 | tf_op jit(solution)/shard_map/kf/pallas_call | solution.py:345
  (20 shorter events, 0.4 us)
Async XLA Ops:
  2.2 6.6 %collective-permute-start = (f32[264,128]{1,0:T(8,128)S(1)}, f32[264,128]{1,0:T(8,128)S(1)}, u32[]{:S(2)}, u32[]{:S(2)}) collective-permute-start(f32[264,128]{1,0:T(8,128)S(1)} %get-tuple-element.32), channel_id=1, source_target_pairs={{0,16},{16,0},{1,17},{17,1},{2,18},{18,2},{3,19},{19,3},{4,20},{20... | collective-permute-start | bytes 405512 | tf_op jit(solution)/shard_map/ppermute | solution.py:308
  8.8 2.9 %copy-start = (s32[1,1,2,1,1,2]{5,4,3,2,1,0:T(1,128)S(1)}, s32[1,1,2,1,1,2]{5,4,3,2,1,0:T(1,128)}, u32[]{:S(2)}) copy-start(s32[1,1,2,1,1,2]{5,4,3,2,1,0:T(1,128)} %param.3) | copy-start | bytes 52
  8.8 8.6 %collective-permute-start.1 = (f32[264,128]{1,0:T(8,128)S(1)}, f32[264,128]{1,0:T(8,128)S(1)}, u32[]{:S(2)}, u32[]{:S(2)}) collective-permute-start(f32[264,128]{1,0:T(8,128)S(1)} %add.18), channel_id=1, source_target_pairs={{0,2},{1,3},{2,0},{3,1},{4,6},{5,7},{6,4},{7,5},{8,10},{9,11},{10,... | collective-permute-start | bytes 405512 | tf_op jit(solution)/shard_map/ppermute | solution.py:308
  11.8 5.7 %collective-permute-start.2 = (f32[256,128]{1,0:T(8,128)S(1)}, f32[256,128]{1,0:T(8,128)S(1)}, u32[]{:S(2)}, u32[]{:S(2)}) collective-permute-start(f32[256,128]{1,0:T(8,128)S(1)} %slice.17.own_ref), channel_id=1, source_target_pairs={{0,8},{4,12},{8,0},{12,4},{1,9},{5,13},{9,1},{13,5},{2,10},{6,14},... | collective-permute-start | bytes 393224 | tf_op jit(solution)/shard_map/ppermute | solution.py:308
  17.5 5.1 %collective-permute-start.3 = (f32[264,128]{1,0:T(8,128)S(1)}, f32[264,128]{1,0:T(8,128)S(1)}, u32[]{:S(2)}, u32[]{:S(2)}) collective-permute-start(f32[264,128]{1,0:T(8,128)S(1)} %broadcast_select_fusion.4), channel_id=1, source_target_pairs={{0,1},{1,0},{2,3},{3,2},{4,5},{5,4},{6,7},{7,6},{8,9},{9,8},{10,11... | collective-permute-start | bytes 405512 | tf_op jit(solution)/shard_map/ppermute | solution.py:308
  22.6 5.1 %collective-permute-start.4 = (f32[264,128]{1,0:T(8,128)S(1)}, f32[264,128]{1,0:T(8,128)S(1)}, u32[]{:S(2)}, u32[]{:S(2)}) collective-permute-start(f32[264,128]{1,0:T(8,128)S(1)} %broadcast_select_fusion.5), channel_id=1, source_target_pairs={{0,8},{4,12},{8,0},{12,4},{1,9},{5,13},{9,1},{13,5},{2,10},{6,14},... | collective-permute-start | bytes 405512 | tf_op jit(solution)/shard_map/ppermute | solution.py:308
  24.1 5.0 %collective-permute-start.6 = (f32[256,128]{1,0:T(8,128)S(1)}, f32[256,128]{1,0:T(8,128)S(1)}, u32[]{:S(2)}, u32[]{:S(2)}) collective-permute-start(f32[256,128]{1,0:T(8,128)S(1)} %slice_select_fusion.1), channel_id=1, source_target_pairs={{0,8},{4,12},{8,0},{12,4},{1,9},{5,13},{9,1},{13,5},{2,10},{6,14},... | collective-permute-start | bytes 393224 | tf_op jit(solution)/shard_map/ppermute | solution.py:308
  27.7 1.5 %collective-permute-start.5 = (f32[264,128]{1,0:T(8,128)S(1)}, f32[264,128]{1,0:T(8,128)S(1)}, u32[]{:S(2)}, u32[]{:S(2)}) collective-permute-start(f32[264,128]{1,0:T(8,128)S(1)} %broadcast_select_fusion.6), channel_id=1, source_target_pairs={{0,4},{4,0},{8,12},{12,8},{1,5},{5,1},{9,13},{13,9},{2,6},{6,2},{1... | collective-permute-start | bytes 405512 | tf_op jit(solution)/shard_map/ppermute | solution.py:308
  29.2 7.0 %collective-permute-start.8 = (f32[256,128]{1,0:T(8,128)S(1)}, f32[256,128]{1,0:T(8,128)S(1)}, u32[]{:S(2)}, u32[]{:S(2)}) collective-permute-start(f32[256,128]{1,0:T(8,128)S(1)} %slice_select_fusion), channel_id=1, source_target_pairs={{0,16},{16,0},{1,17},{17,1},{2,18},{18,2},{3,19},{19,3},{4,20},{20... | collective-permute-start | bytes 393224 | tf_op jit(solution)/shard_map/ppermute | solution.py:308
  30.8 8.6 %collective-permute-start.10 = (f32[256,128]{1,0:T(8,128)S(1)}, f32[256,128]{1,0:T(8,128)S(1)}, u32[]{:S(2)}, u32[]{:S(2)}) collective-permute-start(f32[256,128]{1,0:T(8,128)S(1)} %broadcast_select_fusion.8), channel_id=1, source_target_pairs={{0,16},{16,0},{1,17},{17,1},{2,18},{18,2},{3,19},{19,3},{4,20},{20... | collective-permute-start | bytes 393224 | tf_op jit(solution)/shard_map/ppermute | solution.py:308
  31.3 16.6 %collective-permute-start.7 = (f32[2,256,128]{2,1,0:T(8,128)S(1)}, f32[2,256,128]{2,1,0:T(8,128)S(1)}, u32[]{:S(2)}, u32[]{:S(2)}) collective-permute-start(f32[2,256,128]{2,1,0:T(8,128)S(1)} %pad_maximum_fusion.1), channel_id=1, source_target_pairs={{0,16},{16,0},{1,17},{17,1},{2,18},{18,2},{3,19},{19,3},{4,20},{20... | collective-permute-start | bytes 786440 | tf_op jit(solution)/shard_map/ppermute | solution.py:308
  36.3 3.7 %collective-permute-start.9 = (f32[2,256,128]{2,1,0:T(8,128)S(1)}, f32[2,256,128]{2,1,0:T(8,128)S(1)}, u32[]{:S(2)}, u32[]{:S(2)}) collective-permute-start(f32[2,256,128]{2,1,0:T(8,128)S(1)} %pad_maximum_fusion.2), channel_id=1, source_target_pairs={{0,4},{4,0},{8,12},{12,8},{1,5},{5,1},{9,13},{13,9},{2,6},{6,2},{1... | collective-permute-start | bytes 786440 | tf_op jit(solution)/shard_map/ppermute | solution.py:308
  39.4 8.5 %collective-permute-start.11 = (f32[2,256,128]{2,1,0:T(8,128)S(1)}, f32[2,256,128]{2,1,0:T(8,128)S(1)}, u32[]{:S(2)}, u32[]{:S(2)}) collective-permute-start(f32[2,256,128]{2,1,0:T(8,128)S(1)} %pad_maximum_fusion.3), channel_id=1, source_target_pairs={{0,4},{4,0},{8,12},{12,8},{1,5},{5,1},{9,13},{13,9},{2,6},{6,2},{1... | collective-permute-start | bytes 786440 | tf_op jit(solution)/shard_map/ppermute | solution.py:308

commit v4 on v3

--- a/solution.py
+++ b/solution.py
@@ -107,7 +107,7 @@
     return [tile[g * SUB : (g + 1) * SUB, :] for g in range(tile.shape[0] // SUB)]
 
 
-def factor(tile, lower_ref, inverse_ref, work):
+def factor(tile, turned_ref, inverse_ref, work):
     order = tile.shape[0]
     half = order // 2
     at_row = lax.broadcasted_iota(jnp.int32, tile.shape, 0)
@@ -130,12 +130,23 @@
     inverse_ref[:half, half:] = jnp.zeros((half, half), F32)
     inverse_ref[half:, :half] = -dot(inverse1, dot(under, inverse0)) * scale[half:, :half]
     inverse_ref[half:, half:] = inverse1 * scale[half:, half:]
-    work[:half, :] = jnp.where(at_col[:half] < half, first, 0.0)
-    work[half:, :half] = jnp.zeros((half, half), F32)
-    work[half:, half:] = second[:, :half]
-    up = recip(down)
-    lower_ref[...] = work[...].T * up
-    lower_ref[half:, :half] = under * up[half:, :half]
+    across, up = recip(scale), recip(down)
+    turned_ref[:half, :half] = first[:, :half] * across[:half, :half]
+    turned_ref[:half, half:] = jnp.zeros((half, half), F32)
+    turned_ref[half:, :half] = under * up[half:, :half]
+    turned_ref[half:, half:] = second[:, :half] * across[half:, half:]
+
+
+def turn_back(from_ref, to_ref, tile):
+    width = from_ref.shape[0]
+    at_row = lax.broadcasted_iota(jnp.int32, (tile, tile), 0)
+    at_col = lax.broadcasted_iota(jnp.int32, (tile, tile), 1)
+    same = at_row // (tile // 2) == at_col // (tile // 2)
+    to_ref[...] = from_ref[...]
+    for t in range(0, width, tile):
+        at = slice(t, t + tile)
+        held = from_ref[at, at]
+        to_ref[at, at] = jnp.where(same, held.T, held)
 
 
 def pack_kernel(index_ref, source_ref, mine_ref, *refs):
@@ -183,20 +194,20 @@
     return part + jnp.where(at, 0.0, part).T
 
 
-def first_kernel(packed_ref, block_ref, lower_ref, inverse_ref, left_ref, rest_ref, work):
+def open_packed(packed_ref):
     tile = packed_ref.shape[1]
     at_row = lax.broadcasted_iota(jnp.int32, (tile, tile), 0)
     at_col = lax.broadcasted_iota(jnp.int32, (tile, tile), 1)
     mixed = packed_ref[:tile, :]
-    below = packed_ref[tile : 2 * tile, :]
     tile0 = symmetric(mixed, at_row >= at_col)
     upper1 = jnp.where(at_row < at_col, mixed, 0.0)
     diagonal = jnp.broadcast_to(packed_ref[2 * tile : 2 * tile + 1, :], (tile, tile))
     tile1 = upper1 + upper1.T + jnp.where(at_row == at_col, diagonal, 0.0)
-    block_ref[:tile, :tile] = tile0
-    block_ref[tile:, :tile] = below
-    block_ref[:tile, tile:] = below.T
-    block_ref[tile:, tile:] = tile1
+    return tile0, packed_ref[tile : 2 * tile, :], tile1
+
+
+def first_kernel(packed_ref, lower_ref, inverse_ref, left_ref, rest_ref, work):
+    tile0, below, tile1 = open_packed(packed_ref)
     factor(tile0, lower_ref, inverse_ref, work)
     left = dot(below, inverse_ref[...], NT)
     left_ref[...] = left
@@ -236,12 +247,14 @@
     lower_ref[second, first] = under
     inverse_ref[first, second] = zero
     factor(rest - dot(under, under, NT), lower_ref.at[second, second], inverse_ref.at[second, second], work)
-    inverse_ref[second, first] = -dot(inverse_ref[second, second], dot(under, inverse_ref[first, first]))
-    cross_ref[...] = -dot(inverse_ref[...], dot(left_ref[...], inverse0_ref[...]))
+    corner = dot_split(split(under), split(inverse_ref[first, first]))
+    inverse_ref[second, first] = -dot_split(split(inverse_ref[second, second]), split(corner))
+    cross = dot_split(split(left_ref[...]), split(inverse0_ref[...]))
+    cross_ref[...] = -dot_split(split(inverse_ref[...]), split(cross))
 
 
 def final_kernel(
-    index_ref, keep_ref, own_ref, block_ref, rows_ref, col0_ref, col1_ref,
+    index_ref, keep_ref, own_ref, packed_ref, rows_ref, col0_ref, col1_ref,
     lower0_ref, inverse0_ref, lower1_ref, inverse1_ref, left_ref, cross_ref,
     schur_ref, panels_ref, upper_ref, row_ref,
 ):
@@ -254,13 +267,13 @@
 
     @pl.when(row == 0)
     def _():
-        panels_ref[0] = lower0_ref[...]
+        turn_back(lower0_ref, panels_ref.at[0], tile)
         panels_ref[1] = jnp.zeros((width, width), F32)
 
     @pl.when(row == 1)
     def _():
         panels_ref[0] = left_ref[...]
-        panels_ref[1] = lower1_ref[...]
+        turn_back(lower1_ref, panels_ref.at[1], tile)
 
     @pl.when(row > 1)
     def _():
@@ -273,6 +286,14 @@
     @pl.when(col == 0)
     def _():
         upper_ref[...] = jnp.zeros(upper_ref.shape, F32)
+
+    @pl.when((row == 0) & (col == 0))
+    def _():
+        tile0, below, tile1 = open_packed(packed_ref)
+        row_ref[0, :tile, :tile] = tile0
+        row_ref[0, tile:, :tile] = below
+        row_ref[0, :tile, tile:] = below.T
+        row_ref[0, tile:, tile:] = tile1
 
     @pl.when(col == 1)
     def _():
@@ -297,7 +318,7 @@
             keep = jnp.where(at_row == i, keep_ref[i, j], keep)
         own = own_ref[pl.ds(j, slab_rows, tiles_per), :]
         at = slice(j * tile, (j + 1) * tile)
-        own = jnp.where((row == 0) & (col == 0), block_ref[slab, at], own)
+        own = jnp.where((row == 0) & (col == 0), row_ref[0, slab, at], own)
         schur_ref[pl.ds(j, slab_rows, tiles_per), :] = own - jnp.where(keep > 0, product[:, at], 0.0)
 
 
@@ -393,6 +414,9 @@
     fall_got = after(fall_got, lead)
     lead = after(lead, fall_got)
     got = trade(lead, "col", 1)
+    fall_from, fall_got = after(fall_from, lead), after(fall_got, lead)
+    fall = jnp.where(row % 4 >= 2, fall_got, fall_from)
+    fall_parts = ask_layers(fall)
     low, high = jnp.where(even_col, lead, got), jnp.where(even_col, got, lead)
     panels_in = jnp.stack([low[:piece_rows], high[:piece_rows]])
     high = high[:piece_rows]
@@ -409,14 +433,12 @@
     got = trade(low, "row", 1)
     packed = jnp.where(even_row, low, got)
     lead_parts = ask_layers(jnp.where(even_row, got[:piece_rows], high))
-    fall = jnp.where(row % 4 >= 2, fall_got, fall_from)
-    fall_parts = ask_layers(after(fall, lead_parts[0]))
     rows_in = ask_layers(after(panels_in, lead_parts[0]))
     packed = after(packed, high)
 
-    block0, small_lower, small_inverse, left0, rest0 = run(
+    small_lower, small_inverse, left0, rest0 = run(
         first_kernel,
-        (big, square, square, square, square),
+        (square, square, square, square),
         (packed,),
         scratch=(square,),
         flops=5 * 10**9,
@@ -449,7 +471,7 @@
     schur, panels = run(
         final_kernel,
         ((piece_rows, tile), (2, width, width)),
-        (index, keep, piece, block0, rows_in, col0, col1, lower0, inverse0, lower1, inverse1, left1, cross),
+        (index, keep, piece, packed, rows_in, col0, col1, lower0, inverse0, lower1, inverse1, left1, cross),
         scratch=((2 * width, width), (2, width, width)),
         flops=10**9,
         name="kf",

time: 49.8 us -> 48.3 us (0.970)
  waiting for transfers between devices: 16.1 us -> 14.6 us
    ppermute x12, waiting for transfers between devices: 16.1 us -> 14.6 us  [trade(): lax.ppermute(x, axis, [(i, i ^ k) for i in range(lax.axis_size(axis))])]
where the time goes in v4:
time: 48.3 us; the launch traced here: 48.1 us
  Pallas kernels  17.3 us (36%)
  starting transfers between devices  14.9 us (31%)
  waiting for transfers between devices  14.6 us (30%)
  between operations  0.83 us (2%)
    pallas_call x5, Pallas kernels, run(): pl.pallas_call(kernel, out_shape=tuple((jax.ShapeDtypeStruct(s, F32) for...  17.3 us
    ppermute x12, starting transfers between devices, trade(): lax.ppermute(x, axis, [(i, i ^ k) for i in range(lax.axis_size(axis))])  14.9 us
    ppermute x12, waiting for transfers between devices, trade(): lax.ppermute(x, axis, [(i, i ^ k) for i in range(lax.axis_size(axis))])  14.6 us
  transfers between devices with their start and end apart: 12, of which 5 were waited for; matrix products, arithmetic and copies ran while one was open for 1% of the time, Pallas kernels for 29%

profile of v4, /device:TPU:0, one launch (start us, length us, event | category | flops | bytes accessed | tf_op | source)
XLA Modules:
  0.0 48.1 jit_solution(13044445224248948482)
XLA Ops:
  0.6 0.1 pad_add_fusion.index_ref
  0.7 1.5 %k0.1 = (f32[264,128]{1,0:T(8,128)S(1)}, f32[264,128]{1,0:T(8,128)S(1)}) custom-call(s32[3]{0:T(128)S(1)} %pad_add_fusion.index_ref, f32[512,128]{1,0:T(8,128)} %bitcast.26), custom_call_target="tpu_custom_call" | custom-call | bytes 1000000 | tf_op jit(solution)/shard_map/k0/pallas_call | solution.py:366
  2.2 3.0 %collective-permute-start = (f32[264,128]{1,0:T(8,128)S(1)}, f32[264,128]{1,0:T(8,128)S(1)}, u32[]{:S(2)}, u32[]{:S(2)}) collective-permute-start(f32[264,128]{1,0:T(8,128)S(1)} %get-tuple-element.32), channel_id=1, source_target_pairs={{0,16},{16,0},{1,17},{17,1},{2,18},{18,2},{3,19},{19,3},{4,20},{20... | collective-permute-start | bytes 405512 | tf_op jit(solution)/shard_map/ppermute | solution.py:329
  5.3 3.6 %collective-permute-done = f32[264,128]{1,0:T(8,128)S(1)} collective-permute-done((f32[264,128]{1,0:T(8,128)S(1)}, f32[264,128]{1,0:T(8,128)S(1)}, u32[]{:S(2)}, u32[]{:S(2)}) %collective-permute-start) | collective-permute-done | bytes 135200 | tf_op jit(solution)/shard_map/ppermute | solution.py:329
  8.8 0.0 copy-start
  8.8 2.9 %collective-permute-start.1 = (f32[264,128]{1,0:T(8,128)S(1)}, f32[264,128]{1,0:T(8,128)S(1)}, u32[]{:S(2)}, u32[]{:S(2)}) collective-permute-start(f32[264,128]{1,0:T(8,128)S(1)} %add.18), channel_id=1, source_target_pairs={{0,2},{1,3},{2,0},{3,1},{4,6},{5,7},{6,4},{7,5},{8,10},{9,11},{10,... | collective-permute-start | bytes 405512 | tf_op jit(solution)/shard_map/ppermute | solution.py:329
  11.8 0.0 copy-done
  11.8 1.6 %collective-permute-start.2 = (f32[256,128]{1,0:T(8,128)S(1)}, f32[256,128]{1,0:T(8,128)S(1)}, u32[]{:S(2)}, u32[]{:S(2)}) collective-permute-start(f32[256,128]{1,0:T(8,128)S(1)} %slice.17.own_ref), channel_id=1, source_target_pairs={{0,8},{4,12},{8,0},{12,4},{1,9},{5,13},{9,1},{13,5},{2,10},{6,14},... | collective-permute-start | bytes 393224 | tf_op jit(solution)/shard_map/ppermute | solution.py:329
  13.4 4.1 %collective-permute-done.1 = f32[264,128]{1,0:T(8,128)S(1)} collective-permute-done((f32[264,128]{1,0:T(8,128)S(1)}, f32[264,128]{1,0:T(8,128)S(1)}, u32[]{:S(2)}, u32[]{:S(2)}) %collective-permute-start.1) | collective-permute-done | bytes 135200 | tf_op jit(solution)/shard_map/ppermute | solution.py:329
  17.5 0.0 collective-permute-done.2
  17.5 0.9 %collective-permute-start.3 = (f32[264,128]{1,0:T(8,128)S(1)}, f32[264,128]{1,0:T(8,128)S(1)}, u32[]{:S(2)}, u32[]{:S(2)}) collective-permute-start(f32[264,128]{1,0:T(8,128)S(1)} %broadcast_select_fusion.4), channel_id=1, source_target_pairs={{0,1},{1,0},{2,3},{3,2},{4,5},{5,4},{6,7},{7,6},{8,9},{9,8},{10,11... | collective-permute-start | bytes 405512 | tf_op jit(solution)/shard_map/ppermute | solution.py:329
  18.4 1.6 %collective-permute-start.10 = (f32[256,128]{1,0:T(8,128)S(1)}, f32[256,128]{1,0:T(8,128)S(1)}, u32[]{:S(2)}, u32[]{:S(2)}) collective-permute-start(f32[256,128]{1,0:T(8,128)S(1)} %broadcast_select_fusion.8), channel_id=1, source_target_pairs={{0,16},{16,0},{1,17},{17,1},{2,18},{18,2},{3,19},{19,3},{4,20},{20... | collective-permute-start | bytes 393224 | tf_op jit(solution)/shard_map/ppermute | solution.py:329
  20.0 2.6 %collective-permute-done.3 = f32[264,128]{1,0:T(8,128)S(1)} collective-permute-done((f32[264,128]{1,0:T(8,128)S(1)}, f32[264,128]{1,0:T(8,128)S(1)}, u32[]{:S(2)}, u32[]{:S(2)}) %collective-permute-start.3) | collective-permute-done | bytes 135200 | tf_op jit(solution)/shard_map/ppermute | solution.py:329
  22.6 1.5 %collective-permute-start.4 = (f32[264,128]{1,0:T(8,128)S(1)}, f32[264,128]{1,0:T(8,128)S(1)}, u32[]{:S(2)}, u32[]{:S(2)}) collective-permute-start(f32[264,128]{1,0:T(8,128)S(1)} %broadcast_select_fusion.5), channel_id=1, source_target_pairs={{0,8},{4,12},{8,0},{12,4},{1,9},{5,13},{9,1},{13,5},{2,10},{6,14},... | collective-permute-start | bytes 405512 | tf_op jit(solution)/shard_map/ppermute | solution.py:329
  24.1 0.6 %collective-permute-start.6 = (f32[256,128]{1,0:T(8,128)S(1)}, f32[256,128]{1,0:T(8,128)S(1)}, u32[]{:S(2)}, u32[]{:S(2)}) collective-permute-start(f32[256,128]{1,0:T(8,128)S(1)} %slice_select_fusion.1), channel_id=1, source_target_pairs={{0,8},{4,12},{8,0},{12,4},{1,9},{5,13},{9,1},{13,5},{2,10},{6,14},... | collective-permute-start | bytes 393224 | tf_op jit(solution)/shard_map/ppermute | solution.py:329
  24.8 2.9 %collective-permute-done.4 = f32[264,128]{1,0:T(8,128)S(1)} collective-permute-done((f32[264,128]{1,0:T(8,128)S(1)}, f32[264,128]{1,0:T(8,128)S(1)}, u32[]{:S(2)}, u32[]{:S(2)}) %collective-permute-start.4) | collective-permute-done | bytes 135200 | tf_op jit(solution)/shard_map/ppermute | solution.py:329
  27.7 0.1 collective-permute-start.5
  27.8 1.4 %collective-permute-done.6 = f32[256,128]{1,0:T(8,128)S(1)} collective-permute-done((f32[256,128]{1,0:T(8,128)S(1)}, f32[256,128]{1,0:T(8,128)S(1)}, u32[]{:S(2)}, u32[]{:S(2)}) %collective-permute-start.6) | collective-permute-done | bytes 131104 | tf_op jit(solution)/shard_map/ppermute | solution.py:329
  29.2 0.0 collective-permute-done.5
  29.2 1.6 %collective-permute-start.8 = (f32[256,128]{1,0:T(8,128)S(1)}, f32[256,128]{1,0:T(8,128)S(1)}, u32[]{:S(2)}, u32[]{:S(2)}) collective-permute-start(f32[256,128]{1,0:T(8,128)S(1)} %slice_select_fusion), channel_id=1, source_target_pairs={{0,16},{16,0},{1,17},{17,1},{2,18},{18,2},{3,19},{19,3},{4,20},{20... | collective-permute-start | bytes 393224 | tf_op jit(solution)/shard_map/ppermute | solution.py:329
  30.8 3.4 %k1.1 = (f32[128,128]{1,0:T(8,128)S(1)}, f32[128,128]{1,0:T(8,128)S(1)}, f32[128,128]{1,0:T(8,128)S(1)}, f32[128,128]{1,0:T(8,128)S(1)}) custom-call(f32[264,128]{1,0:T(8,128)S(1)} %broadcast_select_fusion.7.packed_ref), custom_call_target="tpu_custom_call" | custom-call | flops 5000000000 | bytes 1000000 | tf_op jit(solution)/shard_map/k1/pallas_call | solution.py:366
  34.2 0.6 %collective-permute-start.7 = (f32[2,256,128]{2,1,0:T(8,128)S(1)}, f32[2,256,128]{2,1,0:T(8,128)S(1)}, u32[]{:S(2)}, u32[]{:S(2)}) collective-permute-start(f32[2,256,128]{2,1,0:T(8,128)S(1)} %pad_maximum_fusion.1), channel_id=1, source_target_pairs={{0,16},{16,0},{1,17},{17,1},{2,18},{18,2},{3,19},{19,3},{4,20},{20... | collective-permute-start | bytes 786440 | tf_op jit(solution)/shard_map/ppermute | solution.py:329
  34.8 0.0 collective-permute-done.8
  34.9 0.1 collective-permute-start.9
  34.9 2.9 %k2.1 = (f32[256,256]{1,0:T(8,128)S(1)}, f32[256,256]{1,0:T(8,128)S(1)}) custom-call(f32[128,128]{1,0:T(8,128)S(1)} %get-tuple-element.42.lower0_ref, f32[128,128]{1,0:T(8,128)S(1)} %get-tuple-element.43.inverse0_ref, f32[128,128]{1,0:T(8,128)S(1)} %get-tuple-element.44.left_ref, f32[128,128]{1,0:T(8,128)S(1)} %get-tuple-element.45.rest_ref), custom_call_target="tpu_custom_call" | custom-call | flops 5000000000 | bytes 1000000 | tf_op jit(solution)/shard_map/k2/pallas_call | solution.py:366
  37.9 0.0 collective-permute-done.10
  37.9 0.6 %collective-permute-start.11 = (f32[2,256,128]{2,1,0:T(8,128)S(1)}, f32[2,256,128]{2,1,0:T(8,128)S(1)}, u32[]{:S(2)}, u32[]{:S(2)}) collective-permute-start(f32[2,256,128]{2,1,0:T(8,128)S(1)} %pad_maximum_fusion.3), channel_id=1, source_target_pairs={{0,4},{4,0},{8,12},{12,8},{1,5},{5,1},{9,13},{13,9},{2,6},{6,2},{1... | collective-permute-start | bytes 786440 | tf_op jit(solution)/shard_map/ppermute | solution.py:329
  38.5 0.0 collective-permute-done.9
  38.6 7.6 %k3.1 = (f32[256,256]{1,0:T(8,128)S(1)}, f32[256,256]{1,0:T(8,128)S(1)}, f32[256,256]{1,0:T(8,128)S(1)}, f32[256,256]{1,0:T(8,128)S(1)}) custom-call(f32[2,256,128]{2,1,0:T(8,128)S(1)} %get-tuple-element.69.corners_ref, f32[2,256,128]{2,1,0:T(8,128)S(1)} %get-tuple-element.68.belows_ref, f32[256,256]{1,0:T(8,128)S(1)} %get-tuple-element.46.inverse0_ref), custom_call_target="tpu_custom_call" | custom-call | flops 10000000000 | bytes 1000000 | tf_op jit(solution)/shard_map/k3/pallas_call | solution.py:366
  46.2 0.0 collective-permute-done.11
  46.2 0.0 collective-permute-done.7
  46.3 1.8 %kf.1 = (f32[256,128]{1,0:T(8,128)}, f32[2,256,256]{2,1,0:T(8,128)}) custom-call(s32[3]{0:T(128)S(1)} %pad_add_fusion.index_ref, s32[2,2]{1,0:T(2,128)S(1)} %bitcast.24, f32[256,128]{1,0:T(8,128)S(1)} %slice.17.own_ref, f32[264,128]{1,0:T(8,128)S(1)} %broadcast_select_fusion.7.packed_ref, f32[2,2,256,128]{3,2,1,0:T(8,128)S(1)} %pad_maximum_fusion.rows_ref, ...), custom_call_target="tpu_custom_call" | custom-call | flops 1000000000 | bytes 1000000 | tf_op jit(solution)/shard_map/kf/pallas_call | solution.py:366
  (20 shorter events, 0.4 us)
Async XLA Ops:
  2.2 6.6 %collective-permute-start = (f32[264,128]{1,0:T(8,128)S(1)}, f32[264,128]{1,0:T(8,128)S(1)}, u32[]{:S(2)}, u32[]{:S(2)}) collective-permute-start(f32[264,128]{1,0:T(8,128)S(1)} %get-tuple-element.32), channel_id=1, source_target_pairs={{0,16},{16,0},{1,17},{17,1},{2,18},{18,2},{3,19},{19,3},{4,20},{20... | collective-permute-start | bytes 405512 | tf_op jit(solution)/shard_map/ppermute | solution.py:329
  8.8 2.9 %copy-start = (s32[1,1,2,1,1,2]{5,4,3,2,1,0:T(1,128)S(1)}, s32[1,1,2,1,1,2]{5,4,3,2,1,0:T(1,128)}, u32[]{:S(2)}) copy-start(s32[1,1,2,1,1,2]{5,4,3,2,1,0:T(1,128)} %param.3) | copy-start | bytes 52
  8.8 8.6 %collective-permute-start.1 = (f32[264,128]{1,0:T(8,128)S(1)}, f32[264,128]{1,0:T(8,128)S(1)}, u32[]{:S(2)}, u32[]{:S(2)}) collective-permute-start(f32[264,128]{1,0:T(8,128)S(1)} %add.18), channel_id=1, source_target_pairs={{0,2},{1,3},{2,0},{3,1},{4,6},{5,7},{6,4},{7,5},{8,10},{9,11},{10,... | collective-permute-start | bytes 405512 | tf_op jit(solution)/shard_map/ppermute | solution.py:329
  11.8 5.7 %collective-permute-start.2 = (f32[256,128]{1,0:T(8,128)S(1)}, f32[256,128]{1,0:T(8,128)S(1)}, u32[]{:S(2)}, u32[]{:S(2)}) collective-permute-start(f32[256,128]{1,0:T(8,128)S(1)} %slice.17.own_ref), channel_id=1, source_target_pairs={{0,8},{4,12},{8,0},{12,4},{1,9},{5,13},{9,1},{13,5},{2,10},{6,14},... | collective-permute-start | bytes 393224 | tf_op jit(solution)/shard_map/ppermute | solution.py:329
  17.5 5.1 %collective-permute-start.3 = (f32[264,128]{1,0:T(8,128)S(1)}, f32[264,128]{1,0:T(8,128)S(1)}, u32[]{:S(2)}, u32[]{:S(2)}) collective-permute-start(f32[264,128]{1,0:T(8,128)S(1)} %broadcast_select_fusion.4), channel_id=1, source_target_pairs={{0,1},{1,0},{2,3},{3,2},{4,5},{5,4},{6,7},{7,6},{8,9},{9,8},{10,11... | collective-permute-start | bytes 405512 | tf_op jit(solution)/shard_map/ppermute | solution.py:329
  18.4 19.5 %collective-permute-start.10 = (f32[256,128]{1,0:T(8,128)S(1)}, f32[256,128]{1,0:T(8,128)S(1)}, u32[]{:S(2)}, u32[]{:S(2)}) collective-permute-start(f32[256,128]{1,0:T(8,128)S(1)} %broadcast_select_fusion.8), channel_id=1, source_target_pairs={{0,16},{16,0},{1,17},{17,1},{2,18},{18,2},{3,19},{19,3},{4,20},{20... | collective-permute-start | bytes 393224 | tf_op jit(solution)/shard_map/ppermute | solution.py:329
  22.6 5.1 %collective-permute-start.4 = (f32[264,128]{1,0:T(8,128)S(1)}, f32[264,128]{1,0:T(8,128)S(1)}, u32[]{:S(2)}, u32[]{:S(2)}) collective-permute-start(f32[264,128]{1,0:T(8,128)S(1)} %broadcast_select_fusion.5), channel_id=1, source_target_pairs={{0,8},{4,12},{8,0},{12,4},{1,9},{5,13},{9,1},{13,5},{2,10},{6,14},... | collective-permute-start | bytes 405512 | tf_op jit(solution)/shard_map/ppermute | solution.py:329
  24.1 5.0 %collective-permute-start.6 = (f32[256,128]{1,0:T(8,128)S(1)}, f32[256,128]{1,0:T(8,128)S(1)}, u32[]{:S(2)}, u32[]{:S(2)}) collective-permute-start(f32[256,128]{1,0:T(8,128)S(1)} %slice_select_fusion.1), channel_id=1, source_target_pairs={{0,8},{4,12},{8,0},{12,4},{1,9},{5,13},{9,1},{13,5},{2,10},{6,14},... | collective-permute-start | bytes 393224 | tf_op jit(solution)/shard_map/ppermute | solution.py:329
  27.7 1.5 %collective-permute-start.5 = (f32[264,128]{1,0:T(8,128)S(1)}, f32[264,128]{1,0:T(8,128)S(1)}, u32[]{:S(2)}, u32[]{:S(2)}) collective-permute-start(f32[264,128]{1,0:T(8,128)S(1)} %broadcast_select_fusion.6), channel_id=1, source_target_pairs={{0,4},{4,0},{8,12},{12,8},{1,5},{5,1},{9,13},{13,9},{2,6},{6,2},{1... | collective-permute-start | bytes 405512 | tf_op jit(solution)/shard_map/ppermute | solution.py:329
  29.2 5.6 %collective-permute-start.8 = (f32[256,128]{1,0:T(8,128)S(1)}, f32[256,128]{1,0:T(8,128)S(1)}, u32[]{:S(2)}, u32[]{:S(2)}) collective-permute-start(f32[256,128]{1,0:T(8,128)S(1)} %slice_select_fusion), channel_id=1, source_target_pairs={{0,16},{16,0},{1,17},{17,1},{2,18},{18,2},{3,19},{19,3},{4,20},{20... | collective-permute-start | bytes 393224 | tf_op jit(solution)/shard_map/ppermute | solution.py:329
  34.2 12.0 %collective-permute-start.7 = (f32[2,256,128]{2,1,0:T(8,128)S(1)}, f32[2,256,128]{2,1,0:T(8,128)S(1)}, u32[]{:S(2)}, u32[]{:S(2)}) collective-permute-start(f32[2,256,128]{2,1,0:T(8,128)S(1)} %pad_maximum_fusion.1), channel_id=1, source_target_pairs={{0,16},{16,0},{1,17},{17,1},{2,18},{18,2},{3,19},{19,3},{4,20},{20... | collective-permute-start | bytes 786440 | tf_op jit(solution)/shard_map/ppermute | solution.py:329
  34.9 3.6 %collective-permute-start.9 = (f32[2,256,128]{2,1,0:T(8,128)S(1)}, f32[2,256,128]{2,1,0:T(8,128)S(1)}, u32[]{:S(2)}, u32[]{:S(2)}) collective-permute-start(f32[2,256,128]{2,1,0:T(8,128)S(1)} %pad_maximum_fusion.2), channel_id=1, source_target_pairs={{0,4},{4,0},{8,12},{12,8},{1,5},{5,1},{9,13},{13,9},{2,6},{6,2},{1... | collective-permute-start | bytes 786440 | tf_op jit(solution)/shard_map/ppermute | solution.py:329
  37.9 8.2 %collective-permute-start.11 = (f32[2,256,128]{2,1,0:T(8,128)S(1)}, f32[2,256,128]{2,1,0:T(8,128)S(1)}, u32[]{:S(2)}, u32[]{:S(2)}) collective-permute-start(f32[2,256,128]{2,1,0:T(8,128)S(1)} %pad_maximum_fusion.3), channel_id=1, source_target_pairs={{0,4},{4,0},{8,12},{12,8},{1,5},{5,1},{9,13},{13,9},{2,6},{6,2},{1... | collective-permute-start | bytes 786440 | tf_op jit(solution)/shard_map/ppermute | solution.py:329

commit v5 on v4

--- a/solution.py
+++ b/solution.py
@@ -107,30 +107,35 @@
     return [tile[g * SUB : (g + 1) * SUB, :] for g in range(tile.shape[0] // SUB)]
 
 
-def factor(tile, turned_ref, inverse_ref, work):
-    order = tile.shape[0]
-    half = order // 2
+def scales(tile):
     at_row = lax.broadcasted_iota(jnp.int32, tile.shape, 0)
     at_col = lax.broadcasted_iota(jnp.int32, tile.shape, 1)
     diagonal = jnp.sum(jnp.where(at_row == at_col, tile, 0.0), axis=0, keepdims=True)
-    scale = jnp.broadcast_to(lax.rsqrt(diagonal), tile.shape)
-    down = scale.T
-    a = tile * scale * down
-    one = jnp.where(at_row[:half, :half] == at_col[:half, :half], 1.0, 0.0).astype(F32)
-    beside = jnp.where(at_row[:half] + half == at_col[:half], 1.0, 0.0).astype(F32)
+    along = jnp.broadcast_to(lax.rsqrt(diagonal), tile.shape)
+    return along, along.T
+
+
+def factor(tile, along, down, turned_ref, inverse_ref, work):
+    half = tile.shape[0] // 2
+    at_row = lax.broadcasted_iota(jnp.int32, (half, 2 * half), 0)
+    at_col = lax.broadcasted_iota(jnp.int32, (half, 2 * half), 1)
+    a = tile * along * down
+    one = jnp.where(at_row[:, :half] == at_col[:, :half], 1.0, 0.0).astype(F32)
+    beside = jnp.where(at_row + half == at_col, 1.0, 0.0).astype(F32)
+    work[:half, :half] = jnp.zeros((half, half), F32)
+    work[:half, half:] = a[half:, :half]
     work[half:, :half] = a[half:, half:]
     work[half:, half:] = one
-    first = jnp.concatenate(factor_rows(tile_rows(jnp.where(at_col[:half] < half, a[:half], beside))), axis=0)
-    inverse0 = first[:, half:]
-    under = dot(a[half:, :half], inverse0, NT)
+    first = jnp.concatenate(factor_rows(tile_rows(jnp.where(at_col < half, a[:half], beside))), axis=0)
+    under = dot(work[:half, :], first, NT)
     work[half:, :half] -= dot(under, under, NT)
     second = jnp.concatenate(factor_rows(tile_rows(work[half:, :])), axis=0)
-    inverse1 = second[:, half:]
-    inverse_ref[:half, :half] = inverse0 * scale[:half, :half]
+    inverse0, inverse1 = first[:, half:], second[:, half:]
+    inverse_ref[:half, :half] = inverse0 * along[:half, :half]
     inverse_ref[:half, half:] = jnp.zeros((half, half), F32)
-    inverse_ref[half:, :half] = -dot(inverse1, dot(under, inverse0)) * scale[half:, :half]
-    inverse_ref[half:, half:] = inverse1 * scale[half:, half:]
-    across, up = recip(scale), recip(down)
+    inverse_ref[half:, :half] = -dot(inverse1, dot(under, inverse0)) * along[half:, :half]
+    inverse_ref[half:, half:] = inverse1 * along[half:, half:]
+    across, up = recip(along), recip(down)
     turned_ref[:half, :half] = first[:, :half] * across[:half, :half]
     turned_ref[:half, half:] = jnp.zeros((half, half), F32)
     turned_ref[half:, :half] = under * up[half:, :half]
@@ -206,15 +211,20 @@
     return tile0, packed_ref[tile : 2 * tile, :], tile1
 
 
-def first_kernel(packed_ref, lower_ref, inverse_ref, left_ref, rest_ref, work):
+def first_kernel(packed_ref, lower_ref, inverse_ref, left_ref, rest_ref, along_ref, down_ref, work):
     tile0, below, tile1 = open_packed(packed_ref)
-    factor(tile0, lower_ref, inverse_ref, work)
+    along, down = scales(tile1)
+    along_ref[...] = along
+    down_ref[...] = down
+    factor(tile0, *scales(tile0), lower_ref, inverse_ref, work)
     left = dot(below, inverse_ref[...], NT)
     left_ref[...] = left
     rest_ref[...] = tile1 - dot(left, left, NT)
 
 
-def second_kernel(lower0_ref, inverse0_ref, left_ref, rest_ref, lower_ref, inverse_ref, work):
+def second_kernel(
+    lower0_ref, inverse0_ref, left_ref, rest_ref, along_ref, down_ref, lower_ref, inverse_ref, work
+):
     tile = rest_ref.shape[0]
     zero = jnp.zeros((tile, tile), F32)
     first, second = slice(0, tile), slice(tile, 2 * tile)
@@ -223,7 +233,9 @@
     lower_ref[second, first] = left_ref[...]
     inverse_ref[first, first] = inverse0_ref[...]
     inverse_ref[first, second] = zero
-    factor(rest_ref[...], lower_ref.at[second, second], inverse_ref.at[second, second], work)
+    factor(
+        rest_ref[...], along_ref[...], down_ref[...], lower_ref.at[second, second], inverse_ref.at[second, second], work
+    )
     inverse_ref[second, first] = -dot(inverse_ref[second, second], dot(left_ref[...], inverse0_ref[...]))
 
 
@@ -235,8 +247,12 @@
     zero = jnp.zeros((tile, tile), F32)
     unpack([belows_ref.at[t] for t in range(belows_ref.shape[0])], below_ref)
     unpack([corners_ref.at[t] for t in range(corners_ref.shape[0])], corner_ref)
+    scales0, scales1 = scales(corner_ref[first, first]), scales(corner_ref[second, second])
     top = dot(below_ref[first, :], inverse0_ref[...], NT)
-    factor(corner_ref[first, first] - dot(top, top, NT), lower_ref.at[first, first], inverse_ref.at[first, first], work)
+    factor(
+        corner_ref[first, first] - dot(top, top, NT),
+        *scales0, lower_ref.at[first, first], inverse_ref.at[first, first], work,
+    )
     bottom = dot(below_ref[second, :], inverse0_ref[...], NT)
     left_ref[first, :] = top
     left_ref[second, :] = bottom
@@ -246,7 +262,10 @@
     lower_ref[first, second] = zero
     lower_ref[second, first] = under
     inverse_ref[first, second] = zero
-    factor(rest - dot(under, under, NT), lower_ref.at[second, second], inverse_ref.at[second, second], work)
+    factor(
+        rest - dot(under, under, NT),
+        *scales1, lower_ref.at[second, second], inverse_ref.at[second, second], work,
+    )
     corner = dot_split(split(under), split(inverse_ref[first, first]))
     inverse_ref[second, first] = -dot_split(split(inverse_ref[second, second]), split(corner))
     cross = dot_split(split(left_ref[...]), split(inverse0_ref[...]))
@@ -436,9 +455,9 @@
     rows_in = ask_layers(after(panels_in, lead_parts[0]))
     packed = after(packed, high)
 
-    small_lower, small_inverse, left0, rest0 = run(
+    small_lower, small_inverse, left0, rest0, *scales0 = run(
         first_kernel,
-        (square, square, square, square),
+        (square,) * 6,
         (packed,),
         scratch=(square,),
         flops=5 * 10**9,
@@ -449,7 +468,7 @@
     lower0, inverse0 = run(
         second_kernel,
         (big, big),
-        (small_lower, small_inverse, left0, after(rest0, lead)),
+        (small_lower, small_inverse, left0, after(rest0, lead), *scales0),
         scratch=(square,),
         flops=5 * 10**9,
         name="k2",

time: 48.3 us -> 48.6 us (level)
  waiting for transfers between devices: 14.6 us -> 15.6 us
  Pallas kernels: 17.3 us -> 16.7 us
    ppermute x12, waiting for transfers between devices: 14.6 us -> 15.6 us  [trade(): lax.ppermute(x, axis, [(i, i ^ k) for i in range(lax.axis_size(axis))])]
    pallas_call x5, Pallas kernels: 17.3 us -> 16.7 us  [run(): pl.pallas_call(kernel, out_shape=tuple((jax.ShapeDtypeStruct(s, F32) for...]
  transfers between devices with their start and end apart: 12 -> 12, of which waited for: 5 -> 6; matrix products, arithmetic and copies ran while one was open for 1% -> 1% of each run, Pallas kernels for 29% -> 28%
where the time goes in v5:
time: 48.6 us; the launch traced here: 48.5 us
  Pallas kernels  16.7 us (34%)
  waiting for transfers between devices  15.6 us (32%)
  starting transfers between devices  14.9 us (31%)
  between operations  0.83 us (2%)
    pallas_call x5, Pallas kernels, run(): pl.pallas_call(kernel, out_shape=tuple((jax.ShapeDtypeStruct(s, F32) for...  16.7 us
    ppermute x12, waiting for transfers between devices, trade(): lax.ppermute(x, axis, [(i, i ^ k) for i in range(lax.axis_size(axis))])  15.6 us
    ppermute x12, starting transfers between devices, trade(): lax.ppermute(x, axis, [(i, i ^ k) for i in range(lax.axis_size(axis))])  14.9 us
  transfers between devices with their start and end apart: 12, of which 6 were waited for; matrix products, arithmetic and copies ran while one was open for 1% of the time, Pallas kernels for 28%

profile of v5, /device:TPU:0, one launch (start us, length us, event | category | flops | bytes accessed | tf_op | source)
XLA Modules:
  0.0 48.5 jit_solution(11886647486105117866)
XLA Ops:
  0.6 0.1 pad_add_fusion.index_ref
  0.7 1.5 %k0.1 = (f32[264,128]{1,0:T(8,128)S(1)}, f32[264,128]{1,0:T(8,128)S(1)}) custom-call(s32[3]{0:T(128)S(1)} %pad_add_fusion.index_ref, f32[512,128]{1,0:T(8,128)} %bitcast.26), custom_call_target="tpu_custom_call" | custom-call | bytes 1000000 | tf_op jit(solution)/shard_map/k0/pallas_call | solution.py:385
  2.2 3.0 %collective-permute-start = (f32[264,128]{1,0:T(8,128)S(1)}, f32[264,128]{1,0:T(8,128)S(1)}, u32[]{:S(2)}, u32[]{:S(2)}) collective-permute-start(f32[264,128]{1,0:T(8,128)S(1)} %get-tuple-element.34), channel_id=1, source_target_pairs={{0,16},{16,0},{1,17},{17,1},{2,18},{18,2},{3,19},{19,3},{4,20},{20... | collective-permute-start | bytes 405512 | tf_op jit(solution)/shard_map/ppermute | solution.py:348
  5.3 3.6 %collective-permute-done = f32[264,128]{1,0:T(8,128)S(1)} collective-permute-done((f32[264,128]{1,0:T(8,128)S(1)}, f32[264,128]{1,0:T(8,128)S(1)}, u32[]{:S(2)}, u32[]{:S(2)}) %collective-permute-start) | collective-permute-done | bytes 135200 | tf_op jit(solution)/shard_map/ppermute | solution.py:348
  8.8 0.0 copy-start
  8.8 2.9 %collective-permute-start.1 = (f32[264,128]{1,0:T(8,128)S(1)}, f32[264,128]{1,0:T(8,128)S(1)}, u32[]{:S(2)}, u32[]{:S(2)}) collective-permute-start(f32[264,128]{1,0:T(8,128)S(1)} %add.18), channel_id=1, source_target_pairs={{0,2},{1,3},{2,0},{3,1},{4,6},{5,7},{6,4},{7,5},{8,10},{9,11},{10,... | collective-permute-start | bytes 405512 | tf_op jit(solution)/shard_map/ppermute | solution.py:348
  11.8 0.0 copy-done
  11.8 1.6 %collective-permute-start.2 = (f32[256,128]{1,0:T(8,128)S(1)}, f32[256,128]{1,0:T(8,128)S(1)}, u32[]{:S(2)}, u32[]{:S(2)}) collective-permute-start(f32[256,128]{1,0:T(8,128)S(1)} %slice.17.own_ref), channel_id=1, source_target_pairs={{0,8},{4,12},{8,0},{12,4},{1,9},{5,13},{9,1},{13,5},{2,10},{6,14},... | collective-permute-start | bytes 393224 | tf_op jit(solution)/shard_map/ppermute | solution.py:348
  13.4 4.1 %collective-permute-done.1 = f32[264,128]{1,0:T(8,128)S(1)} collective-permute-done((f32[264,128]{1,0:T(8,128)S(1)}, f32[264,128]{1,0:T(8,128)S(1)}, u32[]{:S(2)}, u32[]{:S(2)}) %collective-permute-start.1) | collective-permute-done | bytes 135200 | tf_op jit(solution)/shard_map/ppermute | solution.py:348
  17.5 0.0 collective-permute-done.2
  17.5 0.9 %collective-permute-start.3 = (f32[264,128]{1,0:T(8,128)S(1)}, f32[264,128]{1,0:T(8,128)S(1)}, u32[]{:S(2)}, u32[]{:S(2)}) collective-permute-start(f32[264,128]{1,0:T(8,128)S(1)} %broadcast_select_fusion.4), channel_id=1, source_target_pairs={{0,1},{1,0},{2,3},{3,2},{4,5},{5,4},{6,7},{7,6},{8,9},{9,8},{10,11... | collective-permute-start | bytes 405512 | tf_op jit(solution)/shard_map/ppermute | solution.py:348
  18.4 1.6 %collective-permute-start.10 = (f32[256,128]{1,0:T(8,128)S(1)}, f32[256,128]{1,0:T(8,128)S(1)}, u32[]{:S(2)}, u32[]{:S(2)}) collective-permute-start(f32[256,128]{1,0:T(8,128)S(1)} %broadcast_select_fusion.8), channel_id=1, source_target_pairs={{0,16},{16,0},{1,17},{17,1},{2,18},{18,2},{3,19},{19,3},{4,20},{20... | collective-permute-start | bytes 393224 | tf_op jit(solution)/shard_map/ppermute | solution.py:348
  20.0 2.6 %collective-permute-done.3 = f32[264,128]{1,0:T(8,128)S(1)} collective-permute-done((f32[264,128]{1,0:T(8,128)S(1)}, f32[264,128]{1,0:T(8,128)S(1)}, u32[]{:S(2)}, u32[]{:S(2)}) %collective-permute-start.3) | collective-permute-done | bytes 135200 | tf_op jit(solution)/shard_map/ppermute | solution.py:348
  22.6 1.5 %collective-permute-start.4 = (f32[264,128]{1,0:T(8,128)S(1)}, f32[264,128]{1,0:T(8,128)S(1)}, u32[]{:S(2)}, u32[]{:S(2)}) collective-permute-start(f32[264,128]{1,0:T(8,128)S(1)} %broadcast_select_fusion.5), channel_id=1, source_target_pairs={{0,8},{4,12},{8,0},{12,4},{1,9},{5,13},{9,1},{13,5},{2,10},{6,14},... | collective-permute-start | bytes 405512 | tf_op jit(solution)/shard_map/ppermute | solution.py:348
  24.1 0.6 %collective-permute-start.6 = (f32[256,128]{1,0:T(8,128)S(1)}, f32[256,128]{1,0:T(8,128)S(1)}, u32[]{:S(2)}, u32[]{:S(2)}) collective-permute-start(f32[256,128]{1,0:T(8,128)S(1)} %slice_select_fusion.1), channel_id=1, source_target_pairs={{0,8},{4,12},{8,0},{12,4},{1,9},{5,13},{9,1},{13,5},{2,10},{6,14},... | collective-permute-start | bytes 393224 | tf_op jit(solution)/shard_map/ppermute | solution.py:348
  24.8 2.9 %collective-permute-done.4 = f32[264,128]{1,0:T(8,128)S(1)} collective-permute-done((f32[264,128]{1,0:T(8,128)S(1)}, f32[264,128]{1,0:T(8,128)S(1)}, u32[]{:S(2)}, u32[]{:S(2)}) %collective-permute-start.4) | collective-permute-done | bytes 135200 | tf_op jit(solution)/shard_map/ppermute | solution.py:348
  27.7 0.1 collective-permute-start.5
  27.8 1.4 %collective-permute-done.6 = f32[256,128]{1,0:T(8,128)S(1)} collective-permute-done((f32[256,128]{1,0:T(8,128)S(1)}, f32[256,128]{1,0:T(8,128)S(1)}, u32[]{:S(2)}, u32[]{:S(2)}) %collective-permute-start.6) | collective-permute-done | bytes 131104 | tf_op jit(solution)/shard_map/ppermute | solution.py:348
  29.2 0.0 collective-permute-done.5
  29.2 1.6 %collective-permute-start.8 = (f32[256,128]{1,0:T(8,128)S(1)}, f32[256,128]{1,0:T(8,128)S(1)}, u32[]{:S(2)}, u32[]{:S(2)}) collective-permute-start(f32[256,128]{1,0:T(8,128)S(1)} %slice_select_fusion), channel_id=1, source_target_pairs={{0,16},{16,0},{1,17},{17,1},{2,18},{18,2},{3,19},{19,3},{4,20},{20... | collective-permute-start | bytes 393224 | tf_op jit(solution)/shard_map/ppermute | solution.py:348
  30.8 0.5 %collective-permute-start.7 = (f32[2,256,128]{2,1,0:T(8,128)S(1)}, f32[2,256,128]{2,1,0:T(8,128)S(1)}, u32[]{:S(2)}, u32[]{:S(2)}) collective-permute-start(f32[2,256,128]{2,1,0:T(8,128)S(1)} %pad_maximum_fusion.1), channel_id=1, source_target_pairs={{0,16},{16,0},{1,17},{17,1},{2,18},{18,2},{3,19},{19,3},{4,20},{20... | collective-permute-start | bytes 786440 | tf_op jit(solution)/shard_map/ppermute | solution.py:348
  31.3 3.3 %k1.1 = (f32[128,128]{1,0:T(8,128)S(1)}, f32[128,128]{1,0:T(8,128)S(1)}, f32[128,128]{1,0:T(8,128)S(1)}, f32[128,128]{1,0:T(8,128)S(1)}, f32[128,128]{1,0:T(8,128)S(1)}, /*index=5*/f32[128,128]{1,0:T(8,128)S(1)}) custom-call(f32[264,128]{1,0:T(8,128)S(1)} %broadcast_select_fusion.7.packed_ref), custom_call_target="tpu_custom_call" | custom-call | flops 5000000000 | bytes 1000000 | tf_op jit(solution)/shard_map/k1/pallas_call | solution.py:385
  34.7 1.0 %collective-permute-done.8 = f32[256,128]{1,0:T(8,128)S(1)} collective-permute-done((f32[256,128]{1,0:T(8,128)S(1)}, f32[256,128]{1,0:T(8,128)S(1)}, u32[]{:S(2)}, u32[]{:S(2)}) %collective-permute-start.8) | collective-permute-done | bytes 131104 | tf_op jit(solution)/shard_map/ppermute | solution.py:348
  35.7 0.1 collective-permute-start.9
  35.8 2.8 %k2.1 = (f32[256,256]{1,0:T(8,128)S(1)}, f32[256,256]{1,0:T(8,128)S(1)}) custom-call(f32[128,128]{1,0:T(8,128)S(1)} %get-tuple-element.44.lower0_ref, f32[128,128]{1,0:T(8,128)S(1)} %get-tuple-element.45.inverse0_ref, f32[128,128]{1,0:T(8,128)S(1)} %get-tuple-element.46.left_ref, f32[128,128]{1,0:T(8,128)S(1)} %get-tuple-element.47.rest_ref, ...), custom_call_target="tpu_custom_call" | custom-call | flops 5000000000 | bytes 1000000 | tf_op jit(solution)/shard_map/k2/pallas_call | solution.py:385
  38.5 0.0 collective-permute-done.10
  38.6 0.6 %collective-permute-start.11 = (f32[2,256,128]{2,1,0:T(8,128)S(1)}, f32[2,256,128]{2,1,0:T(8,128)S(1)}, u32[]{:S(2)}, u32[]{:S(2)}) collective-permute-start(f32[2,256,128]{2,1,0:T(8,128)S(1)} %pad_maximum_fusion.3), channel_id=1, source_target_pairs={{0,4},{4,0},{8,12},{12,8},{1,5},{5,1},{9,13},{13,9},{2,6},{6,2},{1... | collective-permute-start | bytes 786440 | tf_op jit(solution)/shard_map/ppermute | solution.py:348
  39.2 0.0 collective-permute-done.9
  39.2 7.3 %k3.1 = (f32[256,256]{1,0:T(8,128)S(1)}, f32[256,256]{1,0:T(8,128)S(1)}, f32[256,256]{1,0:T(8,128)S(1)}, f32[256,256]{1,0:T(8,128)S(1)}) custom-call(f32[2,256,128]{2,1,0:T(8,128)S(1)} %get-tuple-element.73.corners_ref, f32[2,256,128]{2,1,0:T(8,128)S(1)} %get-tuple-element.72.belows_ref, f32[256,256]{1,0:T(8,128)S(1)} %get-tuple-element.50.inverse0_ref), custom_call_target="tpu_custom_call" | custom-call | flops 10000000000 | bytes 1000000 | tf_op jit(solution)/shard_map/k3/pallas_call | solution.py:385
  46.5 0.0 collective-permute-done.11
  46.6 0.0 collective-permute-done.7
  46.7 1.8 %kf.1 = (f32[256,128]{1,0:T(8,128)}, f32[2,256,256]{2,1,0:T(8,128)}) custom-call(s32[3]{0:T(128)S(1)} %pad_add_fusion.index_ref, s32[2,2]{1,0:T(2,128)S(1)} %bitcast.24, f32[256,128]{1,0:T(8,128)S(1)} %slice.17.own_ref, f32[264,128]{1,0:T(8,128)S(1)} %broadcast_select_fusion.7.packed_ref, f32[2,2,256,128]{3,2,1,0:T(8,128)S(1)} %pad_maximum_fusion.rows_ref, ...), custom_call_target="tpu_custom_call" | custom-call | flops 1000000000 | bytes 1000000 | tf_op jit(solution)/shard_map/kf/pallas_call | solution.py:385
  (20 shorter events, 0.4 us)
Async XLA Ops:
  2.2 6.6 %collective-permute-start = (f32[264,128]{1,0:T(8,128)S(1)}, f32[264,128]{1,0:T(8,128)S(1)}, u32[]{:S(2)}, u32[]{:S(2)}) collective-permute-start(f32[264,128]{1,0:T(8,128)S(1)} %get-tuple-element.34), channel_id=1, source_target_pairs={{0,16},{16,0},{1,17},{17,1},{2,18},{18,2},{3,19},{19,3},{4,20},{20... | collective-permute-start | bytes 405512 | tf_op jit(solution)/shard_map/ppermute | solution.py:348
  8.8 2.9 %copy-start = (s32[1,1,2,1,1,2]{5,4,3,2,1,0:T(1,128)S(1)}, s32[1,1,2,1,1,2]{5,4,3,2,1,0:T(1,128)}, u32[]{:S(2)}) copy-start(s32[1,1,2,1,1,2]{5,4,3,2,1,0:T(1,128)} %param.3) | copy-start | bytes 52
  8.8 8.6 %collective-permute-start.1 = (f32[264,128]{1,0:T(8,128)S(1)}, f32[264,128]{1,0:T(8,128)S(1)}, u32[]{:S(2)}, u32[]{:S(2)}) collective-permute-start(f32[264,128]{1,0:T(8,128)S(1)} %add.18), channel_id=1, source_target_pairs={{0,2},{1,3},{2,0},{3,1},{4,6},{5,7},{6,4},{7,5},{8,10},{9,11},{10,... | collective-permute-start | bytes 405512 | tf_op jit(solution)/shard_map/ppermute | solution.py:348
  11.8 5.7 %collective-permute-start.2 = (f32[256,128]{1,0:T(8,128)S(1)}, f32[256,128]{1,0:T(8,128)S(1)}, u32[]{:S(2)}, u32[]{:S(2)}) collective-permute-start(f32[256,128]{1,0:T(8,128)S(1)} %slice.17.own_ref), channel_id=1, source_target_pairs={{0,8},{4,12},{8,0},{12,4},{1,9},{5,13},{9,1},{13,5},{2,10},{6,14},... | collective-permute-start | bytes 393224 | tf_op jit(solution)/shard_map/ppermute | solution.py:348
  17.5 5.1 %collective-permute-start.3 = (f32[264,128]{1,0:T(8,128)S(1)}, f32[264,128]{1,0:T(8,128)S(1)}, u32[]{:S(2)}, u32[]{:S(2)}) collective-permute-start(f32[264,128]{1,0:T(8,128)S(1)} %broadcast_select_fusion.4), channel_id=1, source_target_pairs={{0,1},{1,0},{2,3},{3,2},{4,5},{5,4},{6,7},{7,6},{8,9},{9,8},{10,11... | collective-permute-start | bytes 405512 | tf_op jit(solution)/shard_map/ppermute | solution.py:348
  18.4 20.1 %collective-permute-start.10 = (f32[256,128]{1,0:T(8,128)S(1)}, f32[256,128]{1,0:T(8,128)S(1)}, u32[]{:S(2)}, u32[]{:S(2)}) collective-permute-start(f32[256,128]{1,0:T(8,128)S(1)} %broadcast_select_fusion.8), channel_id=1, source_target_pairs={{0,16},{16,0},{1,17},{17,1},{2,18},{18,2},{3,19},{19,3},{4,20},{20... | collective-permute-start | bytes 393224 | tf_op jit(solution)/shard_map/ppermute | solution.py:348
  22.6 5.1 %collective-permute-start.4 = (f32[264,128]{1,0:T(8,128)S(1)}, f32[264,128]{1,0:T(8,128)S(1)}, u32[]{:S(2)}, u32[]{:S(2)}) collective-permute-start(f32[264,128]{1,0:T(8,128)S(1)} %broadcast_select_fusion.5), channel_id=1, source_target_pairs={{0,8},{4,12},{8,0},{12,4},{1,9},{5,13},{9,1},{13,5},{2,10},{6,14},... | collective-permute-start | bytes 405512 | tf_op jit(solution)/shard_map/ppermute | solution.py:348
  24.1 5.0 %collective-permute-start.6 = (f32[256,128]{1,0:T(8,128)S(1)}, f32[256,128]{1,0:T(8,128)S(1)}, u32[]{:S(2)}, u32[]{:S(2)}) collective-permute-start(f32[256,128]{1,0:T(8,128)S(1)} %slice_select_fusion.1), channel_id=1, source_target_pairs={{0,8},{4,12},{8,0},{12,4},{1,9},{5,13},{9,1},{13,5},{2,10},{6,14},... | collective-permute-start | bytes 393224 | tf_op jit(solution)/shard_map/ppermute | solution.py:348
  27.7 1.5 %collective-permute-start.5 = (f32[264,128]{1,0:T(8,128)S(1)}, f32[264,128]{1,0:T(8,128)S(1)}, u32[]{:S(2)}, u32[]{:S(2)}) collective-permute-start(f32[264,128]{1,0:T(8,128)S(1)} %broadcast_select_fusion.6), channel_id=1, source_target_pairs={{0,4},{4,0},{8,12},{12,8},{1,5},{5,1},{9,13},{13,9},{2,6},{6,2},{1... | collective-permute-start | bytes 405512 | tf_op jit(solution)/shard_map/ppermute | solution.py:348
  29.2 6.4 %collective-permute-start.8 = (f32[256,128]{1,0:T(8,128)S(1)}, f32[256,128]{1,0:T(8,128)S(1)}, u32[]{:S(2)}, u32[]{:S(2)}) collective-permute-start(f32[256,128]{1,0:T(8,128)S(1)} %slice_select_fusion), channel_id=1, source_target_pairs={{0,16},{16,0},{1,17},{17,1},{2,18},{18,2},{3,19},{19,3},{4,20},{20... | collective-permute-start | bytes 393224 | tf_op jit(solution)/shard_map/ppermute | solution.py:348
  30.8 15.8 %collective-permute-start.7 = (f32[2,256,128]{2,1,0:T(8,128)S(1)}, f32[2,256,128]{2,1,0:T(8,128)S(1)}, u32[]{:S(2)}, u32[]{:S(2)}) collective-permute-start(f32[2,256,128]{2,1,0:T(8,128)S(1)} %pad_maximum_fusion.1), channel_id=1, source_target_pairs={{0,16},{16,0},{1,17},{17,1},{2,18},{18,2},{3,19},{19,3},{4,20},{20... | collective-permute-start | bytes 786440 | tf_op jit(solution)/shard_map/ppermute | solution.py:348
  35.7 3.5 %collective-permute-start.9 = (f32[2,256,128]{2,1,0:T(8,128)S(1)}, f32[2,256,128]{2,1,0:T(8,128)S(1)}, u32[]{:S(2)}, u32[]{:S(2)}) collective-permute-start(f32[2,256,128]{2,1,0:T(8,128)S(1)} %pad_maximum_fusion.2), channel_id=1, source_target_pairs={{0,4},{4,0},{8,12},{12,8},{1,5},{5,1},{9,13},{13,9},{2,6},{6,2},{1... | collective-permute-start | bytes 786440 | tf_op jit(solution)/shard_map/ppermute | solution.py:348
  38.6 7.9 %collective-permute-start.11 = (f32[2,256,128]{2,1,0:T(8,128)S(1)}, f32[2,256,128]{2,1,0:T(8,128)S(1)}, u32[]{:S(2)}, u32[]{:S(2)}) collective-permute-start(f32[2,256,128]{2,1,0:T(8,128)S(1)} %pad_maximum_fusion.3), channel_id=1, source_target_pairs={{0,4},{4,0},{8,12},{12,8},{1,5},{5,1},{9,13},{13,9},{2,6},{6,2},{1... | collective-permute-start | bytes 786440 | tf_op jit(solution)/shard_map/ppermute | solution.py:348

commit v6 on v5

--- a/solution.py
+++ b/solution.py
@@ -452,7 +452,6 @@
     got = trade(low, "row", 1)
     packed = jnp.where(even_row, low, got)
     lead_parts = ask_layers(jnp.where(even_row, got[:piece_rows], high))
-    rows_in = ask_layers(after(panels_in, lead_parts[0]))
     packed = after(packed, high)
 
     small_lower, small_inverse, left0, rest0, *scales0 = run(
@@ -463,6 +462,7 @@
         flops=5 * 10**9,
         name="k1",
     )
+    rows_in = ask_layers(after(panels_in, rest0))
     lead = in_order(lead_parts, rest0)
     lead_other = trade(lead, "row", 1)
     lower0, inverse0 = run(

time: 48.6 us -> 47.8 us (0.984)
  waiting for transfers between devices: 15.6 us -> 14.6 us
    ppermute x12, waiting for transfers between devices: 15.6 us -> 14.6 us  [trade(): lax.ppermute(x, axis, [(i, i ^ k) for i in range(lax.axis_size(axis))])]
  transfers between devices with their start and end apart: 12 -> 12, of which waited for: 6 -> 5; matrix products, arithmetic and copies ran while one was open for 1% -> 1% of each run, Pallas kernels for 28% -> 28%
where the time goes in v6:
time: 47.8 us; the launch traced here: 47.6 us
  Pallas kernels  16.7 us (35%)
  starting transfers between devices  14.9 us (31%)
  waiting for transfers between devices  14.6 us (31%)
  between operations  0.83 us (2%)
    pallas_call x5, Pallas kernels, run(): pl.pallas_call(kernel, out_shape=tuple((jax.ShapeDtypeStruct(s, F32) for...  16.7 us
    ppermute x12, starting transfers between devices, trade(): lax.ppermute(x, axis, [(i, i ^ k) for i in range(lax.axis_size(axis))])  14.9 us
    ppermute x12, waiting for transfers between devices, trade(): lax.ppermute(x, axis, [(i, i ^ k) for i in range(lax.axis_size(axis))])  14.6 us
  transfers between devices with their start and end apart: 12, of which 5 were waited for; matrix products, arithmetic and copies ran while one was open for 1% of the time, Pallas kernels for 28%

profile of v6, /device:TPU:0, one launch (start us, length us, event | category | flops | bytes accessed | tf_op | source)
XLA Modules:
  0.0 47.6 jit_solution(16007068502608231044)
XLA Ops:
  0.6 0.1 pad_add_fusion.index_ref
  0.7 1.5 %k0.1 = (f32[264,128]{1,0:T(8,128)S(1)}, f32[264,128]{1,0:T(8,128)S(1)}) custom-call(s32[3]{0:T(128)S(1)} %pad_add_fusion.index_ref, f32[512,128]{1,0:T(8,128)} %bitcast.26), custom_call_target="tpu_custom_call" | custom-call | bytes 1000000 | tf_op jit(solution)/shard_map/k0/pallas_call | solution.py:385
  2.2 3.0 %collective-permute-start = (f32[264,128]{1,0:T(8,128)S(1)}, f32[264,128]{1,0:T(8,128)S(1)}, u32[]{:S(2)}, u32[]{:S(2)}) collective-permute-start(f32[264,128]{1,0:T(8,128)S(1)} %get-tuple-element.34), channel_id=1, source_target_pairs={{0,16},{16,0},{1,17},{17,1},{2,18},{18,2},{3,19},{19,3},{4,20},{20... | collective-permute-start | bytes 405512 | tf_op jit(solution)/shard_map/ppermute | solution.py:348
  5.3 3.6 %collective-permute-done = f32[264,128]{1,0:T(8,128)S(1)} collective-permute-done((f32[264,128]{1,0:T(8,128)S(1)}, f32[264,128]{1,0:T(8,128)S(1)}, u32[]{:S(2)}, u32[]{:S(2)}) %collective-permute-start) | collective-permute-done | bytes 135200 | tf_op jit(solution)/shard_map/ppermute | solution.py:348
  8.8 0.0 copy-start
  8.8 2.9 %collective-permute-start.1 = (f32[264,128]{1,0:T(8,128)S(1)}, f32[264,128]{1,0:T(8,128)S(1)}, u32[]{:S(2)}, u32[]{:S(2)}) collective-permute-start(f32[264,128]{1,0:T(8,128)S(1)} %add.18), channel_id=1, source_target_pairs={{0,2},{1,3},{2,0},{3,1},{4,6},{5,7},{6,4},{7,5},{8,10},{9,11},{10,... | collective-permute-start | bytes 405512 | tf_op jit(solution)/shard_map/ppermute | solution.py:348
  11.8 0.0 copy-done
  11.8 1.6 %collective-permute-start.2 = (f32[256,128]{1,0:T(8,128)S(1)}, f32[256,128]{1,0:T(8,128)S(1)}, u32[]{:S(2)}, u32[]{:S(2)}) collective-permute-start(f32[256,128]{1,0:T(8,128)S(1)} %slice.17.own_ref), channel_id=1, source_target_pairs={{0,8},{4,12},{8,0},{12,4},{1,9},{5,13},{9,1},{13,5},{2,10},{6,14},... | collective-permute-start | bytes 393224 | tf_op jit(solution)/shard_map/ppermute | solution.py:348
  13.4 4.1 %collective-permute-done.1 = f32[264,128]{1,0:T(8,128)S(1)} collective-permute-done((f32[264,128]{1,0:T(8,128)S(1)}, f32[264,128]{1,0:T(8,128)S(1)}, u32[]{:S(2)}, u32[]{:S(2)}) %collective-permute-start.1) | collective-permute-done | bytes 135200 | tf_op jit(solution)/shard_map/ppermute | solution.py:348
  17.5 0.0 collective-permute-done.2
  17.5 0.9 %collective-permute-start.3 = (f32[264,128]{1,0:T(8,128)S(1)}, f32[264,128]{1,0:T(8,128)S(1)}, u32[]{:S(2)}, u32[]{:S(2)}) collective-permute-start(f32[264,128]{1,0:T(8,128)S(1)} %broadcast_select_fusion.4), channel_id=1, source_target_pairs={{0,1},{1,0},{2,3},{3,2},{4,5},{5,4},{6,7},{7,6},{8,9},{9,8},{10,11... | collective-permute-start | bytes 405512 | tf_op jit(solution)/shard_map/ppermute | solution.py:348
  18.4 1.6 %collective-permute-start.10 = (f32[256,128]{1,0:T(8,128)S(1)}, f32[256,128]{1,0:T(8,128)S(1)}, u32[]{:S(2)}, u32[]{:S(2)}) collective-permute-start(f32[256,128]{1,0:T(8,128)S(1)} %broadcast_select_fusion.8), channel_id=1, source_target_pairs={{0,16},{16,0},{1,17},{17,1},{2,18},{18,2},{3,19},{19,3},{4,20},{20... | collective-permute-start | bytes 393224 | tf_op jit(solution)/shard_map/ppermute | solution.py:348
  20.0 2.6 %collective-permute-done.3 = f32[264,128]{1,0:T(8,128)S(1)} collective-permute-done((f32[264,128]{1,0:T(8,128)S(1)}, f32[264,128]{1,0:T(8,128)S(1)}, u32[]{:S(2)}, u32[]{:S(2)}) %collective-permute-start.3) | collective-permute-done | bytes 135200 | tf_op jit(solution)/shard_map/ppermute | solution.py:348
  22.6 1.5 %collective-permute-start.4 = (f32[264,128]{1,0:T(8,128)S(1)}, f32[264,128]{1,0:T(8,128)S(1)}, u32[]{:S(2)}, u32[]{:S(2)}) collective-permute-start(f32[264,128]{1,0:T(8,128)S(1)} %broadcast_select_fusion.5), channel_id=1, source_target_pairs={{0,8},{4,12},{8,0},{12,4},{1,9},{5,13},{9,1},{13,5},{2,10},{6,14},... | collective-permute-start | bytes 405512 | tf_op jit(solution)/shard_map/ppermute | solution.py:348
  24.1 0.6 %collective-permute-start.6 = (f32[256,128]{1,0:T(8,128)S(1)}, f32[256,128]{1,0:T(8,128)S(1)}, u32[]{:S(2)}, u32[]{:S(2)}) collective-permute-start(f32[256,128]{1,0:T(8,128)S(1)} %slice_select_fusion.1), channel_id=1, source_target_pairs={{0,8},{4,12},{8,0},{12,4},{1,9},{5,13},{9,1},{13,5},{2,10},{6,14},... | collective-permute-start | bytes 393224 | tf_op jit(solution)/shard_map/ppermute | solution.py:348
  24.8 2.9 %collective-permute-done.4 = f32[264,128]{1,0:T(8,128)S(1)} collective-permute-done((f32[264,128]{1,0:T(8,128)S(1)}, f32[264,128]{1,0:T(8,128)S(1)}, u32[]{:S(2)}, u32[]{:S(2)}) %collective-permute-start.4) | collective-permute-done | bytes 135200 | tf_op jit(solution)/shard_map/ppermute | solution.py:348
  27.7 0.1 collective-permute-start.5
  27.8 1.4 %collective-permute-done.6 = f32[256,128]{1,0:T(8,128)S(1)} collective-permute-done((f32[256,128]{1,0:T(8,128)S(1)}, f32[256,128]{1,0:T(8,128)S(1)}, u32[]{:S(2)}, u32[]{:S(2)}) %collective-permute-start.6) | collective-permute-done | bytes 131104 | tf_op jit(solution)/shard_map/ppermute | solution.py:348
  29.2 0.0 collective-permute-done.5
  29.2 1.6 %collective-permute-start.8 = (f32[256,128]{1,0:T(8,128)S(1)}, f32[256,128]{1,0:T(8,128)S(1)}, u32[]{:S(2)}, u32[]{:S(2)}) collective-permute-start(f32[256,128]{1,0:T(8,128)S(1)} %slice_select_fusion), channel_id=1, source_target_pairs={{0,16},{16,0},{1,17},{17,1},{2,18},{18,2},{3,19},{19,3},{4,20},{20... | collective-permute-start | bytes 393224 | tf_op jit(solution)/shard_map/ppermute | solution.py:348
  30.8 3.3 %k1.1 = (f32[128,128]{1,0:T(8,128)S(1)}, f32[128,128]{1,0:T(8,128)S(1)}, f32[128,128]{1,0:T(8,128)S(1)}, f32[128,128]{1,0:T(8,128)S(1)}, f32[128,128]{1,0:T(8,128)S(1)}, /*index=5*/f32[128,128]{1,0:T(8,128)S(1)}) custom-call(f32[264,128]{1,0:T(8,128)S(1)} %broadcast_select_fusion.7.packed_ref), custom_call_target="tpu_custom_call" | custom-call | flops 5000000000 | bytes 1000000 | tf_op jit(solution)/shard_map/k1/pallas_call | solution.py:385
  34.1 0.6 %collective-permute-start.7 = (f32[2,256,128]{2,1,0:T(8,128)S(1)}, f32[2,256,128]{2,1,0:T(8,128)S(1)}, u32[]{:S(2)}, u32[]{:S(2)}) collective-permute-start(f32[2,256,128]{2,1,0:T(8,128)S(1)} %pad_maximum_fusion.1), channel_id=1, source_target_pairs={{0,16},{16,0},{1,17},{17,1},{2,18},{18,2},{3,19},{19,3},{4,20},{20... | collective-permute-start | bytes 786440 | tf_op jit(solution)/shard_map/ppermute | solution.py:348
  34.7 0.0 collective-permute-done.8
  34.8 0.1 collective-permute-start.9
  34.9 2.8 %k2.1 = (f32[256,256]{1,0:T(8,128)S(1)}, f32[256,256]{1,0:T(8,128)S(1)}) custom-call(f32[128,128]{1,0:T(8,128)S(1)} %get-tuple-element.44.lower0_ref, f32[128,128]{1,0:T(8,128)S(1)} %get-tuple-element.45.inverse0_ref, f32[128,128]{1,0:T(8,128)S(1)} %get-tuple-element.46.left_ref, f32[128,128]{1,0:T(8,128)S(1)} %get-tuple-element.47.rest_ref, ...), custom_call_target="tpu_custom_call" | custom-call | flops 5000000000 | bytes 1000000 | tf_op jit(solution)/shard_map/k2/pallas_call | solution.py:385
  37.7 0.0 collective-permute-done.10
  37.7 0.6 %collective-permute-start.11 = (f32[2,256,128]{2,1,0:T(8,128)S(1)}, f32[2,256,128]{2,1,0:T(8,128)S(1)}, u32[]{:S(2)}, u32[]{:S(2)}) collective-permute-start(f32[2,256,128]{2,1,0:T(8,128)S(1)} %pad_maximum_fusion.3), channel_id=1, source_target_pairs={{0,4},{4,0},{8,12},{12,8},{1,5},{5,1},{9,13},{13,9},{2,6},{6,2},{1... | collective-permute-start | bytes 786440 | tf_op jit(solution)/shard_map/ppermute | solution.py:348
  38.3 0.0 collective-permute-done.9
  38.3 7.3 %k3.1 = (f32[256,256]{1,0:T(8,128)S(1)}, f32[256,256]{1,0:T(8,128)S(1)}, f32[256,256]{1,0:T(8,128)S(1)}, f32[256,256]{1,0:T(8,128)S(1)}) custom-call(f32[2,256,128]{2,1,0:T(8,128)S(1)} %get-tuple-element.73.corners_ref, f32[2,256,128]{2,1,0:T(8,128)S(1)} %get-tuple-element.72.belows_ref, f32[256,256]{1,0:T(8,128)S(1)} %get-tuple-element.50.inverse0_ref), custom_call_target="tpu_custom_call" | custom-call | flops 10000000000 | bytes 1000000 | tf_op jit(solution)/shard_map/k3/pallas_call | solution.py:385
  45.7 0.0 collective-permute-done.11
  45.7 0.0 collective-permute-done.7
  45.8 1.8 %kf.1 = (f32[256,128]{1,0:T(8,128)}, f32[2,256,256]{2,1,0:T(8,128)}) custom-call(s32[3]{0:T(128)S(1)} %pad_add_fusion.index_ref, s32[2,2]{1,0:T(2,128)S(1)} %bitcast.24, f32[256,128]{1,0:T(8,128)S(1)} %slice.17.own_ref, f32[264,128]{1,0:T(8,128)S(1)} %broadcast_select_fusion.7.packed_ref, f32[2,2,256,128]{3,2,1,0:T(8,128)S(1)} %pad_maximum_fusion.rows_ref, ...), custom_call_target="tpu_custom_call" | custom-call | flops 1000000000 | bytes 1000000 | tf_op jit(solution)/shard_map/kf/pallas_call | solution.py:385
  (20 shorter events, 0.4 us)
Async XLA Ops:
  2.2 6.6 %collective-permute-start = (f32[264,128]{1,0:T(8,128)S(1)}, f32[264,128]{1,0:T(8,128)S(1)}, u32[]{:S(2)}, u32[]{:S(2)}) collective-permute-start(f32[264,128]{1,0:T(8,128)S(1)} %get-tuple-element.34), channel_id=1, source_target_pairs={{0,16},{16,0},{1,17},{17,1},{2,18},{18,2},{3,19},{19,3},{4,20},{20... | collective-permute-start | bytes 405512 | tf_op jit(solution)/shard_map/ppermute | solution.py:348
  8.8 2.9 %copy-start = (s32[1,1,2,1,1,2]{5,4,3,2,1,0:T(1,128)S(1)}, s32[1,1,2,1,1,2]{5,4,3,2,1,0:T(1,128)}, u32[]{:S(2)}) copy-start(s32[1,1,2,1,1,2]{5,4,3,2,1,0:T(1,128)} %param.3) | copy-start | bytes 52
  8.8 8.6 %collective-permute-start.1 = (f32[264,128]{1,0:T(8,128)S(1)}, f32[264,128]{1,0:T(8,128)S(1)}, u32[]{:S(2)}, u32[]{:S(2)}) collective-permute-start(f32[264,128]{1,0:T(8,128)S(1)} %add.18), channel_id=1, source_target_pairs={{0,2},{1,3},{2,0},{3,1},{4,6},{5,7},{6,4},{7,5},{8,10},{9,11},{10,... | collective-permute-start | bytes 405512 | tf_op jit(solution)/shard_map/ppermute | solution.py:348
  11.8 5.7 %collective-permute-start.2 = (f32[256,128]{1,0:T(8,128)S(1)}, f32[256,128]{1,0:T(8,128)S(1)}, u32[]{:S(2)}, u32[]{:S(2)}) collective-permute-start(f32[256,128]{1,0:T(8,128)S(1)} %slice.17.own_ref), channel_id=1, source_target_pairs={{0,8},{4,12},{8,0},{12,4},{1,9},{5,13},{9,1},{13,5},{2,10},{6,14},... | collective-permute-start | bytes 393224 | tf_op jit(solution)/shard_map/ppermute | solution.py:348
  17.5 5.1 %collective-permute-start.3 = (f32[264,128]{1,0:T(8,128)S(1)}, f32[264,128]{1,0:T(8,128)S(1)}, u32[]{:S(2)}, u32[]{:S(2)}) collective-permute-start(f32[264,128]{1,0:T(8,128)S(1)} %broadcast_select_fusion.4), channel_id=1, source_target_pairs={{0,1},{1,0},{2,3},{3,2},{4,5},{5,4},{6,7},{7,6},{8,9},{9,8},{10,11... | collective-permute-start | bytes 405512 | tf_op jit(solution)/shard_map/ppermute | solution.py:348
  18.4 19.3 %collective-permute-start.10 = (f32[256,128]{1,0:T(8,128)S(1)}, f32[256,128]{1,0:T(8,128)S(1)}, u32[]{:S(2)}, u32[]{:S(2)}) collective-permute-start(f32[256,128]{1,0:T(8,128)S(1)} %broadcast_select_fusion.8), channel_id=1, source_target_pairs={{0,16},{16,0},{1,17},{17,1},{2,18},{18,2},{3,19},{19,3},{4,20},{20... | collective-permute-start | bytes 393224 | tf_op jit(solution)/shard_map/ppermute | solution.py:348
  22.6 5.1 %collective-permute-start.4 = (f32[264,128]{1,0:T(8,128)S(1)}, f32[264,128]{1,0:T(8,128)S(1)}, u32[]{:S(2)}, u32[]{:S(2)}) collective-permute-start(f32[264,128]{1,0:T(8,128)S(1)} %broadcast_select_fusion.5), channel_id=1, source_target_pairs={{0,8},{4,12},{8,0},{12,4},{1,9},{5,13},{9,1},{13,5},{2,10},{6,14},... | collective-permute-start | bytes 405512 | tf_op jit(solution)/shard_map/ppermute | solution.py:348
  24.1 5.0 %collective-permute-start.6 = (f32[256,128]{1,0:T(8,128)S(1)}, f32[256,128]{1,0:T(8,128)S(1)}, u32[]{:S(2)}, u32[]{:S(2)}) collective-permute-start(f32[256,128]{1,0:T(8,128)S(1)} %slice_select_fusion.1), channel_id=1, source_target_pairs={{0,8},{4,12},{8,0},{12,4},{1,9},{5,13},{9,1},{13,5},{2,10},{6,14},... | collective-permute-start | bytes 393224 | tf_op jit(solution)/shard_map/ppermute | solution.py:348
  27.7 1.5 %collective-permute-start.5 = (f32[264,128]{1,0:T(8,128)S(1)}, f32[264,128]{1,0:T(8,128)S(1)}, u32[]{:S(2)}, u32[]{:S(2)}) collective-permute-start(f32[264,128]{1,0:T(8,128)S(1)} %broadcast_select_fusion.6), channel_id=1, source_target_pairs={{0,4},{4,0},{8,12},{12,8},{1,5},{5,1},{9,13},{13,9},{2,6},{6,2},{1... | collective-permute-start | bytes 405512 | tf_op jit(solution)/shard_map/ppermute | solution.py:348
  29.2 5.5 %collective-permute-start.8 = (f32[256,128]{1,0:T(8,128)S(1)}, f32[256,128]{1,0:T(8,128)S(1)}, u32[]{:S(2)}, u32[]{:S(2)}) collective-permute-start(f32[256,128]{1,0:T(8,128)S(1)} %slice_select_fusion), channel_id=1, source_target_pairs={{0,16},{16,0},{1,17},{17,1},{2,18},{18,2},{3,19},{19,3},{4,20},{20... | collective-permute-start | bytes 393224 | tf_op jit(solution)/shard_map/ppermute | solution.py:348
  34.1 11.6 %collective-permute-start.7 = (f32[2,256,128]{2,1,0:T(8,128)S(1)}, f32[2,256,128]{2,1,0:T(8,128)S(1)}, u32[]{:S(2)}, u32[]{:S(2)}) collective-permute-start(f32[2,256,128]{2,1,0:T(8,128)S(1)} %pad_maximum_fusion.1), channel_id=1, source_target_pairs={{0,16},{16,0},{1,17},{17,1},{2,18},{18,2},{3,19},{19,3},{4,20},{20... | collective-permute-start | bytes 786440 | tf_op jit(solution)/shard_map/ppermute | solution.py:348
  34.8 3.5 %collective-permute-start.9 = (f32[2,256,128]{2,1,0:T(8,128)S(1)}, f32[2,256,128]{2,1,0:T(8,128)S(1)}, u32[]{:S(2)}, u32[]{:S(2)}) collective-permute-start(f32[2,256,128]{2,1,0:T(8,128)S(1)} %pad_maximum_fusion.2), channel_id=1, source_target_pairs={{0,4},{4,0},{8,12},{12,8},{1,5},{5,1},{9,13},{13,9},{2,6},{6,2},{1... | collective-permute-start | bytes 786440 | tf_op jit(solution)/shard_map/ppermute | solution.py:348
  37.7 7.9 %collective-permute-start.11 = (f32[2,256,128]{2,1,0:T(8,128)S(1)}, f32[2,256,128]{2,1,0:T(8,128)S(1)}, u32[]{:S(2)}, u32[]{:S(2)}) collective-permute-start(f32[2,256,128]{2,1,0:T(8,128)S(1)} %pad_maximum_fusion.3), channel_id=1, source_target_pairs={{0,4},{4,0},{8,12},{12,8},{1,5},{5,1},{9,13},{13,9},{2,6},{6,2},{1... | collective-permute-start | bytes 786440 | tf_op jit(solution)/shard_map/ppermute | solution.py:348

commit v7 on v6

--- a/solution.py
+++ b/solution.py
@@ -17,6 +17,13 @@
     return lax.dot_general(
         a, b, dims, precision=lax.Precision.HIGHEST, preferred_element_type=F32
     )
+
+
+AXES = ("layer", "row", "col")
+
+
+def position():
+    return tuple(lax.axis_index(a).astype(jnp.int32) for a in AXES)
 
 
 def split(x):
@@ -82,8 +89,12 @@
             if not last:
                 s0, s1 = side[j], side[j + 1]
                 v0, v1 = s * s0 - q * s1, p * s1 - q * s0
+                final = j + 2 == SUB
+                if not final:
+                    v0, v1 = v0 * r, v1 * r
                 for k in range(SUB):
-                    ahead[k] = ahead[k] - (s0 * row_splat(v0, k) + s1 * row_splat(v1, k)) * r
+                    step = s0 * row_splat(v0, k) + s1 * row_splat(v1, k)
+                    ahead[k] = ahead[k] - (step * r if final else step)
                 near = near - (s0 * w0 + s1 * w1)
             y = y - (m0 * w0 + m1 * w1)
             root0 = lax.rsqrt(p)
@@ -154,12 +165,12 @@
         to_ref[at, at] = jnp.where(same, held.T, held)
 
 
-def pack_kernel(index_ref, source_ref, mine_ref, *refs):
+def pack_kernel(source_ref, mine_ref, *refs):
     *send_refs, linear_ref, arrived = refs
     load = pltpu.make_async_copy(source_ref, linear_ref, arrived)
     load.start()
-    layer = index_ref[0]
-    first = (index_ref[1] == 0) & (index_ref[2] == 0)
+    layer, row, col = position()
+    first = (row == 0) & (col == 0)
     height, tile = mine_ref.shape
     load.wait()
     piece = linear_ref.shape[0] // (len(send_refs) + 1)
@@ -273,11 +284,11 @@
 
 
 def final_kernel(
-    index_ref, keep_ref, own_ref, packed_ref, rows_ref, col0_ref, col1_ref,
+    keep_ref, own_ref, packed_ref, rows_ref, col0_ref, col1_ref,
     lower0_ref, inverse0_ref, lower1_ref, inverse1_ref, left_ref, cross_ref,
     schur_ref, panels_ref, upper_ref, row_ref,
 ):
-    layer, row, col = index_ref[0], index_ref[1], index_ref[2]
+    layer, row, col = position()
     width = upper_ref.shape[1]
     tiles_per = keep_ref.shape[0]
     tile = width // tiles_per
@@ -339,9 +350,6 @@
         at = slice(j * tile, (j + 1) * tile)
         own = jnp.where((row == 0) & (col == 0), row_ref[0, slab, at], own)
         schur_ref[pl.ds(j, slab_rows, tiles_per), :] = own - jnp.where(keep > 0, product[:, at], 0.0)
-
-
-AXES = ("layer", "row", "col")
 
 
 def trade(x, axis, k):
@@ -396,7 +404,7 @@
 
 def on_device(partials, pattern):
     layers, rows, cols = (lax.axis_size(a) for a in AXES)
-    layer, row, col = (lax.axis_index(a).astype(jnp.int32) for a in AXES)
+    layer, row, col = position()
     width = partials.shape[3]
     tiles_per = pattern.shape[2]
     tile = width // tiles_per
@@ -404,16 +412,14 @@
     piece_rows = slab_rows * tiles_per
     height = 2 * tile + SUB
     even_row, even_col = row % 2 == 0, col % 2 == 0
-    index = jnp.stack([layer, row, col])
     square, big = (tile, tile), (width, width)
 
     mine, *sends = run(
         pack_kernel,
         ((height, tile),) * layers,
-        (index, pltpu.with_memory_space_constraint(partials.reshape(width * tiles_per, tile), pltpu.HBM)),
+        (pltpu.with_memory_space_constraint(partials.reshape(width * tiles_per, tile), pltpu.HBM),),
         scratch=((width * tiles_per, tile), pltpu.SemaphoreType.DMA),
         name="k0",
-        smem=1,
         source=pltpu.HBM,
     )
     front = total([mine] + [trade(x, "layer", k + 1) for k, x in enumerate(sends)])
@@ -490,11 +496,11 @@
     schur, panels = run(
         final_kernel,
         ((piece_rows, tile), (2, width, width)),
-        (index, keep, piece, packed, rows_in, col0, col1, lower0, inverse0, lower1, inverse1, left1, cross),
+        (keep, piece, packed, rows_in, col0, col1, lower0, inverse0, lower1, inverse1, left1, cross),
         scratch=((2 * width, width), (2, width, width)),
         flops=10**9,
         name="kf",
-        smem=2,
+        smem=1,
     )
     return (
         schur.reshape(1, 1, 1, slab_rows, 1, 1, width),

time: 47.8 us -> 47.1 us (0.985)
  Pallas kernels: 16.7 us -> 16.2 us
    pallas_call x5, Pallas kernels: 16.7 us -> 16.2 us  [run(): pl.pallas_call(kernel, out_shape=tuple((jax.ShapeDtypeStruct(s, F32) for...]
where the time goes in v7:
time: 47.1 us; the launch traced here: 47 us
  Pallas kernels  16.2 us (34%)
  starting transfers between devices  14.9 us (32%)
  waiting for transfers between devices  14.6 us (31%)
  between operations  0.8 us (2%)
    pallas_call x5, Pallas kernels, run(): pl.pallas_call(kernel, out_shape=tuple((jax.ShapeDtypeStruct(s, F32) for...  16.2 us
    ppermute x12, starting transfers between devices, trade(): lax.ppermute(x, axis, [(i, i ^ k) for i in range(lax.axis_size(axis))])  14.9 us
    ppermute x12, waiting for transfers between devices, trade(): lax.ppermute(x, axis, [(i, i ^ k) for i in range(lax.axis_size(axis))])  14.6 us
  transfers between devices with their start and end apart: 12, of which 5 were waited for; matrix products, arithmetic and copies ran while one was open for 1% of the time, Pallas kernels for 28%

profile of v7, /device:TPU:0, one launch (start us, length us, event | category | flops | bytes accessed | tf_op | source)
XLA Modules:
  0.0 47.0 jit_solution(2036218322994773419)
XLA Ops:
  0.6 1.0 %k0.1 = (f32[264,128]{1,0:T(8,128)S(1)}, f32[264,128]{1,0:T(8,128)S(1)}) custom-call(f32[512,128]{1,0:T(8,128)} %bitcast.23), custom_call_target="tpu_custom_call" | custom-call | bytes 1000000 | tf_op jit(solution)/shard_map/k0/pallas_call | solution.py:393
  1.6 3.0 %collective-permute-start = (f32[264,128]{1,0:T(8,128)S(1)}, f32[264,128]{1,0:T(8,128)S(1)}, u32[]{:S(2)}, u32[]{:S(2)}) collective-permute-start(f32[264,128]{1,0:T(8,128)S(1)} %get-tuple-element.34), channel_id=1, source_target_pairs={{0,16},{16,0},{1,17},{17,1},{2,18},{18,2},{3,19},{19,3},{4,20},{20... | collective-permute-start | bytes 405512 | tf_op jit(solution)/shard_map/ppermute | solution.py:356
  4.6 3.6 %collective-permute-done = f32[264,128]{1,0:T(8,128)S(1)} collective-permute-done((f32[264,128]{1,0:T(8,128)S(1)}, f32[264,128]{1,0:T(8,128)S(1)}, u32[]{:S(2)}, u32[]{:S(2)}) %collective-permute-start) | collective-permute-done | bytes 135200 | tf_op jit(solution)/shard_map/ppermute | solution.py:356
  8.2 0.0 copy-start
  8.2 2.9 %collective-permute-start.1 = (f32[264,128]{1,0:T(8,128)S(1)}, f32[264,128]{1,0:T(8,128)S(1)}, u32[]{:S(2)}, u32[]{:S(2)}) collective-permute-start(f32[264,128]{1,0:T(8,128)S(1)} %add.18), channel_id=1, source_target_pairs={{0,2},{1,3},{2,0},{3,1},{4,6},{5,7},{6,4},{7,5},{8,10},{9,11},{10,... | collective-permute-start | bytes 405512 | tf_op jit(solution)/shard_map/ppermute | solution.py:356
  11.1 0.0 copy-done
  11.2 1.6 %collective-permute-start.2 = (f32[256,128]{1,0:T(8,128)S(1)}, f32[256,128]{1,0:T(8,128)S(1)}, u32[]{:S(2)}, u32[]{:S(2)}) collective-permute-start(f32[256,128]{1,0:T(8,128)S(1)} %slice.17.own_ref), channel_id=1, source_target_pairs={{0,8},{4,12},{8,0},{12,4},{1,9},{5,13},{9,1},{13,5},{2,10},{6,14},... | collective-permute-start | bytes 393224 | tf_op jit(solution)/shard_map/ppermute | solution.py:356
  12.7 4.1 %collective-permute-done.1 = f32[264,128]{1,0:T(8,128)S(1)} collective-permute-done((f32[264,128]{1,0:T(8,128)S(1)}, f32[264,128]{1,0:T(8,128)S(1)}, u32[]{:S(2)}, u32[]{:S(2)}) %collective-permute-start.1) | collective-permute-done | bytes 135200 | tf_op jit(solution)/shard_map/ppermute | solution.py:356
  16.9 0.0 collective-permute-done.2
  16.9 0.9 %collective-permute-start.3 = (f32[264,128]{1,0:T(8,128)S(1)}, f32[264,128]{1,0:T(8,128)S(1)}, u32[]{:S(2)}, u32[]{:S(2)}) collective-permute-start(f32[264,128]{1,0:T(8,128)S(1)} %broadcast_select_fusion.4), channel_id=1, source_target_pairs={{0,1},{1,0},{2,3},{3,2},{4,5},{5,4},{6,7},{7,6},{8,9},{9,8},{10,11... | collective-permute-start | bytes 405512 | tf_op jit(solution)/shard_map/ppermute | solution.py:356
  17.8 1.6 %collective-permute-start.10 = (f32[256,128]{1,0:T(8,128)S(1)}, f32[256,128]{1,0:T(8,128)S(1)}, u32[]{:S(2)}, u32[]{:S(2)}) collective-permute-start(f32[256,128]{1,0:T(8,128)S(1)} %broadcast_select_fusion.8), channel_id=1, source_target_pairs={{0,16},{16,0},{1,17},{17,1},{2,18},{18,2},{3,19},{19,3},{4,20},{20... | collective-permute-start | bytes 393224 | tf_op jit(solution)/shard_map/ppermute | solution.py:356
  19.3 2.6 %collective-permute-done.3 = f32[264,128]{1,0:T(8,128)S(1)} collective-permute-done((f32[264,128]{1,0:T(8,128)S(1)}, f32[264,128]{1,0:T(8,128)S(1)}, u32[]{:S(2)}, u32[]{:S(2)}) %collective-permute-start.3) | collective-permute-done | bytes 135200 | tf_op jit(solution)/shard_map/ppermute | solution.py:356
  22.0 1.5 %collective-permute-start.4 = (f32[264,128]{1,0:T(8,128)S(1)}, f32[264,128]{1,0:T(8,128)S(1)}, u32[]{:S(2)}, u32[]{:S(2)}) collective-permute-start(f32[264,128]{1,0:T(8,128)S(1)} %broadcast_select_fusion.5), channel_id=1, source_target_pairs={{0,8},{4,12},{8,0},{12,4},{1,9},{5,13},{9,1},{13,5},{2,10},{6,14},... | collective-permute-start | bytes 405512 | tf_op jit(solution)/shard_map/ppermute | solution.py:356
  23.5 0.6 %collective-permute-start.6 = (f32[256,128]{1,0:T(8,128)S(1)}, f32[256,128]{1,0:T(8,128)S(1)}, u32[]{:S(2)}, u32[]{:S(2)}) collective-permute-start(f32[256,128]{1,0:T(8,128)S(1)} %slice_select_fusion.1), channel_id=1, source_target_pairs={{0,8},{4,12},{8,0},{12,4},{1,9},{5,13},{9,1},{13,5},{2,10},{6,14},... | collective-permute-start | bytes 393224 | tf_op jit(solution)/shard_map/ppermute | solution.py:356
  24.1 2.9 %collective-permute-done.4 = f32[264,128]{1,0:T(8,128)S(1)} collective-permute-done((f32[264,128]{1,0:T(8,128)S(1)}, f32[264,128]{1,0:T(8,128)S(1)}, u32[]{:S(2)}, u32[]{:S(2)}) %collective-permute-start.4) | collective-permute-done | bytes 135200 | tf_op jit(solution)/shard_map/ppermute | solution.py:356
  27.1 0.1 collective-permute-start.5
  27.2 1.3 %collective-permute-done.6 = f32[256,128]{1,0:T(8,128)S(1)} collective-permute-done((f32[256,128]{1,0:T(8,128)S(1)}, f32[256,128]{1,0:T(8,128)S(1)}, u32[]{:S(2)}, u32[]{:S(2)}) %collective-permute-start.6) | collective-permute-done | bytes 131104 | tf_op jit(solution)/shard_map/ppermute | solution.py:356
  28.6 0.0 collective-permute-done.5
  28.6 1.6 %collective-permute-start.8 = (f32[256,128]{1,0:T(8,128)S(1)}, f32[256,128]{1,0:T(8,128)S(1)}, u32[]{:S(2)}, u32[]{:S(2)}) collective-permute-start(f32[256,128]{1,0:T(8,128)S(1)} %slice_select_fusion), channel_id=1, source_target_pairs={{0,16},{16,0},{1,17},{17,1},{2,18},{18,2},{3,19},{19,3},{4,20},{20... | collective-permute-start | bytes 393224 | tf_op jit(solution)/shard_map/ppermute | solution.py:356
  30.2 3.3 %k1.1 = (f32[128,128]{1,0:T(8,128)S(1)}, f32[128,128]{1,0:T(8,128)S(1)}, f32[128,128]{1,0:T(8,128)S(1)}, f32[128,128]{1,0:T(8,128)S(1)}, f32[128,128]{1,0:T(8,128)S(1)}, /*index=5*/f32[128,128]{1,0:T(8,128)S(1)}) custom-call(f32[264,128]{1,0:T(8,128)S(1)} %broadcast_select_fusion.7.packed_ref), custom_call_target="tpu_custom_call" | custom-call | flops 5000000000 | bytes 1000000 | tf_op jit(solution)/shard_map/k1/pallas_call | solution.py:393
  33.5 0.6 %collective-permute-start.7 = (f32[2,256,128]{2,1,0:T(8,128)S(1)}, f32[2,256,128]{2,1,0:T(8,128)S(1)}, u32[]{:S(2)}, u32[]{:S(2)}) collective-permute-start(f32[2,256,128]{2,1,0:T(8,128)S(1)} %pad_maximum_fusion.1), channel_id=1, source_target_pairs={{0,16},{16,0},{1,17},{17,1},{2,18},{18,2},{3,19},{19,3},{4,20},{20... | collective-permute-start | bytes 786440 | tf_op jit(solution)/shard_map/ppermute | solution.py:356
  34.1 0.0 collective-permute-done.8
  34.2 0.1 collective-permute-start.9
  34.3 2.7 %k2.1 = (f32[256,256]{1,0:T(8,128)S(1)}, f32[256,256]{1,0:T(8,128)S(1)}) custom-call(f32[128,128]{1,0:T(8,128)S(1)} %get-tuple-element.44.lower0_ref, f32[128,128]{1,0:T(8,128)S(1)} %get-tuple-element.45.inverse0_ref, f32[128,128]{1,0:T(8,128)S(1)} %get-tuple-element.46.left_ref, f32[128,128]{1,0:T(8,128)S(1)} %get-tuple-element.47.rest_ref, ...), custom_call_target="tpu_custom_call" | custom-call | flops 5000000000 | bytes 1000000 | tf_op jit(solution)/shard_map/k2/pallas_call | solution.py:393
  37.0 0.0 collective-permute-done.10
  37.1 0.6 %collective-permute-start.11 = (f32[2,256,128]{2,1,0:T(8,128)S(1)}, f32[2,256,128]{2,1,0:T(8,128)S(1)}, u32[]{:S(2)}, u32[]{:S(2)}) collective-permute-start(f32[2,256,128]{2,1,0:T(8,128)S(1)} %pad_maximum_fusion.3), channel_id=1, source_target_pairs={{0,4},{4,0},{8,12},{12,8},{1,5},{5,1},{9,13},{13,9},{2,6},{6,2},{1... | collective-permute-start | bytes 786440 | tf_op jit(solution)/shard_map/ppermute | solution.py:356
  37.7 0.0 collective-permute-done.9
  37.7 7.3 %k3.1 = (f32[256,256]{1,0:T(8,128)S(1)}, f32[256,256]{1,0:T(8,128)S(1)}, f32[256,256]{1,0:T(8,128)S(1)}, f32[256,256]{1,0:T(8,128)S(1)}) custom-call(f32[2,256,128]{2,1,0:T(8,128)S(1)} %get-tuple-element.73.corners_ref, f32[2,256,128]{2,1,0:T(8,128)S(1)} %get-tuple-element.72.belows_ref, f32[256,256]{1,0:T(8,128)S(1)} %get-tuple-element.50.inverse0_ref), custom_call_target="tpu_custom_call" | custom-call | flops 10000000000 | bytes 1000000 | tf_op jit(solution)/shard_map/k3/pallas_call | solution.py:393
  45.0 0.0 collective-permute-done.11
  45.1 0.0 collective-permute-done.7
  45.2 1.8 %kf.1 = (f32[256,128]{1,0:T(8,128)}, f32[2,256,256]{2,1,0:T(8,128)}) custom-call(s32[2,2]{1,0:T(2,128)S(1)} %bitcast.21, f32[256,128]{1,0:T(8,128)S(1)} %slice.17.own_ref, f32[264,128]{1,0:T(8,128)S(1)} %broadcast_select_fusion.7.packed_ref, f32[2,2,256,128]{3,2,1,0:T(8,128)S(1)} %pad_maximum_fusion.rows_ref, f32[2,256,128]{2,1,0:T(8,128)S(1)} %get-tuple-element.69.col0_ref, ...), custom_call_target="tpu_custom_call" | custom-call | flops 1000000000 | bytes 1000000 | tf_op jit(solution)/shard_map/kf/pallas_call | solution.py:393
  (20 shorter events, 0.4 us)
Async XLA Ops:
  1.6 6.6 %collective-permute-start = (f32[264,128]{1,0:T(8,128)S(1)}, f32[264,128]{1,0:T(8,128)S(1)}, u32[]{:S(2)}, u32[]{:S(2)}) collective-permute-start(f32[264,128]{1,0:T(8,128)S(1)} %get-tuple-element.34), channel_id=1, source_target_pairs={{0,16},{16,0},{1,17},{17,1},{2,18},{18,2},{3,19},{19,3},{4,20},{20... | collective-permute-start | bytes 405512 | tf_op jit(solution)/shard_map/ppermute | solution.py:356
  8.2 2.9 %copy-start = (s32[1,1,2,1,1,2]{5,4,3,2,1,0:T(1,128)S(1)}, s32[1,1,2,1,1,2]{5,4,3,2,1,0:T(1,128)}, u32[]{:S(2)}) copy-start(s32[1,1,2,1,1,2]{5,4,3,2,1,0:T(1,128)} %param.3) | copy-start | bytes 52
  8.2 8.6 %collective-permute-start.1 = (f32[264,128]{1,0:T(8,128)S(1)}, f32[264,128]{1,0:T(8,128)S(1)}, u32[]{:S(2)}, u32[]{:S(2)}) collective-permute-start(f32[264,128]{1,0:T(8,128)S(1)} %add.18), channel_id=1, source_target_pairs={{0,2},{1,3},{2,0},{3,1},{4,6},{5,7},{6,4},{7,5},{8,10},{9,11},{10,... | collective-permute-start | bytes 405512 | tf_op jit(solution)/shard_map/ppermute | solution.py:356
  11.2 5.7 %collective-permute-start.2 = (f32[256,128]{1,0:T(8,128)S(1)}, f32[256,128]{1,0:T(8,128)S(1)}, u32[]{:S(2)}, u32[]{:S(2)}) collective-permute-start(f32[256,128]{1,0:T(8,128)S(1)} %slice.17.own_ref), channel_id=1, source_target_pairs={{0,8},{4,12},{8,0},{12,4},{1,9},{5,13},{9,1},{13,5},{2,10},{6,14},... | collective-permute-start | bytes 393224 | tf_op jit(solution)/shard_map/ppermute | solution.py:356
  16.9 5.1 %collective-permute-start.3 = (f32[264,128]{1,0:T(8,128)S(1)}, f32[264,128]{1,0:T(8,128)S(1)}, u32[]{:S(2)}, u32[]{:S(2)}) collective-permute-start(f32[264,128]{1,0:T(8,128)S(1)} %broadcast_select_fusion.4), channel_id=1, source_target_pairs={{0,1},{1,0},{2,3},{3,2},{4,5},{5,4},{6,7},{7,6},{8,9},{9,8},{10,11... | collective-permute-start | bytes 405512 | tf_op jit(solution)/shard_map/ppermute | solution.py:356
  17.8 19.3 %collective-permute-start.10 = (f32[256,128]{1,0:T(8,128)S(1)}, f32[256,128]{1,0:T(8,128)S(1)}, u32[]{:S(2)}, u32[]{:S(2)}) collective-permute-start(f32[256,128]{1,0:T(8,128)S(1)} %broadcast_select_fusion.8), channel_id=1, source_target_pairs={{0,16},{16,0},{1,17},{17,1},{2,18},{18,2},{3,19},{19,3},{4,20},{20... | collective-permute-start | bytes 393224 | tf_op jit(solution)/shard_map/ppermute | solution.py:356
  22.0 5.1 %collective-permute-start.4 = (f32[264,128]{1,0:T(8,128)S(1)}, f32[264,128]{1,0:T(8,128)S(1)}, u32[]{:S(2)}, u32[]{:S(2)}) collective-permute-start(f32[264,128]{1,0:T(8,128)S(1)} %broadcast_select_fusion.5), channel_id=1, source_target_pairs={{0,8},{4,12},{8,0},{12,4},{1,9},{5,13},{9,1},{13,5},{2,10},{6,14},... | collective-permute-start | bytes 405512 | tf_op jit(solution)/shard_map/ppermute | solution.py:356
  23.5 5.0 %collective-permute-start.6 = (f32[256,128]{1,0:T(8,128)S(1)}, f32[256,128]{1,0:T(8,128)S(1)}, u32[]{:S(2)}, u32[]{:S(2)}) collective-permute-start(f32[256,128]{1,0:T(8,128)S(1)} %slice_select_fusion.1), channel_id=1, source_target_pairs={{0,8},{4,12},{8,0},{12,4},{1,9},{5,13},{9,1},{13,5},{2,10},{6,14},... | collective-permute-start | bytes 393224 | tf_op jit(solution)/shard_map/ppermute | solution.py:356
  27.1 1.5 %collective-permute-start.5 = (f32[264,128]{1,0:T(8,128)S(1)}, f32[264,128]{1,0:T(8,128)S(1)}, u32[]{:S(2)}, u32[]{:S(2)}) collective-permute-start(f32[264,128]{1,0:T(8,128)S(1)} %broadcast_select_fusion.6), channel_id=1, source_target_pairs={{0,4},{4,0},{8,12},{12,8},{1,5},{5,1},{9,13},{13,9},{2,6},{6,2},{1... | collective-permute-start | bytes 405512 | tf_op jit(solution)/shard_map/ppermute | solution.py:356
  28.6 5.5 %collective-permute-start.8 = (f32[256,128]{1,0:T(8,128)S(1)}, f32[256,128]{1,0:T(8,128)S(1)}, u32[]{:S(2)}, u32[]{:S(2)}) collective-permute-start(f32[256,128]{1,0:T(8,128)S(1)} %slice_select_fusion), channel_id=1, source_target_pairs={{0,16},{16,0},{1,17},{17,1},{2,18},{18,2},{3,19},{19,3},{4,20},{20... | collective-permute-start | bytes 393224 | tf_op jit(solution)/shard_map/ppermute | solution.py:356
  33.5 11.6 %collective-permute-start.7 = (f32[2,256,128]{2,1,0:T(8,128)S(1)}, f32[2,256,128]{2,1,0:T(8,128)S(1)}, u32[]{:S(2)}, u32[]{:S(2)}) collective-permute-start(f32[2,256,128]{2,1,0:T(8,128)S(1)} %pad_maximum_fusion.1), channel_id=1, source_target_pairs={{0,16},{16,0},{1,17},{17,1},{2,18},{18,2},{3,19},{19,3},{4,20},{20... | collective-permute-start | bytes 786440 | tf_op jit(solution)/shard_map/ppermute | solution.py:356
  34.2 3.5 %collective-permute-start.9 = (f32[2,256,128]{2,1,0:T(8,128)S(1)}, f32[2,256,128]{2,1,0:T(8,128)S(1)}, u32[]{:S(2)}, u32[]{:S(2)}) collective-permute-start(f32[2,256,128]{2,1,0:T(8,128)S(1)} %pad_maximum_fusion.2), channel_id=1, source_target_pairs={{0,4},{4,0},{8,12},{12,8},{1,5},{5,1},{9,13},{13,9},{2,6},{6,2},{1... | collective-permute-start | bytes 786440 | tf_op jit(solution)/shard_map/ppermute | solution.py:356
  37.1 7.9 %collective-permute-start.11 = (f32[2,256,128]{2,1,0:T(8,128)S(1)}, f32[2,256,128]{2,1,0:T(8,128)S(1)}, u32[]{:S(2)}, u32[]{:S(2)}) collective-permute-start(f32[2,256,128]{2,1,0:T(8,128)S(1)} %pad_maximum_fusion.3), channel_id=1, source_target_pairs={{0,4},{4,0},{8,12},{12,8},{1,5},{5,1},{9,13},{13,9},{2,6},{6,2},{1... | collective-permute-start | bytes 786440 | tf_op jit(solution)/shard_map/ppermute | solution.py:356

commit v8 on v7

--- a/solution.py
+++ b/solution.py
@@ -345,7 +345,7 @@
     for j in range(tiles_per):
         keep = jnp.zeros((slab_rows, tile), jnp.int32)
         for i in range(tiles_per):
-            keep = jnp.where(at_row == i, keep_ref[i, j], keep)
+            keep = jnp.where(at_row == i, jnp.broadcast_to(keep_ref[i : i + 1, j : j + 1], keep.shape), keep)
         own = own_ref[pl.ds(j, slab_rows, tiles_per), :]
         at = slice(j * tile, (j + 1) * tile)
         own = jnp.where((row == 0) & (col == 0), row_ref[0, slab, at], own)
@@ -387,13 +387,12 @@
     return lax.optimization_barrier((x,) + others)[0]
 
 
-def run(kernel, outs, ins, scratch=(), flops=0, name=None, smem=0, source=pltpu.VMEM):
+def run(kernel, outs, ins, scratch=(), flops=0, name=None, source=pltpu.VMEM):
     vmem = pl.BlockSpec(memory_space=pltpu.VMEM)
-    ins_at = [pl.BlockSpec(memory_space=pltpu.SMEM)] * smem + [pl.BlockSpec(memory_space=source)] * (len(ins) - smem)
     return pl.pallas_call(
         kernel,
         out_shape=tuple(jax.ShapeDtypeStruct(s, F32) for s in outs),
-        in_specs=ins_at,
+        in_specs=[pl.BlockSpec(memory_space=source)] * len(ins),
         out_specs=tuple(vmem for _ in outs),
         scratch_shapes=[pltpu.VMEM(s, F32) if isinstance(s, tuple) else s for s in scratch],
         compiler_params=pltpu.CompilerParams(vmem_limit_bytes=24 * 1024 * 1024),
@@ -500,7 +499,6 @@
         scratch=((2 * width, width), (2, width, width)),
         flops=10**9,
         name="kf",
-        smem=1,
     )
     return (
         schur.reshape(1, 1, 1, slab_rows, 1, 1, width),

time: 47.1 us -> 46.6 us (0.989)
  Pallas kernels: 16.2 us -> 15.6 us
    pallas_call x5, Pallas kernels: 16.2 us -> 15.6 us  [run(): pl.pallas_call(kernel, out_shape=tuple((jax.ShapeDtypeStruct(s, F32) for...]
  transfers between devices with their start and end apart: 12 -> 12, of which waited for: 5 -> 5; matrix products, arithmetic and copies ran while one was open for 1% -> 1% of each run, Pallas kernels for 28% -> 29%
where the time goes in v8:
time: 46.6 us; the launch traced here: 46.4 us
  Pallas kernels  15.6 us (33%)
  starting transfers between devices  14.9 us (32%)
  waiting for transfers between devices  14.6 us (31%)
  between operations  0.8 us (2%)
    pallas_call x5, Pallas kernels, run(): pl.pallas_call(kernel, out_shape=tuple((jax.ShapeDtypeStruct(s, F32) for...  15.6 us
    ppermute x12, starting transfers between devices, trade(): lax.ppermute(x, axis, [(i, i ^ k) for i in range(lax.axis_size(axis))])  14.9 us
    ppermute x12, waiting for transfers between devices, trade(): lax.ppermute(x, axis, [(i, i ^ k) for i in range(lax.axis_size(axis))])  14.6 us
  transfers between devices with their start and end apart: 12, of which 5 were waited for; matrix products, arithmetic and copies ran while one was open for 1% of the time, Pallas kernels for 29%

profile of v8, /device:TPU:0, one launch (start us, length us, event | category | flops | bytes accessed | tf_op | source)
XLA Modules:
  0.0 46.4 jit_solution(8866394767256346352)
XLA Ops:
  0.6 1.0 %k0.1 = (f32[264,128]{1,0:T(8,128)S(1)}, f32[264,128]{1,0:T(8,128)S(1)}) custom-call(f32[512,128]{1,0:T(8,128)} %bitcast.23), custom_call_target="tpu_custom_call" | custom-call | bytes 1000000 | tf_op jit(solution)/shard_map/k0/pallas_call | solution.py:392
  1.6 3.0 %collective-permute-start = (f32[264,128]{1,0:T(8,128)S(1)}, f32[264,128]{1,0:T(8,128)S(1)}, u32[]{:S(2)}, u32[]{:S(2)}) collective-permute-start(f32[264,128]{1,0:T(8,128)S(1)} %get-tuple-element.34), channel_id=1, source_target_pairs={{0,16},{16,0},{1,17},{17,1},{2,18},{18,2},{3,19},{19,3},{4,20},{20... | collective-permute-start | bytes 405512 | tf_op jit(solution)/shard_map/ppermute | solution.py:356
  4.6 3.6 %collective-permute-done = f32[264,128]{1,0:T(8,128)S(1)} collective-permute-done((f32[264,128]{1,0:T(8,128)S(1)}, f32[264,128]{1,0:T(8,128)S(1)}, u32[]{:S(2)}, u32[]{:S(2)}) %collective-permute-start) | collective-permute-done | bytes 135200 | tf_op jit(solution)/shard_map/ppermute | solution.py:356
  8.2 0.0 copy-start
  8.2 2.9 %collective-permute-start.1 = (f32[264,128]{1,0:T(8,128)S(1)}, f32[264,128]{1,0:T(8,128)S(1)}, u32[]{:S(2)}, u32[]{:S(2)}) collective-permute-start(f32[264,128]{1,0:T(8,128)S(1)} %add.18), channel_id=1, source_target_pairs={{0,2},{1,3},{2,0},{3,1},{4,6},{5,7},{6,4},{7,5},{8,10},{9,11},{10,... | collective-permute-start | bytes 405512 | tf_op jit(solution)/shard_map/ppermute | solution.py:356
  11.1 0.0 copy-done
  11.2 1.6 %collective-permute-start.2 = (f32[256,128]{1,0:T(8,128)S(1)}, f32[256,128]{1,0:T(8,128)S(1)}, u32[]{:S(2)}, u32[]{:S(2)}) collective-permute-start(f32[256,128]{1,0:T(8,128)S(1)} %slice.17.own_ref), channel_id=1, source_target_pairs={{0,8},{4,12},{8,0},{12,4},{1,9},{5,13},{9,1},{13,5},{2,10},{6,14},... | collective-permute-start | bytes 393224 | tf_op jit(solution)/shard_map/ppermute | solution.py:356
  12.7 4.1 %collective-permute-done.1 = f32[264,128]{1,0:T(8,128)S(1)} collective-permute-done((f32[264,128]{1,0:T(8,128)S(1)}, f32[264,128]{1,0:T(8,128)S(1)}, u32[]{:S(2)}, u32[]{:S(2)}) %collective-permute-start.1) | collective-permute-done | bytes 135200 | tf_op jit(solution)/shard_map/ppermute | solution.py:356
  16.9 0.0 collective-permute-done.2
  16.9 0.9 %collective-permute-start.3 = (f32[264,128]{1,0:T(8,128)S(1)}, f32[264,128]{1,0:T(8,128)S(1)}, u32[]{:S(2)}, u32[]{:S(2)}) collective-permute-start(f32[264,128]{1,0:T(8,128)S(1)} %broadcast_select_fusion.4), channel_id=1, source_target_pairs={{0,1},{1,0},{2,3},{3,2},{4,5},{5,4},{6,7},{7,6},{8,9},{9,8},{10,11... | collective-permute-start | bytes 405512 | tf_op jit(solution)/shard_map/ppermute | solution.py:356
  17.8 1.6 %collective-permute-start.10 = (f32[256,128]{1,0:T(8,128)S(1)}, f32[256,128]{1,0:T(8,128)S(1)}, u32[]{:S(2)}, u32[]{:S(2)}) collective-permute-start(f32[256,128]{1,0:T(8,128)S(1)} %broadcast_select_fusion.8), channel_id=1, source_target_pairs={{0,16},{16,0},{1,17},{17,1},{2,18},{18,2},{3,19},{19,3},{4,20},{20... | collective-permute-start | bytes 393224 | tf_op jit(solution)/shard_map/ppermute | solution.py:356
  19.3 2.6 %collective-permute-done.3 = f32[264,128]{1,0:T(8,128)S(1)} collective-permute-done((f32[264,128]{1,0:T(8,128)S(1)}, f32[264,128]{1,0:T(8,128)S(1)}, u32[]{:S(2)}, u32[]{:S(2)}) %collective-permute-start.3) | collective-permute-done | bytes 135200 | tf_op jit(solution)/shard_map/ppermute | solution.py:356
  22.0 1.5 %collective-permute-start.4 = (f32[264,128]{1,0:T(8,128)S(1)}, f32[264,128]{1,0:T(8,128)S(1)}, u32[]{:S(2)}, u32[]{:S(2)}) collective-permute-start(f32[264,128]{1,0:T(8,128)S(1)} %broadcast_select_fusion.5), channel_id=1, source_target_pairs={{0,8},{4,12},{8,0},{12,4},{1,9},{5,13},{9,1},{13,5},{2,10},{6,14},... | collective-permute-start | bytes 405512 | tf_op jit(solution)/shard_map/ppermute | solution.py:356
  23.5 0.6 %collective-permute-start.6 = (f32[256,128]{1,0:T(8,128)S(1)}, f32[256,128]{1,0:T(8,128)S(1)}, u32[]{:S(2)}, u32[]{:S(2)}) collective-permute-start(f32[256,128]{1,0:T(8,128)S(1)} %slice_select_fusion.1), channel_id=1, source_target_pairs={{0,8},{4,12},{8,0},{12,4},{1,9},{5,13},{9,1},{13,5},{2,10},{6,14},... | collective-permute-start | bytes 393224 | tf_op jit(solution)/shard_map/ppermute | solution.py:356
  24.1 2.9 %collective-permute-done.4 = f32[264,128]{1,0:T(8,128)S(1)} collective-permute-done((f32[264,128]{1,0:T(8,128)S(1)}, f32[264,128]{1,0:T(8,128)S(1)}, u32[]{:S(2)}, u32[]{:S(2)}) %collective-permute-start.4) | collective-permute-done | bytes 135200 | tf_op jit(solution)/shard_map/ppermute | solution.py:356
  27.1 0.1 collective-permute-start.5
  27.2 1.3 %collective-permute-done.6 = f32[256,128]{1,0:T(8,128)S(1)} collective-permute-done((f32[256,128]{1,0:T(8,128)S(1)}, f32[256,128]{1,0:T(8,128)S(1)}, u32[]{:S(2)}, u32[]{:S(2)}) %collective-permute-start.6) | collective-permute-done | bytes 131104 | tf_op jit(solution)/shard_map/ppermute | solution.py:356
  28.6 0.0 collective-permute-done.5
  28.6 1.6 %collective-permute-start.8 = (f32[256,128]{1,0:T(8,128)S(1)}, f32[256,128]{1,0:T(8,128)S(1)}, u32[]{:S(2)}, u32[]{:S(2)}) collective-permute-start(f32[256,128]{1,0:T(8,128)S(1)} %slice_select_fusion), channel_id=1, source_target_pairs={{0,16},{16,0},{1,17},{17,1},{2,18},{18,2},{3,19},{19,3},{4,20},{20... | collective-permute-start | bytes 393224 | tf_op jit(solution)/shard_map/ppermute | solution.py:356
  30.2 3.3 %k1.1 = (f32[128,128]{1,0:T(8,128)S(1)}, f32[128,128]{1,0:T(8,128)S(1)}, f32[128,128]{1,0:T(8,128)S(1)}, f32[128,128]{1,0:T(8,128)S(1)}, f32[128,128]{1,0:T(8,128)S(1)}, /*index=5*/f32[128,128]{1,0:T(8,128)S(1)}) custom-call(f32[264,128]{1,0:T(8,128)S(1)} %broadcast_select_fusion.7.packed_ref), custom_call_target="tpu_custom_call" | custom-call | flops 5000000000 | bytes 1000000 | tf_op jit(solution)/shard_map/k1/pallas_call | solution.py:392
  33.5 0.6 %collective-permute-start.7 = (f32[2,256,128]{2,1,0:T(8,128)S(1)}, f32[2,256,128]{2,1,0:T(8,128)S(1)}, u32[]{:S(2)}, u32[]{:S(2)}) collective-permute-start(f32[2,256,128]{2,1,0:T(8,128)S(1)} %pad_maximum_fusion.1), channel_id=1, source_target_pairs={{0,16},{16,0},{1,17},{17,1},{2,18},{18,2},{3,19},{19,3},{4,20},{20... | collective-permute-start | bytes 786440 | tf_op jit(solution)/shard_map/ppermute | solution.py:356
  34.1 0.0 collective-permute-done.8
  34.2 0.1 collective-permute-start.9
  34.3 2.7 %k2.1 = (f32[256,256]{1,0:T(8,128)S(1)}, f32[256,256]{1,0:T(8,128)S(1)}) custom-call(f32[128,128]{1,0:T(8,128)S(1)} %get-tuple-element.44.lower0_ref, f32[128,128]{1,0:T(8,128)S(1)} %get-tuple-element.45.inverse0_ref, f32[128,128]{1,0:T(8,128)S(1)} %get-tuple-element.46.left_ref, f32[128,128]{1,0:T(8,128)S(1)} %get-tuple-element.47.rest_ref, ...), custom_call_target="tpu_custom_call" | custom-call | flops 5000000000 | bytes 1000000 | tf_op jit(solution)/shard_map/k2/pallas_call | solution.py:392
  37.0 0.0 collective-permute-done.10
  37.1 0.6 %collective-permute-start.11 = (f32[2,256,128]{2,1,0:T(8,128)S(1)}, f32[2,256,128]{2,1,0:T(8,128)S(1)}, u32[]{:S(2)}, u32[]{:S(2)}) collective-permute-start(f32[2,256,128]{2,1,0:T(8,128)S(1)} %pad_maximum_fusion.3), channel_id=1, source_target_pairs={{0,4},{4,0},{8,12},{12,8},{1,5},{5,1},{9,13},{13,9},{2,6},{6,2},{1... | collective-permute-start | bytes 786440 | tf_op jit(solution)/shard_map/ppermute | solution.py:356
  37.7 0.0 collective-permute-done.9
  37.7 7.3 %k3.1 = (f32[256,256]{1,0:T(8,128)S(1)}, f32[256,256]{1,0:T(8,128)S(1)}, f32[256,256]{1,0:T(8,128)S(1)}, f32[256,256]{1,0:T(8,128)S(1)}) custom-call(f32[2,256,128]{2,1,0:T(8,128)S(1)} %get-tuple-element.73.corners_ref, f32[2,256,128]{2,1,0:T(8,128)S(1)} %get-tuple-element.72.belows_ref, f32[256,256]{1,0:T(8,128)S(1)} %get-tuple-element.50.inverse0_ref), custom_call_target="tpu_custom_call" | custom-call | flops 10000000000 | bytes 1000000 | tf_op jit(solution)/shard_map/k3/pallas_call | solution.py:392
  45.0 0.0 collective-permute-done.11
  45.1 0.0 collective-permute-done.7
  45.2 1.2 %kf.1 = (f32[256,128]{1,0:T(8,128)}, f32[2,256,256]{2,1,0:T(8,128)}) custom-call(s32[2,2]{1,0:T(2,128)S(1)} %bitcast.21, f32[256,128]{1,0:T(8,128)S(1)} %slice.17.own_ref, f32[264,128]{1,0:T(8,128)S(1)} %broadcast_select_fusion.7.packed_ref, f32[2,2,256,128]{3,2,1,0:T(8,128)S(1)} %pad_maximum_fusion.rows_ref, f32[2,256,128]{2,1,0:T(8,128)S(1)} %get-tuple-element.69.col0_ref, ...), custom_call_target="tpu_custom_call" | custom-call | flops 1000000000 | bytes 1000000 | tf_op jit(solution)/shard_map/kf/pallas_call | solution.py:392
  (20 shorter events, 0.4 us)
Async XLA Ops:
  1.6 6.6 %collective-permute-start = (f32[264,128]{1,0:T(8,128)S(1)}, f32[264,128]{1,0:T(8,128)S(1)}, u32[]{:S(2)}, u32[]{:S(2)}) collective-permute-start(f32[264,128]{1,0:T(8,128)S(1)} %get-tuple-element.34), channel_id=1, source_target_pairs={{0,16},{16,0},{1,17},{17,1},{2,18},{18,2},{3,19},{19,3},{4,20},{20... | collective-permute-start | bytes 405512 | tf_op jit(solution)/shard_map/ppermute | solution.py:356
  8.2 2.9 %copy-start = (s32[1,1,2,1,1,2]{5,4,3,2,1,0:T(1,128)S(1)}, s32[1,1,2,1,1,2]{5,4,3,2,1,0:T(1,128)}, u32[]{:S(2)}) copy-start(s32[1,1,2,1,1,2]{5,4,3,2,1,0:T(1,128)} %param.3) | copy-start | bytes 52
  8.2 8.6 %collective-permute-start.1 = (f32[264,128]{1,0:T(8,128)S(1)}, f32[264,128]{1,0:T(8,128)S(1)}, u32[]{:S(2)}, u32[]{:S(2)}) collective-permute-start(f32[264,128]{1,0:T(8,128)S(1)} %add.18), channel_id=1, source_target_pairs={{0,2},{1,3},{2,0},{3,1},{4,6},{5,7},{6,4},{7,5},{8,10},{9,11},{10,... | collective-permute-start | bytes 405512 | tf_op jit(solution)/shard_map/ppermute | solution.py:356
  11.2 5.7 %collective-permute-start.2 = (f32[256,128]{1,0:T(8,128)S(1)}, f32[256,128]{1,0:T(8,128)S(1)}, u32[]{:S(2)}, u32[]{:S(2)}) collective-permute-start(f32[256,128]{1,0:T(8,128)S(1)} %slice.17.own_ref), channel_id=1, source_target_pairs={{0,8},{4,12},{8,0},{12,4},{1,9},{5,13},{9,1},{13,5},{2,10},{6,14},... | collective-permute-start | bytes 393224 | tf_op jit(solution)/shard_map/ppermute | solution.py:356
  16.9 5.1 %collective-permute-start.3 = (f32[264,128]{1,0:T(8,128)S(1)}, f32[264,128]{1,0:T(8,128)S(1)}, u32[]{:S(2)}, u32[]{:S(2)}) collective-permute-start(f32[264,128]{1,0:T(8,128)S(1)} %broadcast_select_fusion.4), channel_id=1, source_target_pairs={{0,1},{1,0},{2,3},{3,2},{4,5},{5,4},{6,7},{7,6},{8,9},{9,8},{10,11... | collective-permute-start | bytes 405512 | tf_op jit(solution)/shard_map/ppermute | solution.py:356
  17.8 19.3 %collective-permute-start.10 = (f32[256,128]{1,0:T(8,128)S(1)}, f32[256,128]{1,0:T(8,128)S(1)}, u32[]{:S(2)}, u32[]{:S(2)}) collective-permute-start(f32[256,128]{1,0:T(8,128)S(1)} %broadcast_select_fusion.8), channel_id=1, source_target_pairs={{0,16},{16,0},{1,17},{17,1},{2,18},{18,2},{3,19},{19,3},{4,20},{20... | collective-permute-start | bytes 393224 | tf_op jit(solution)/shard_map/ppermute | solution.py:356
  22.0 5.1 %collective-permute-start.4 = (f32[264,128]{1,0:T(8,128)S(1)}, f32[264,128]{1,0:T(8,128)S(1)}, u32[]{:S(2)}, u32[]{:S(2)}) collective-permute-start(f32[264,128]{1,0:T(8,128)S(1)} %broadcast_select_fusion.5), channel_id=1, source_target_pairs={{0,8},{4,12},{8,0},{12,4},{1,9},{5,13},{9,1},{13,5},{2,10},{6,14},... | collective-permute-start | bytes 405512 | tf_op jit(solution)/shard_map/ppermute | solution.py:356
  23.5 5.0 %collective-permute-start.6 = (f32[256,128]{1,0:T(8,128)S(1)}, f32[256,128]{1,0:T(8,128)S(1)}, u32[]{:S(2)}, u32[]{:S(2)}) collective-permute-start(f32[256,128]{1,0:T(8,128)S(1)} %slice_select_fusion.1), channel_id=1, source_target_pairs={{0,8},{4,12},{8,0},{12,4},{1,9},{5,13},{9,1},{13,5},{2,10},{6,14},... | collective-permute-start | bytes 393224 | tf_op jit(solution)/shard_map/ppermute | solution.py:356
  27.1 1.5 %collective-permute-start.5 = (f32[264,128]{1,0:T(8,128)S(1)}, f32[264,128]{1,0:T(8,128)S(1)}, u32[]{:S(2)}, u32[]{:S(2)}) collective-permute-start(f32[264,128]{1,0:T(8,128)S(1)} %broadcast_select_fusion.6), channel_id=1, source_target_pairs={{0,4},{4,0},{8,12},{12,8},{1,5},{5,1},{9,13},{13,9},{2,6},{6,2},{1... | collective-permute-start | bytes 405512 | tf_op jit(solution)/shard_map/ppermute | solution.py:356
  28.6 5.5 %collective-permute-start.8 = (f32[256,128]{1,0:T(8,128)S(1)}, f32[256,128]{1,0:T(8,128)S(1)}, u32[]{:S(2)}, u32[]{:S(2)}) collective-permute-start(f32[256,128]{1,0:T(8,128)S(1)} %slice_select_fusion), channel_id=1, source_target_pairs={{0,16},{16,0},{1,17},{17,1},{2,18},{18,2},{3,19},{19,3},{4,20},{20... | collective-permute-start | bytes 393224 | tf_op jit(solution)/shard_map/ppermute | solution.py:356
  33.5 11.6 %collective-permute-start.7 = (f32[2,256,128]{2,1,0:T(8,128)S(1)}, f32[2,256,128]{2,1,0:T(8,128)S(1)}, u32[]{:S(2)}, u32[]{:S(2)}) collective-permute-start(f32[2,256,128]{2,1,0:T(8,128)S(1)} %pad_maximum_fusion.1), channel_id=1, source_target_pairs={{0,16},{16,0},{1,17},{17,1},{2,18},{18,2},{3,19},{19,3},{4,20},{20... | collective-permute-start | bytes 786440 | tf_op jit(solution)/shard_map/ppermute | solution.py:356
  34.2 3.5 %collective-permute-start.9 = (f32[2,256,128]{2,1,0:T(8,128)S(1)}, f32[2,256,128]{2,1,0:T(8,128)S(1)}, u32[]{:S(2)}, u32[]{:S(2)}) collective-permute-start(f32[2,256,128]{2,1,0:T(8,128)S(1)} %pad_maximum_fusion.2), channel_id=1, source_target_pairs={{0,4},{4,0},{8,12},{12,8},{1,5},{5,1},{9,13},{13,9},{2,6},{6,2},{1... | collective-permute-start | bytes 786440 | tf_op jit(solution)/shard_map/ppermute | solution.py:356
  37.1 7.9 %collective-permute-start.11 = (f32[2,256,128]{2,1,0:T(8,128)S(1)}, f32[2,256,128]{2,1,0:T(8,128)S(1)}, u32[]{:S(2)}, u32[]{:S(2)}) collective-permute-start(f32[2,256,128]{2,1,0:T(8,128)S(1)} %pad_maximum_fusion.3), channel_id=1, source_target_pairs={{0,4},{4,0},{8,12},{12,8},{1,5},{5,1},{9,13},{13,9},{2,6},{6,2},{1... | collective-permute-start | bytes 786440 | tf_op jit(solution)/shard_map/ppermute | solution.py:356

commit v9 on v8

--- a/solution.py
+++ b/solution.py
@@ -196,12 +196,10 @@
             ref[piece:, :] = jnp.zeros((height - piece, tile), F32)
 
 
-def unpack(pieces, to_ref):
-    tile = pieces[0].shape[1]
+def joined(pieces):
     slab = pieces[0].shape[0] // 2
-    for t, piece in enumerate(pieces):
-        to_ref[t * slab : (t + 1) * slab, :tile] = piece[pl.ds(0, slab, 2), :]
-        to_ref[t * slab : (t + 1) * slab, tile:] = piece[pl.ds(1, slab, 2), :]
+    halves = [[piece[pl.ds(j, slab, 2), :] for j in range(2)] for piece in pieces]
+    return jnp.concatenate([jnp.concatenate(half, axis=1) for half in halves], axis=0)
 
 
 def symmetric(lower, keep):
@@ -251,24 +249,24 @@
 
 
 def third_kernel(
-    corners_ref, belows_ref, inverse0_ref, left_ref, lower_ref, inverse_ref, cross_ref, corner_ref, below_ref, work,
+    corners_ref, belows_ref, inverse0_ref, left_ref, lower_ref, inverse_ref, cross_ref, work,
 ):
     tile = work.shape[0]
     first, second = slice(0, tile), slice(tile, 2 * tile)
     zero = jnp.zeros((tile, tile), F32)
-    unpack([belows_ref.at[t] for t in range(belows_ref.shape[0])], below_ref)
-    unpack([corners_ref.at[t] for t in range(corners_ref.shape[0])], corner_ref)
-    scales0, scales1 = scales(corner_ref[first, first]), scales(corner_ref[second, second])
-    top = dot(below_ref[first, :], inverse0_ref[...], NT)
+    below = joined([belows_ref.at[t] for t in range(belows_ref.shape[0])])
+    corner = joined([corners_ref.at[t] for t in range(corners_ref.shape[0])])
+    scales0, scales1 = scales(corner[first, first]), scales(corner[second, second])
+    top = dot(below[first, :], inverse0_ref[...], NT)
     factor(
-        corner_ref[first, first] - dot(top, top, NT),
+        corner[first, first] - dot(top, top, NT),
         *scales0, lower_ref.at[first, first], inverse_ref.at[first, first], work,
     )
-    bottom = dot(below_ref[second, :], inverse0_ref[...], NT)
+    bottom = dot(below[second, :], inverse0_ref[...], NT)
     left_ref[first, :] = top
     left_ref[second, :] = bottom
-    ahead = corner_ref[second, first] - dot(bottom, top, NT)
-    rest = corner_ref[second, second] - dot(bottom, bottom, NT)
+    ahead = corner[second, first] - dot(bottom, top, NT)
+    rest = corner[second, second] - dot(bottom, bottom, NT)
     under = dot(ahead, inverse_ref[first, first], NT)
     lower_ref[first, second] = zero
     lower_ref[second, first] = under
@@ -277,8 +275,8 @@
         rest - dot(under, under, NT),
         *scales1, lower_ref.at[second, second], inverse_ref.at[second, second], work,
     )
-    corner = dot_split(split(under), split(inverse_ref[first, first]))
-    inverse_ref[second, first] = -dot_split(split(inverse_ref[second, second]), split(corner))
+    bridge = dot_split(split(under), split(inverse_ref[first, first]))
+    inverse_ref[second, first] = -dot_split(split(inverse_ref[second, second]), split(bridge))
     cross = dot_split(split(left_ref[...]), split(inverse0_ref[...]))
     cross_ref[...] = -dot_split(split(inverse_ref[...]), split(cross))
 
@@ -307,9 +305,7 @@
 
     @pl.when(row > 1)
     def _():
-        for k in range(2):
-            unpack([rows_ref.at[t, k] for t in range(slabs)], row_ref.at[k])
-        f0, f1 = split(row_ref[0]), split(row_ref[1])
+        f0, f1 = (split(joined([rows_ref.at[t, k] for t in range(slabs)])) for k in range(2))
         panels_ref[0] = dot_split(f0, split(inverse0_ref[...]), NT)
         panels_ref[1] = dot_split(f0, split(cross_ref[...]), NT) + dot_split(f1, split(inverse1_ref[...]), NT)
 
@@ -332,9 +328,7 @@
 
     @pl.when(col > 1)
     def _():
-        for k, ref in enumerate((col0_ref, col1_ref)):
-            unpack([ref.at[t] for t in range(slabs)], row_ref.at[k])
-        g0, g1 = split(row_ref[0]), split(row_ref[1])
+        g0, g1 = (split(joined([ref.at[t] for t in range(slabs)])) for ref in (col0_ref, col1_ref))
         upper_ref[:width, :] = dot_split(split(inverse0_ref[...]), g0)
         upper_ref[width:, :] = dot_split(split(cross_ref[...]), g0) + dot_split(split(inverse1_ref[...]), g1)
 
@@ -486,7 +480,7 @@
         third_kernel,
         (big, big, big, big),
         (corners, belows, inverse0),
-        scratch=(big, big, square),
+        scratch=(square,),
         flops=10**10,
         name="k3",
     )

time: 46.6 us -> 46.6 us (level)
  no operation moved by 1% of the time
where the time goes in v9:
time: 46.6 us; the launch traced here: 46.4 us
  Pallas kernels  15.6 us (33%)
  starting transfers between devices  14.9 us (32%)
  waiting for transfers between devices  14.6 us (31%)
  between operations  0.8 us (2%)
    pallas_call x5, Pallas kernels, run(): pl.pallas_call(kernel, out_shape=tuple((jax.ShapeDtypeStruct(s, F32) for...  15.6 us
    ppermute x12, starting transfers between devices, trade(): lax.ppermute(x, axis, [(i, i ^ k) for i in range(lax.axis_size(axis))])  14.9 us
    ppermute x12, waiting for transfers between devices, trade(): lax.ppermute(x, axis, [(i, i ^ k) for i in range(lax.axis_size(axis))])  14.6 us
  transfers between devices with their start and end apart: 12, of which 5 were waited for; matrix products, arithmetic and copies ran while one was open for 1% of the time, Pallas kernels for 29%

profile of v9, /device:TPU:0, one launch (start us, length us, event | category | flops | bytes accessed | tf_op | source)
XLA Modules:
  0.0 46.4 jit_solution(3841692440233844596)
XLA Ops:
  0.6 1.0 %k0.1 = (f32[264,128]{1,0:T(8,128)S(1)}, f32[264,128]{1,0:T(8,128)S(1)}) custom-call(f32[512,128]{1,0:T(8,128)} %bitcast.23), custom_call_target="tpu_custom_call" | custom-call | bytes 1000000 | tf_op jit(solution)/shard_map/k0/pallas_call | solution.py:386
  1.6 3.0 %collective-permute-start = (f32[264,128]{1,0:T(8,128)S(1)}, f32[264,128]{1,0:T(8,128)S(1)}, u32[]{:S(2)}, u32[]{:S(2)}) collective-permute-start(f32[264,128]{1,0:T(8,128)S(1)} %get-tuple-element.34), channel_id=1, source_target_pairs={{0,16},{16,0},{1,17},{17,1},{2,18},{18,2},{3,19},{19,3},{4,20},{20... | collective-permute-start | bytes 405512 | tf_op jit(solution)/shard_map/ppermute | solution.py:350
  4.6 3.6 %collective-permute-done = f32[264,128]{1,0:T(8,128)S(1)} collective-permute-done((f32[264,128]{1,0:T(8,128)S(1)}, f32[264,128]{1,0:T(8,128)S(1)}, u32[]{:S(2)}, u32[]{:S(2)}) %collective-permute-start) | collective-permute-done | bytes 135200 | tf_op jit(solution)/shard_map/ppermute | solution.py:350
  8.2 0.0 copy-start
  8.2 2.9 %collective-permute-start.1 = (f32[264,128]{1,0:T(8,128)S(1)}, f32[264,128]{1,0:T(8,128)S(1)}, u32[]{:S(2)}, u32[]{:S(2)}) collective-permute-start(f32[264,128]{1,0:T(8,128)S(1)} %add.18), channel_id=1, source_target_pairs={{0,2},{1,3},{2,0},{3,1},{4,6},{5,7},{6,4},{7,5},{8,10},{9,11},{10,... | collective-permute-start | bytes 405512 | tf_op jit(solution)/shard_map/ppermute | solution.py:350
  11.1 0.0 copy-done
  11.2 1.6 %collective-permute-start.2 = (f32[256,128]{1,0:T(8,128)S(1)}, f32[256,128]{1,0:T(8,128)S(1)}, u32[]{:S(2)}, u32[]{:S(2)}) collective-permute-start(f32[256,128]{1,0:T(8,128)S(1)} %slice.17.own_ref), channel_id=1, source_target_pairs={{0,8},{4,12},{8,0},{12,4},{1,9},{5,13},{9,1},{13,5},{2,10},{6,14},... | collective-permute-start | bytes 393224 | tf_op jit(solution)/shard_map/ppermute | solution.py:350
  12.7 4.1 %collective-permute-done.1 = f32[264,128]{1,0:T(8,128)S(1)} collective-permute-done((f32[264,128]{1,0:T(8,128)S(1)}, f32[264,128]{1,0:T(8,128)S(1)}, u32[]{:S(2)}, u32[]{:S(2)}) %collective-permute-start.1) | collective-permute-done | bytes 135200 | tf_op jit(solution)/shard_map/ppermute | solution.py:350
  16.9 0.0 collective-permute-done.2
  16.9 0.9 %collective-permute-start.3 = (f32[264,128]{1,0:T(8,128)S(1)}, f32[264,128]{1,0:T(8,128)S(1)}, u32[]{:S(2)}, u32[]{:S(2)}) collective-permute-start(f32[264,128]{1,0:T(8,128)S(1)} %broadcast_select_fusion.4), channel_id=1, source_target_pairs={{0,1},{1,0},{2,3},{3,2},{4,5},{5,4},{6,7},{7,6},{8,9},{9,8},{10,11... | collective-permute-start | bytes 405512 | tf_op jit(solution)/shard_map/ppermute | solution.py:350
  17.8 1.6 %collective-permute-start.10 = (f32[256,128]{1,0:T(8,128)S(1)}, f32[256,128]{1,0:T(8,128)S(1)}, u32[]{:S(2)}, u32[]{:S(2)}) collective-permute-start(f32[256,128]{1,0:T(8,128)S(1)} %broadcast_select_fusion.8), channel_id=1, source_target_pairs={{0,16},{16,0},{1,17},{17,1},{2,18},{18,2},{3,19},{19,3},{4,20},{20... | collective-permute-start | bytes 393224 | tf_op jit(solution)/shard_map/ppermute | solution.py:350
  19.3 2.6 %collective-permute-done.3 = f32[264,128]{1,0:T(8,128)S(1)} collective-permute-done((f32[264,128]{1,0:T(8,128)S(1)}, f32[264,128]{1,0:T(8,128)S(1)}, u32[]{:S(2)}, u32[]{:S(2)}) %collective-permute-start.3) | collective-permute-done | bytes 135200 | tf_op jit(solution)/shard_map/ppermute | solution.py:350
  22.0 1.5 %collective-permute-start.4 = (f32[264,128]{1,0:T(8,128)S(1)}, f32[264,128]{1,0:T(8,128)S(1)}, u32[]{:S(2)}, u32[]{:S(2)}) collective-permute-start(f32[264,128]{1,0:T(8,128)S(1)} %broadcast_select_fusion.5), channel_id=1, source_target_pairs={{0,8},{4,12},{8,0},{12,4},{1,9},{5,13},{9,1},{13,5},{2,10},{6,14},... | collective-permute-start | bytes 405512 | tf_op jit(solution)/shard_map/ppermute | solution.py:350
  23.5 0.6 %collective-permute-start.6 = (f32[256,128]{1,0:T(8,128)S(1)}, f32[256,128]{1,0:T(8,128)S(1)}, u32[]{:S(2)}, u32[]{:S(2)}) collective-permute-start(f32[256,128]{1,0:T(8,128)S(1)} %slice_select_fusion.1), channel_id=1, source_target_pairs={{0,8},{4,12},{8,0},{12,4},{1,9},{5,13},{9,1},{13,5},{2,10},{6,14},... | collective-permute-start | bytes 393224 | tf_op jit(solution)/shard_map/ppermute | solution.py:350
  24.1 2.9 %collective-permute-done.4 = f32[264,128]{1,0:T(8,128)S(1)} collective-permute-done((f32[264,128]{1,0:T(8,128)S(1)}, f32[264,128]{1,0:T(8,128)S(1)}, u32[]{:S(2)}, u32[]{:S(2)}) %collective-permute-start.4) | collective-permute-done | bytes 135200 | tf_op jit(solution)/shard_map/ppermute | solution.py:350
  27.1 0.1 collective-permute-start.5
  27.2 1.3 %collective-permute-done.6 = f32[256,128]{1,0:T(8,128)S(1)} collective-permute-done((f32[256,128]{1,0:T(8,128)S(1)}, f32[256,128]{1,0:T(8,128)S(1)}, u32[]{:S(2)}, u32[]{:S(2)}) %collective-permute-start.6) | collective-permute-done | bytes 131104 | tf_op jit(solution)/shard_map/ppermute | solution.py:350
  28.6 0.0 collective-permute-done.5
  28.6 1.6 %collective-permute-start.8 = (f32[256,128]{1,0:T(8,128)S(1)}, f32[256,128]{1,0:T(8,128)S(1)}, u32[]{:S(2)}, u32[]{:S(2)}) collective-permute-start(f32[256,128]{1,0:T(8,128)S(1)} %slice_select_fusion), channel_id=1, source_target_pairs={{0,16},{16,0},{1,17},{17,1},{2,18},{18,2},{3,19},{19,3},{4,20},{20... | collective-permute-start | bytes 393224 | tf_op jit(solution)/shard_map/ppermute | solution.py:350
  30.2 3.3 %k1.1 = (f32[128,128]{1,0:T(8,128)S(1)}, f32[128,128]{1,0:T(8,128)S(1)}, f32[128,128]{1,0:T(8,128)S(1)}, f32[128,128]{1,0:T(8,128)S(1)}, f32[128,128]{1,0:T(8,128)S(1)}, /*index=5*/f32[128,128]{1,0:T(8,128)S(1)}) custom-call(f32[264,128]{1,0:T(8,128)S(1)} %broadcast_select_fusion.7.packed_ref), custom_call_target="tpu_custom_call" | custom-call | flops 5000000000 | bytes 1000000 | tf_op jit(solution)/shard_map/k1/pallas_call | solution.py:386
  33.5 0.6 %collective-permute-start.7 = (f32[2,256,128]{2,1,0:T(8,128)S(1)}, f32[2,256,128]{2,1,0:T(8,128)S(1)}, u32[]{:S(2)}, u32[]{:S(2)}) collective-permute-start(f32[2,256,128]{2,1,0:T(8,128)S(1)} %pad_maximum_fusion.1), channel_id=1, source_target_pairs={{0,16},{16,0},{1,17},{17,1},{2,18},{18,2},{3,19},{19,3},{4,20},{20... | collective-permute-start | bytes 786440 | tf_op jit(solution)/shard_map/ppermute | solution.py:350
  34.1 0.0 collective-permute-done.8
  34.2 0.1 collective-permute-start.9
  34.3 2.7 %k2.1 = (f32[256,256]{1,0:T(8,128)S(1)}, f32[256,256]{1,0:T(8,128)S(1)}) custom-call(f32[128,128]{1,0:T(8,128)S(1)} %get-tuple-element.44.lower0_ref, f32[128,128]{1,0:T(8,128)S(1)} %get-tuple-element.45.inverse0_ref, f32[128,128]{1,0:T(8,128)S(1)} %get-tuple-element.46.left_ref, f32[128,128]{1,0:T(8,128)S(1)} %get-tuple-element.47.rest_ref, ...), custom_call_target="tpu_custom_call" | custom-call | flops 5000000000 | bytes 1000000 | tf_op jit(solution)/shard_map/k2/pallas_call | solution.py:386
  37.0 0.0 collective-permute-done.10
  37.1 0.6 %collective-permute-start.11 = (f32[2,256,128]{2,1,0:T(8,128)S(1)}, f32[2,256,128]{2,1,0:T(8,128)S(1)}, u32[]{:S(2)}, u32[]{:S(2)}) collective-permute-start(f32[2,256,128]{2,1,0:T(8,128)S(1)} %pad_maximum_fusion.3), channel_id=1, source_target_pairs={{0,4},{4,0},{8,12},{12,8},{1,5},{5,1},{9,13},{13,9},{2,6},{6,2},{1... | collective-permute-start | bytes 786440 | tf_op jit(solution)/shard_map/ppermute | solution.py:350
  37.7 0.0 collective-permute-done.9
  37.7 7.3 %k3.1 = (f32[256,256]{1,0:T(8,128)S(1)}, f32[256,256]{1,0:T(8,128)S(1)}, f32[256,256]{1,0:T(8,128)S(1)}, f32[256,256]{1,0:T(8,128)S(1)}) custom-call(f32[2,256,128]{2,1,0:T(8,128)S(1)} %get-tuple-element.73.corners_ref, f32[2,256,128]{2,1,0:T(8,128)S(1)} %get-tuple-element.72.belows_ref, f32[256,256]{1,0:T(8,128)S(1)} %get-tuple-element.50.inverse0_ref), custom_call_target="tpu_custom_call" | custom-call | flops 10000000000 | bytes 1000000 | tf_op jit(solution)/shard_map/k3/pallas_call | solution.py:386
  45.0 0.0 collective-permute-done.11
  45.1 0.0 collective-permute-done.7
  45.2 1.2 %kf.1 = (f32[256,128]{1,0:T(8,128)}, f32[2,256,256]{2,1,0:T(8,128)}) custom-call(s32[2,2]{1,0:T(2,128)S(1)} %bitcast.21, f32[256,128]{1,0:T(8,128)S(1)} %slice.17.own_ref, f32[264,128]{1,0:T(8,128)S(1)} %broadcast_select_fusion.7.packed_ref, f32[2,2,256,128]{3,2,1,0:T(8,128)S(1)} %pad_maximum_fusion.rows_ref, f32[2,256,128]{2,1,0:T(8,128)S(1)} %get-tuple-element.69.col0_ref, ...), custom_call_target="tpu_custom_call" | custom-call | flops 1000000000 | bytes 1000000 | tf_op jit(solution)/shard_map/kf/pallas_call | solution.py:386
  (20 shorter events, 0.4 us)
Async XLA Ops:
  1.6 6.6 %collective-permute-start = (f32[264,128]{1,0:T(8,128)S(1)}, f32[264,128]{1,0:T(8,128)S(1)}, u32[]{:S(2)}, u32[]{:S(2)}) collective-permute-start(f32[264,128]{1,0:T(8,128)S(1)} %get-tuple-element.34), channel_id=1, source_target_pairs={{0,16},{16,0},{1,17},{17,1},{2,18},{18,2},{3,19},{19,3},{4,20},{20... | collective-permute-start | bytes 405512 | tf_op jit(solution)/shard_map/ppermute | solution.py:350
  8.2 2.9 %copy-start = (s32[1,1,2,1,1,2]{5,4,3,2,1,0:T(1,128)S(1)}, s32[1,1,2,1,1,2]{5,4,3,2,1,0:T(1,128)}, u32[]{:S(2)}) copy-start(s32[1,1,2,1,1,2]{5,4,3,2,1,0:T(1,128)} %param.3) | copy-start | bytes 52
  8.2 8.6 %collective-permute-start.1 = (f32[264,128]{1,0:T(8,128)S(1)}, f32[264,128]{1,0:T(8,128)S(1)}, u32[]{:S(2)}, u32[]{:S(2)}) collective-permute-start(f32[264,128]{1,0:T(8,128)S(1)} %add.18), channel_id=1, source_target_pairs={{0,2},{1,3},{2,0},{3,1},{4,6},{5,7},{6,4},{7,5},{8,10},{9,11},{10,... | collective-permute-start | bytes 405512 | tf_op jit(solution)/shard_map/ppermute | solution.py:350
  11.2 5.7 %collective-permute-start.2 = (f32[256,128]{1,0:T(8,128)S(1)}, f32[256,128]{1,0:T(8,128)S(1)}, u32[]{:S(2)}, u32[]{:S(2)}) collective-permute-start(f32[256,128]{1,0:T(8,128)S(1)} %slice.17.own_ref), channel_id=1, source_target_pairs={{0,8},{4,12},{8,0},{12,4},{1,9},{5,13},{9,1},{13,5},{2,10},{6,14},... | collective-permute-start | bytes 393224 | tf_op jit(solution)/shard_map/ppermute | solution.py:350
  16.9 5.1 %collective-permute-start.3 = (f32[264,128]{1,0:T(8,128)S(1)}, f32[264,128]{1,0:T(8,128)S(1)}, u32[]{:S(2)}, u32[]{:S(2)}) collective-permute-start(f32[264,128]{1,0:T(8,128)S(1)} %broadcast_select_fusion.4), channel_id=1, source_target_pairs={{0,1},{1,0},{2,3},{3,2},{4,5},{5,4},{6,7},{7,6},{8,9},{9,8},{10,11... | collective-permute-start | bytes 405512 | tf_op jit(solution)/shard_map/ppermute | solution.py:350
  17.8 19.3 %collective-permute-start.10 = (f32[256,128]{1,0:T(8,128)S(1)}, f32[256,128]{1,0:T(8,128)S(1)}, u32[]{:S(2)}, u32[]{:S(2)}) collective-permute-start(f32[256,128]{1,0:T(8,128)S(1)} %broadcast_select_fusion.8), channel_id=1, source_target_pairs={{0,16},{16,0},{1,17},{17,1},{2,18},{18,2},{3,19},{19,3},{4,20},{20... | collective-permute-start | bytes 393224 | tf_op jit(solution)/shard_map/ppermute | solution.py:350
  22.0 5.1 %collective-permute-start.4 = (f32[264,128]{1,0:T(8,128)S(1)}, f32[264,128]{1,0:T(8,128)S(1)}, u32[]{:S(2)}, u32[]{:S(2)}) collective-permute-start(f32[264,128]{1,0:T(8,128)S(1)} %broadcast_select_fusion.5), channel_id=1, source_target_pairs={{0,8},{4,12},{8,0},{12,4},{1,9},{5,13},{9,1},{13,5},{2,10},{6,14},... | collective-permute-start | bytes 405512 | tf_op jit(solution)/shard_map/ppermute | solution.py:350
  23.5 5.0 %collective-permute-start.6 = (f32[256,128]{1,0:T(8,128)S(1)}, f32[256,128]{1,0:T(8,128)S(1)}, u32[]{:S(2)}, u32[]{:S(2)}) collective-permute-start(f32[256,128]{1,0:T(8,128)S(1)} %slice_select_fusion.1), channel_id=1, source_target_pairs={{0,8},{4,12},{8,0},{12,4},{1,9},{5,13},{9,1},{13,5},{2,10},{6,14},... | collective-permute-start | bytes 393224 | tf_op jit(solution)/shard_map/ppermute | solution.py:350
  27.1 1.5 %collective-permute-start.5 = (f32[264,128]{1,0:T(8,128)S(1)}, f32[264,128]{1,0:T(8,128)S(1)}, u32[]{:S(2)}, u32[]{:S(2)}) collective-permute-start(f32[264,128]{1,0:T(8,128)S(1)} %broadcast_select_fusion.6), channel_id=1, source_target_pairs={{0,4},{4,0},{8,12},{12,8},{1,5},{5,1},{9,13},{13,9},{2,6},{6,2},{1... | collective-permute-start | bytes 405512 | tf_op jit(solution)/shard_map/ppermute | solution.py:350
  28.6 5.5 %collective-permute-start.8 = (f32[256,128]{1,0:T(8,128)S(1)}, f32[256,128]{1,0:T(8,128)S(1)}, u32[]{:S(2)}, u32[]{:S(2)}) collective-permute-start(f32[256,128]{1,0:T(8,128)S(1)} %slice_select_fusion), channel_id=1, source_target_pairs={{0,16},{16,0},{1,17},{17,1},{2,18},{18,2},{3,19},{19,3},{4,20},{20... | collective-permute-start | bytes 393224 | tf_op jit(solution)/shard_map/ppermute | solution.py:350
  33.5 11.6 %collective-permute-start.7 = (f32[2,256,128]{2,1,0:T(8,128)S(1)}, f32[2,256,128]{2,1,0:T(8,128)S(1)}, u32[]{:S(2)}, u32[]{:S(2)}) collective-permute-start(f32[2,256,128]{2,1,0:T(8,128)S(1)} %pad_maximum_fusion.1), channel_id=1, source_target_pairs={{0,16},{16,0},{1,17},{17,1},{2,18},{18,2},{3,19},{19,3},{4,20},{20... | collective-permute-start | bytes 786440 | tf_op jit(solution)/shard_map/ppermute | solution.py:350
  34.2 3.5 %collective-permute-start.9 = (f32[2,256,128]{2,1,0:T(8,128)S(1)}, f32[2,256,128]{2,1,0:T(8,128)S(1)}, u32[]{:S(2)}, u32[]{:S(2)}) collective-permute-start(f32[2,256,128]{2,1,0:T(8,128)S(1)} %pad_maximum_fusion.2), channel_id=1, source_target_pairs={{0,4},{4,0},{8,12},{12,8},{1,5},{5,1},{9,13},{13,9},{2,6},{6,2},{1... | collective-permute-start | bytes 786440 | tf_op jit(solution)/shard_map/ppermute | solution.py:350
  37.1 7.9 %collective-permute-start.11 = (f32[2,256,128]{2,1,0:T(8,128)S(1)}, f32[2,256,128]{2,1,0:T(8,128)S(1)}, u32[]{:S(2)}, u32[]{:S(2)}) collective-permute-start(f32[2,256,128]{2,1,0:T(8,128)S(1)} %pad_maximum_fusion.3), channel_id=1, source_target_pairs={{0,4},{4,0},{8,12},{12,8},{1,5},{5,1},{9,13},{13,9},{2,6},{6,2},{1... | collective-permute-start | bytes 786440 | tf_op jit(solution)/shard_map/ppermute | solution.py:350

commit v10 on v8

--- a/solution.py
+++ b/solution.py
@@ -339,8 +339,18 @@
         upper_ref[width:, :] = dot_split(split(cross_ref[...]), g0) + dot_split(split(inverse1_ref[...]), g1)
 
     slab = pl.ds(pl.multiple_of(layer * slab_rows, slab_rows), slab_rows)
-    product = dot_split(split(panels_ref[0, slab, :]), split(upper_ref[:width, :]))
-    product += dot_split(split(panels_ref[1, slab, :]), split(upper_ref[width:, :]))
+
+    @pl.when(col == 0)
+    def _():
+        row_ref[1, :slab_rows, :] = jnp.zeros((slab_rows, width), F32)
+
+    @pl.when(col > 0)
+    def _():
+        first = dot_split(split(panels_ref[0, slab, :]), split(upper_ref[:width, :]))
+        second = dot_split(split(panels_ref[1, slab, :]), split(upper_ref[width:, :]))
+        row_ref[1, :slab_rows, :] = first + second
+
+    product = row_ref[1, :slab_rows, :]
     at_row = (lax.broadcasted_iota(jnp.int32, (slab_rows, tile), 0) + layer * slab_rows) // tile
     for j in range(tiles_per):
         keep = jnp.zeros((slab_rows, tile), jnp.int32)

time: 46.6 us -> 46.5 us (level)
  no operation moved by 1% of the time
where the time goes in v10:
time: 46.5 us; the launch traced here: 46.3 us
  Pallas kernels  15.5 us (33%)
  starting transfers between devices  14.9 us (32%)
  waiting for transfers between devices  14.6 us (31%)
  between operations  0.8 us (2%)
    pallas_call x5, Pallas kernels, run(): pl.pallas_call(kernel, out_shape=tuple((jax.ShapeDtypeStruct(s, F32) for...  15.5 us
    ppermute x12, starting transfers between devices, trade(): lax.ppermute(x, axis, [(i, i ^ k) for i in range(lax.axis_size(axis))])  14.9 us
    ppermute x12, waiting for transfers between devices, trade(): lax.ppermute(x, axis, [(i, i ^ k) for i in range(lax.axis_size(axis))])  14.6 us
  transfers between devices with their start and end apart: 12, of which 5 were waited for; matrix products, arithmetic and copies ran while one was open for 1% of the time, Pallas kernels for 29%

profile of v10, /device:TPU:0, one launch (start us, length us, event | category | flops | bytes accessed | tf_op | source)
XLA Modules:
  0.0 46.3 jit_solution(14747450860340135488)
XLA Ops:
  0.6 1.0 %k0.1 = (f32[264,128]{1,0:T(8,128)S(1)}, f32[264,128]{1,0:T(8,128)S(1)}) custom-call(f32[512,128]{1,0:T(8,128)} %bitcast.23), custom_call_target="tpu_custom_call" | custom-call | bytes 1000000 | tf_op jit(solution)/shard_map/k0/pallas_call | solution.py:402
  1.6 3.0 %collective-permute-start = (f32[264,128]{1,0:T(8,128)S(1)}, f32[264,128]{1,0:T(8,128)S(1)}, u32[]{:S(2)}, u32[]{:S(2)}) collective-permute-start(f32[264,128]{1,0:T(8,128)S(1)} %get-tuple-element.34), channel_id=1, source_target_pairs={{0,16},{16,0},{1,17},{17,1},{2,18},{18,2},{3,19},{19,3},{4,20},{20... | collective-permute-start | bytes 405512 | tf_op jit(solution)/shard_map/ppermute | solution.py:366
  4.6 3.6 %collective-permute-done = f32[264,128]{1,0:T(8,128)S(1)} collective-permute-done((f32[264,128]{1,0:T(8,128)S(1)}, f32[264,128]{1,0:T(8,128)S(1)}, u32[]{:S(2)}, u32[]{:S(2)}) %collective-permute-start) | collective-permute-done | bytes 135200 | tf_op jit(solution)/shard_map/ppermute | solution.py:366
  8.2 0.0 copy-start
  8.2 2.9 %collective-permute-start.1 = (f32[264,128]{1,0:T(8,128)S(1)}, f32[264,128]{1,0:T(8,128)S(1)}, u32[]{:S(2)}, u32[]{:S(2)}) collective-permute-start(f32[264,128]{1,0:T(8,128)S(1)} %add.18), channel_id=1, source_target_pairs={{0,2},{1,3},{2,0},{3,1},{4,6},{5,7},{6,4},{7,5},{8,10},{9,11},{10,... | collective-permute-start | bytes 405512 | tf_op jit(solution)/shard_map/ppermute | solution.py:366
  11.1 0.0 copy-done
  11.2 1.6 %collective-permute-start.2 = (f32[256,128]{1,0:T(8,128)S(1)}, f32[256,128]{1,0:T(8,128)S(1)}, u32[]{:S(2)}, u32[]{:S(2)}) collective-permute-start(f32[256,128]{1,0:T(8,128)S(1)} %slice.17.own_ref), channel_id=1, source_target_pairs={{0,8},{4,12},{8,0},{12,4},{1,9},{5,13},{9,1},{13,5},{2,10},{6,14},... | collective-permute-start | bytes 393224 | tf_op jit(solution)/shard_map/ppermute | solution.py:366
  12.7 4.1 %collective-permute-done.1 = f32[264,128]{1,0:T(8,128)S(1)} collective-permute-done((f32[264,128]{1,0:T(8,128)S(1)}, f32[264,128]{1,0:T(8,128)S(1)}, u32[]{:S(2)}, u32[]{:S(2)}) %collective-permute-start.1) | collective-permute-done | bytes 135200 | tf_op jit(solution)/shard_map/ppermute | solution.py:366
  16.9 0.0 collective-permute-done.2
  16.9 0.9 %collective-permute-start.3 = (f32[264,128]{1,0:T(8,128)S(1)}, f32[264,128]{1,0:T(8,128)S(1)}, u32[]{:S(2)}, u32[]{:S(2)}) collective-permute-start(f32[264,128]{1,0:T(8,128)S(1)} %broadcast_select_fusion.4), channel_id=1, source_target_pairs={{0,1},{1,0},{2,3},{3,2},{4,5},{5,4},{6,7},{7,6},{8,9},{9,8},{10,11... | collective-permute-start | bytes 405512 | tf_op jit(solution)/shard_map/ppermute | solution.py:366
  17.8 1.6 %collective-permute-start.10 = (f32[256,128]{1,0:T(8,128)S(1)}, f32[256,128]{1,0:T(8,128)S(1)}, u32[]{:S(2)}, u32[]{:S(2)}) collective-permute-start(f32[256,128]{1,0:T(8,128)S(1)} %broadcast_select_fusion.8), channel_id=1, source_target_pairs={{0,16},{16,0},{1,17},{17,1},{2,18},{18,2},{3,19},{19,3},{4,20},{20... | collective-permute-start | bytes 393224 | tf_op jit(solution)/shard_map/ppermute | solution.py:366
  19.3 2.6 %collective-permute-done.3 = f32[264,128]{1,0:T(8,128)S(1)} collective-permute-done((f32[264,128]{1,0:T(8,128)S(1)}, f32[264,128]{1,0:T(8,128)S(1)}, u32[]{:S(2)}, u32[]{:S(2)}) %collective-permute-start.3) | collective-permute-done | bytes 135200 | tf_op jit(solution)/shard_map/ppermute | solution.py:366
  22.0 1.5 %collective-permute-start.4 = (f32[264,128]{1,0:T(8,128)S(1)}, f32[264,128]{1,0:T(8,128)S(1)}, u32[]{:S(2)}, u32[]{:S(2)}) collective-permute-start(f32[264,128]{1,0:T(8,128)S(1)} %broadcast_select_fusion.5), channel_id=1, source_target_pairs={{0,8},{4,12},{8,0},{12,4},{1,9},{5,13},{9,1},{13,5},{2,10},{6,14},... | collective-permute-start | bytes 405512 | tf_op jit(solution)/shard_map/ppermute | solution.py:366
  23.5 0.6 %collective-permute-start.6 = (f32[256,128]{1,0:T(8,128)S(1)}, f32[256,128]{1,0:T(8,128)S(1)}, u32[]{:S(2)}, u32[]{:S(2)}) collective-permute-start(f32[256,128]{1,0:T(8,128)S(1)} %slice_select_fusion.1), channel_id=1, source_target_pairs={{0,8},{4,12},{8,0},{12,4},{1,9},{5,13},{9,1},{13,5},{2,10},{6,14},... | collective-permute-start | bytes 393224 | tf_op jit(solution)/shard_map/ppermute | solution.py:366
  24.1 2.9 %collective-permute-done.4 = f32[264,128]{1,0:T(8,128)S(1)} collective-permute-done((f32[264,128]{1,0:T(8,128)S(1)}, f32[264,128]{1,0:T(8,128)S(1)}, u32[]{:S(2)}, u32[]{:S(2)}) %collective-permute-start.4) | collective-permute-done | bytes 135200 | tf_op jit(solution)/shard_map/ppermute | solution.py:366
  27.1 0.1 collective-permute-start.5
  27.2 1.3 %collective-permute-done.6 = f32[256,128]{1,0:T(8,128)S(1)} collective-permute-done((f32[256,128]{1,0:T(8,128)S(1)}, f32[256,128]{1,0:T(8,128)S(1)}, u32[]{:S(2)}, u32[]{:S(2)}) %collective-permute-start.6) | collective-permute-done | bytes 131104 | tf_op jit(solution)/shard_map/ppermute | solution.py:366
  28.6 0.0 collective-permute-done.5
  28.6 1.6 %collective-permute-start.8 = (f32[256,128]{1,0:T(8,128)S(1)}, f32[256,128]{1,0:T(8,128)S(1)}, u32[]{:S(2)}, u32[]{:S(2)}) collective-permute-start(f32[256,128]{1,0:T(8,128)S(1)} %slice_select_fusion), channel_id=1, source_target_pairs={{0,16},{16,0},{1,17},{17,1},{2,18},{18,2},{3,19},{19,3},{4,20},{20... | collective-permute-start | bytes 393224 | tf_op jit(solution)/shard_map/ppermute | solution.py:366
  30.2 3.3 %k1.1 = (f32[128,128]{1,0:T(8,128)S(1)}, f32[128,128]{1,0:T(8,128)S(1)}, f32[128,128]{1,0:T(8,128)S(1)}, f32[128,128]{1,0:T(8,128)S(1)}, f32[128,128]{1,0:T(8,128)S(1)}, /*index=5*/f32[128,128]{1,0:T(8,128)S(1)}) custom-call(f32[264,128]{1,0:T(8,128)S(1)} %broadcast_select_fusion.7.packed_ref), custom_call_target="tpu_custom_call" | custom-call | flops 5000000000 | bytes 1000000 | tf_op jit(solution)/shard_map/k1/pallas_call | solution.py:402
  33.5 0.6 %collective-permute-start.7 = (f32[2,256,128]{2,1,0:T(8,128)S(1)}, f32[2,256,128]{2,1,0:T(8,128)S(1)}, u32[]{:S(2)}, u32[]{:S(2)}) collective-permute-start(f32[2,256,128]{2,1,0:T(8,128)S(1)} %pad_maximum_fusion.1), channel_id=1, source_target_pairs={{0,16},{16,0},{1,17},{17,1},{2,18},{18,2},{3,19},{19,3},{4,20},{20... | collective-permute-start | bytes 786440 | tf_op jit(solution)/shard_map/ppermute | solution.py:366
  34.1 0.0 collective-permute-done.8
  34.2 0.1 collective-permute-start.9
  34.3 2.7 %k2.1 = (f32[256,256]{1,0:T(8,128)S(1)}, f32[256,256]{1,0:T(8,128)S(1)}) custom-call(f32[128,128]{1,0:T(8,128)S(1)} %get-tuple-element.44.lower0_ref, f32[128,128]{1,0:T(8,128)S(1)} %get-tuple-element.45.inverse0_ref, f32[128,128]{1,0:T(8,128)S(1)} %get-tuple-element.46.left_ref, f32[128,128]{1,0:T(8,128)S(1)} %get-tuple-element.47.rest_ref, ...), custom_call_target="tpu_custom_call" | custom-call | flops 5000000000 | bytes 1000000 | tf_op jit(solution)/shard_map/k2/pallas_call | solution.py:402
  37.0 0.0 collective-permute-done.10
  37.1 0.6 %collective-permute-start.11 = (f32[2,256,128]{2,1,0:T(8,128)S(1)}, f32[2,256,128]{2,1,0:T(8,128)S(1)}, u32[]{:S(2)}, u32[]{:S(2)}) collective-permute-start(f32[2,256,128]{2,1,0:T(8,128)S(1)} %pad_maximum_fusion.3), channel_id=1, source_target_pairs={{0,4},{4,0},{8,12},{12,8},{1,5},{5,1},{9,13},{13,9},{2,6},{6,2},{1... | collective-permute-start | bytes 786440 | tf_op jit(solution)/shard_map/ppermute | solution.py:366
  37.7 0.0 collective-permute-done.9
  37.7 7.3 %k3.1 = (f32[256,256]{1,0:T(8,128)S(1)}, f32[256,256]{1,0:T(8,128)S(1)}, f32[256,256]{1,0:T(8,128)S(1)}, f32[256,256]{1,0:T(8,128)S(1)}) custom-call(f32[2,256,128]{2,1,0:T(8,128)S(1)} %get-tuple-element.73.corners_ref, f32[2,256,128]{2,1,0:T(8,128)S(1)} %get-tuple-element.72.belows_ref, f32[256,256]{1,0:T(8,128)S(1)} %get-tuple-element.50.inverse0_ref), custom_call_target="tpu_custom_call" | custom-call | flops 10000000000 | bytes 1000000 | tf_op jit(solution)/shard_map/k3/pallas_call | solution.py:402
  45.0 0.0 collective-permute-done.11
  45.1 0.0 collective-permute-done.7
  45.2 1.1 %kf.1 = (f32[256,128]{1,0:T(8,128)}, f32[2,256,256]{2,1,0:T(8,128)}) custom-call(s32[2,2]{1,0:T(2,128)S(1)} %bitcast.21, f32[256,128]{1,0:T(8,128)S(1)} %slice.17.own_ref, f32[264,128]{1,0:T(8,128)S(1)} %broadcast_select_fusion.7.packed_ref, f32[2,2,256,128]{3,2,1,0:T(8,128)S(1)} %pad_maximum_fusion.rows_ref, f32[2,256,128]{2,1,0:T(8,128)S(1)} %get-tuple-element.69.col0_ref, ...), custom_call_target="tpu_custom_call" | custom-call | flops 1000000000 | bytes 1000000 | tf_op jit(solution)/shard_map/kf/pallas_call | solution.py:402
  (20 shorter events, 0.4 us)
Async XLA Ops:
  1.6 6.6 %collective-permute-start = (f32[264,128]{1,0:T(8,128)S(1)}, f32[264,128]{1,0:T(8,128)S(1)}, u32[]{:S(2)}, u32[]{:S(2)}) collective-permute-start(f32[264,128]{1,0:T(8,128)S(1)} %get-tuple-element.34), channel_id=1, source_target_pairs={{0,16},{16,0},{1,17},{17,1},{2,18},{18,2},{3,19},{19,3},{4,20},{20... | collective-permute-start | bytes 405512 | tf_op jit(solution)/shard_map/ppermute | solution.py:366
  8.2 2.9 %copy-start = (s32[1,1,2,1,1,2]{5,4,3,2,1,0:T(1,128)S(1)}, s32[1,1,2,1,1,2]{5,4,3,2,1,0:T(1,128)}, u32[]{:S(2)}) copy-start(s32[1,1,2,1,1,2]{5,4,3,2,1,0:T(1,128)} %param.3) | copy-start | bytes 52
  8.2 8.6 %collective-permute-start.1 = (f32[264,128]{1,0:T(8,128)S(1)}, f32[264,128]{1,0:T(8,128)S(1)}, u32[]{:S(2)}, u32[]{:S(2)}) collective-permute-start(f32[264,128]{1,0:T(8,128)S(1)} %add.18), channel_id=1, source_target_pairs={{0,2},{1,3},{2,0},{3,1},{4,6},{5,7},{6,4},{7,5},{8,10},{9,11},{10,... | collective-permute-start | bytes 405512 | tf_op jit(solution)/shard_map/ppermute | solution.py:366
  11.2 5.7 %collective-permute-start.2 = (f32[256,128]{1,0:T(8,128)S(1)}, f32[256,128]{1,0:T(8,128)S(1)}, u32[]{:S(2)}, u32[]{:S(2)}) collective-permute-start(f32[256,128]{1,0:T(8,128)S(1)} %slice.17.own_ref), channel_id=1, source_target_pairs={{0,8},{4,12},{8,0},{12,4},{1,9},{5,13},{9,1},{13,5},{2,10},{6,14},... | collective-permute-start | bytes 393224 | tf_op jit(solution)/shard_map/ppermute | solution.py:366
  16.9 5.1 %collective-permute-start.3 = (f32[264,128]{1,0:T(8,128)S(1)}, f32[264,128]{1,0:T(8,128)S(1)}, u32[]{:S(2)}, u32[]{:S(2)}) collective-permute-start(f32[264,128]{1,0:T(8,128)S(1)} %broadcast_select_fusion.4), channel_id=1, source_target_pairs={{0,1},{1,0},{2,3},{3,2},{4,5},{5,4},{6,7},{7,6},{8,9},{9,8},{10,11... | collective-permute-start | bytes 405512 | tf_op jit(solution)/shard_map/ppermute | solution.py:366
  17.8 19.3 %collective-permute-start.10 = (f32[256,128]{1,0:T(8,128)S(1)}, f32[256,128]{1,0:T(8,128)S(1)}, u32[]{:S(2)}, u32[]{:S(2)}) collective-permute-start(f32[256,128]{1,0:T(8,128)S(1)} %broadcast_select_fusion.8), channel_id=1, source_target_pairs={{0,16},{16,0},{1,17},{17,1},{2,18},{18,2},{3,19},{19,3},{4,20},{20... | collective-permute-start | bytes 393224 | tf_op jit(solution)/shard_map/ppermute | solution.py:366
  22.0 5.1 %collective-permute-start.4 = (f32[264,128]{1,0:T(8,128)S(1)}, f32[264,128]{1,0:T(8,128)S(1)}, u32[]{:S(2)}, u32[]{:S(2)}) collective-permute-start(f32[264,128]{1,0:T(8,128)S(1)} %broadcast_select_fusion.5), channel_id=1, source_target_pairs={{0,8},{4,12},{8,0},{12,4},{1,9},{5,13},{9,1},{13,5},{2,10},{6,14},... | collective-permute-start | bytes 405512 | tf_op jit(solution)/shard_map/ppermute | solution.py:366
  23.5 5.0 %collective-permute-start.6 = (f32[256,128]{1,0:T(8,128)S(1)}, f32[256,128]{1,0:T(8,128)S(1)}, u32[]{:S(2)}, u32[]{:S(2)}) collective-permute-start(f32[256,128]{1,0:T(8,128)S(1)} %slice_select_fusion.1), channel_id=1, source_target_pairs={{0,8},{4,12},{8,0},{12,4},{1,9},{5,13},{9,1},{13,5},{2,10},{6,14},... | collective-permute-start | bytes 393224 | tf_op jit(solution)/shard_map/ppermute | solution.py:366
  27.1 1.5 %collective-permute-start.5 = (f32[264,128]{1,0:T(8,128)S(1)}, f32[264,128]{1,0:T(8,128)S(1)}, u32[]{:S(2)}, u32[]{:S(2)}) collective-permute-start(f32[264,128]{1,0:T(8,128)S(1)} %broadcast_select_fusion.6), channel_id=1, source_target_pairs={{0,4},{4,0},{8,12},{12,8},{1,5},{5,1},{9,13},{13,9},{2,6},{6,2},{1... | collective-permute-start | bytes 405512 | tf_op jit(solution)/shard_map/ppermute | solution.py:366
  28.6 5.5 %collective-permute-start.8 = (f32[256,128]{1,0:T(8,128)S(1)}, f32[256,128]{1,0:T(8,128)S(1)}, u32[]{:S(2)}, u32[]{:S(2)}) collective-permute-start(f32[256,128]{1,0:T(8,128)S(1)} %slice_select_fusion), channel_id=1, source_target_pairs={{0,16},{16,0},{1,17},{17,1},{2,18},{18,2},{3,19},{19,3},{4,20},{20... | collective-permute-start | bytes 393224 | tf_op jit(solution)/shard_map/ppermute | solution.py:366
  33.5 11.6 %collective-permute-start.7 = (f32[2,256,128]{2,1,0:T(8,128)S(1)}, f32[2,256,128]{2,1,0:T(8,128)S(1)}, u32[]{:S(2)}, u32[]{:S(2)}) collective-permute-start(f32[2,256,128]{2,1,0:T(8,128)S(1)} %pad_maximum_fusion.1), channel_id=1, source_target_pairs={{0,16},{16,0},{1,17},{17,1},{2,18},{18,2},{3,19},{19,3},{4,20},{20... | collective-permute-start | bytes 786440 | tf_op jit(solution)/shard_map/ppermute | solution.py:366
  34.2 3.5 %collective-permute-start.9 = (f32[2,256,128]{2,1,0:T(8,128)S(1)}, f32[2,256,128]{2,1,0:T(8,128)S(1)}, u32[]{:S(2)}, u32[]{:S(2)}) collective-permute-start(f32[2,256,128]{2,1,0:T(8,128)S(1)} %pad_maximum_fusion.2), channel_id=1, source_target_pairs={{0,4},{4,0},{8,12},{12,8},{1,5},{5,1},{9,13},{13,9},{2,6},{6,2},{1... | collective-permute-start | bytes 786440 | tf_op jit(solution)/shard_map/ppermute | solution.py:366
  37.1 7.9 %collective-permute-start.11 = (f32[2,256,128]{2,1,0:T(8,128)S(1)}, f32[2,256,128]{2,1,0:T(8,128)S(1)}, u32[]{:S(2)}, u32[]{:S(2)}) collective-permute-start(f32[2,256,128]{2,1,0:T(8,128)S(1)} %pad_maximum_fusion.3), channel_id=1, source_target_pairs={{0,4},{4,0},{8,12},{12,8},{1,5},{5,1},{9,13},{13,9},{2,6},{6,2},{1... | collective-permute-start | bytes 786440 | tf_op jit(solution)/shard_map/ppermute | solution.py:366
